TPU v7x, 32 devices: a whole 2x2x4 slice. The times are simulated.
32 devices in a mesh: parts: 2 (over y), dof: 1, mode: 8 (over z, x), sub: 2 (over core).
Axes of the slice: x: 2, y: 2, z: 4, core: 2. Of those that a mesh axis runs over, the one named last changes fastest.
Arguments:
- modes: bfloat16 [8192, 1024], P(('dof', 'sub'), ('parts', 'mode')), parts along dimension 1, may hold values from -6 to 6
- gyroscopic: bfloat16 [4, 32, 16, 128, 128], P(('parts', 'dof', 'sub'), 'mode'), parts along dimension 0, may hold values from -0.125 to 0.125
- centrifugal: bfloat16 [4, 32, 16, 128, 128], P(('parts', 'dof', 'sub'), 'mode'), parts along dimension 0, may hold values from -0.125 to 0.125
- pattern: int32 [2, 32, 16], P(('dof', 'sub'), 'mode'), may hold values from 0 to 63, as said below
Outputs:
- projected: float32 [4, 512, 512], P('parts', ('dof', 'sub'), 'mode'), parts along dimension 0
There are 2 independent parts, one for each index of `parts`. A program takes and returns all parts, laid end to end along the dimension named above; an argument that names none is the same for every part. Nothing has to cross between parts.
Inputs may be any that keep to these rules, and one draw needn't show every extreme that they name: `pattern`: block row r names 16 distinct block columns (r + o) mod 64 with -8 <= o <= 8; o = 0 is among them, and so is o = 8 or o = -8.
All inputs are finite; a program needn't handle non-finite values.
Results may differ from a plain program's by a relative error of at most 0.0029.
Values may be sent and summed in bfloat16 or wider, within the bound.
No kernel may reach another device: no remote copies, remote signals or barrier semaphores. Data moves between devices by JAX's collectives and lax.ppermute only.
A program may use at most 64 MiB of HBM per device.

v0:
```python
import math

import jax
import jax.numpy as jnp
from jax import lax
from jax.sharding import PartitionSpec as P

HB = 8


def extended_2(block, sides, width):
    for axis, dim in sides:
        count = lax.axis_size(axis)
        forward = [(i, i + 1) for i in range(count - 1)]
        forward.append((count - 1, 0))
        backward = [(target, source) for source, target in forward]
        low = lax.ppermute(
            lax.slice_in_dim(block, block.shape[dim] - width, None, axis=dim), axis, forward
        )
        high = lax.ppermute(lax.slice_in_dim(block, 0, width, axis=dim), axis, backward)
        block = jnp.concatenate([low, block, high], axis=dim)
    return block


def body(modes, gyroscopic, centrifugal, pattern):
    mode_count = lax.axis_size("mode")
    dof_count = lax.axis_size("dof")
    sub_count = lax.axis_size("sub")
    unit_count = dof_count * sub_count
    rows_dev = gyroscopic.shape[1]
    per_unit = rows_dev * mode_count
    block_size = gyroscopic.shape[3]
    mode_width = modes.shape[1] * mode_count
    block_total = unit_count * per_unit
    rim_depth = HB
    unit_index = lax.axis_index(("dof", "sub"))
    mode_index = lax.axis_index("mode")
    wide_phi = lax.all_gather(modes, "mode", axis=1, tiled=True)
    extended = extended_2(wide_phi, ((("dof", "sub"), 0),), rim_depth * block_size)
    ext_blocks = extended.reshape(per_unit + 2 * rim_depth, block_size, mode_width)
    local_index = jnp.mod(pattern[0] - unit_index * per_unit + rim_depth, block_total)
    nearby = ext_blocks[local_index]
    gyro_image = jnp.einsum(
        "jkab,jkbn->jan", gyroscopic[0], nearby, preferred_element_type=jnp.float32
    ).astype(jnp.bfloat16)
    spin_image = jnp.einsum(
        "jkab,jkbn->jan", centrifugal[0], nearby, preferred_element_type=jnp.float32
    ).astype(jnp.bfloat16)
    images = jnp.stack((gyro_image, spin_image)).reshape(2, rows_dev * block_size, mode_width)
    scaling = 1.0 / math.sqrt(block_total * block_size)
    own_rows = lax.dynamic_slice_in_dim(
        wide_phi, mode_index * rows_dev * block_size, rows_dev * block_size, 0
    )
    partial_value = (
        jnp.einsum("rm,xrn->xmn", own_rows, images, preferred_element_type=jnp.float32) * scaling
    )
    rows_out = mode_width // unit_count
    cols_out = mode_width // mode_count
    partial_value = partial_value.reshape(2, dof_count, sub_count, rows_out, mode_count, cols_out)
    partial_value = partial_value.transpose(0, 1, 4, 2, 3, 5).reshape(
        2, dof_count * mode_count * sub_count * rows_out, cols_out
    )
    return lax.psum_scatter(partial_value, ("dof", "mode", "sub"), scatter_dimension=1, tiled=True)


def solution(mesh):
    return jax.shard_map(
        body,
        mesh=mesh,
        in_specs=(
            P(("dof", "sub"), ("parts", "mode")),
            P(("parts", "dof", "sub"), "mode", None, None, None),
            P(("parts", "dof", "sub"), "mode", None, None, None),
            P(("dof", "sub"), "mode", None),
        ),
        out_specs=P("parts", ("dof", "sub"), "mode"),
        check_vma=False,
    )
```

profile of v0, /device:TPU:0, one launch (start us, length us, event | category | flops | bytes accessed | tf_op | source)
XLA Modules:
  0.0 208.3 jit_solution(5386684872861572886)
XLA Ops:
  6.5 0.7 all-gather.2.cloned.1.call-update
  7.3 0.0 reduce-scatter.2.cloned.1.call-start
  7.3 78.3 %all-gather.2.cloned.1.call-done = bf16[4096,512]{0,1:T(8,128)(2,1)} async-done(((bf16[4096,64]{0,1:T(8,128)(2,1)}), bf16[4096,512]{0,1:T(8,128)(2,1)}) %all-gather.2.cloned.1.call-update) | async-done | bytes 4194320 | tf_op jit(solution)/shard_map/all_gather | solution.py:38
  85.6 3.1 %fusion.24 = (bf16[1024,512]{0,1:T(8,128)(2,1)}, bf16[1024,512]{0,1:T(8,128)(2,1)}) fusion(bf16[4096,512]{0,1:T(8,128)(2,1)} %all-gather.2.cloned.1.call-done), kind=kLoop, calls=%fused_computation.24 | loop fusion | bytes 4194304 | tf_op jit(solution)/shard_map/slice | solution.py:18
  88.7 0.5 collective-permute-start.1
  89.2 0.7 compare_select_fusion
  89.9 0.1 reshape.78
  90.0 2.7 %collective-permute-done = bf16[1024,512]{0,1:T(8,128)(2,1)S(1)} collective-permute-done((bf16[1024,512]{0,1:T(8,128)(2,1)}, bf16[1024,512]{0,1:T(8,128)(2,1)S(1)}, u32[]{:S(2)}, u32[]{:S(2)}) %collective-permute-start) | collective-permute-done | bytes 1048608 | tf_op jit(solution)/shard_map/ppermute | solution.py:17
  92.7 0.5 collective-permute-done.1
  93.2 7.7 %pad_maximum_fusion = bf16[6144,512]{0,1:T(8,128)(2,1)} fusion(bf16[1024,512]{0,1:T(8,128)(2,1)} %collective-permute-done.1, bf16[4096,512]{0,1:T(8,128)(2,1)} %all-gather.2.cloned.1.call-done, bf16[1024,512]{0,1:T(8,128)(2,1)S(1)} %collective-permute-done), kind=kLoop, calls=%fused_computation.1 | loop fusion | flops 18874368 | bytes 12582912 | tf_op jit(solution)/shard_map/concatenate | solution.py:21
  100.8 8.6 %copy.14 = bf16[6144,512]{1,0:T(8,128)(2,1)} copy(bf16[6144,512]{0,1:T(8,128)(2,1)} %pad_maximum_fusion) | data formatting | bytes 12582912 | tf_op jit(solution)/shard_map/concatenate | solution.py:21
  109.4 8.3 %gather_fusion = bf16[64,128,512]{2,1,0:T(8,128)(2,1)} fusion(bf16[48,128,512]{2,1,0:T(8,128)(2,1)} %bitcast.53, s32[1024]{0:T(1024)S(1)} %pad_clamp_fusion), kind=kCustom, calls=%fused_computation | custom fusion | bytes 16777472 | tf_op jit(solution)/shard_map/gather | solution.py:42
  117.8 4.8 %fusion.10 = bf16[4,512,128]{1,2,0:T(8,128)(2,1)S(1)} fusion(bf16[4,16,128,512]{3,2,1,0:T(8,128)(2,1)} %bitcast.51, bf16[1,4,16,128,128]{4,3,2,1,0:T(8,128)(2,1)S(1)} %copy-done), kind=kOutput, calls=%fused_computation.9 | convolution fusion | flops 1074003968 | bytes 11010048 | tf_op jit(solution)/shard_map/jkab,jkbn->jan/dot_general | solution.py:46
  122.6 1.0 copy-done.1
  123.5 0.6 copy-done.2
  124.1 1.3 fusion.13
  125.4 1.0 copy.15
  126.4 0.2 copy.16
  126.6 3.3 %multiply_bitcast_fusion = f32[2,512,512]{1,2,0:T(8,128)} fusion(bf16[1,512,512]{1,2,0:T(8,128)(2,1)S(1)} %copy.16, bf16[1,512,512]{1,2,0:T(8,128)(2,1)} %copy.15, bf16[4096,512]{0,1:T(8,128)(2,1)} %all-gather.2.cloned.1.call-done, s32[]{:T(128)S(6)} %select_n.29), kind=kOutput, calls=%fused_computation.6 | convolution fusion | flops 537919488 | bytes 3670020 | tf_op jit(solution)/shard_map/rm,xrn->xmn/dot_general | solution.py:55
  129.9 3.5 %reshape.74 = f32[2,1,2,256,8,64]{3,2,5,4,0,1:T(2,128)} reshape(f32[2,512,512]{1,2,0:T(8,128)} %multiply_bitcast_fusion) | data formatting | bytes 4194304 | tf_op jit(solution)/shard_map/reshape | solution.py:59
  133.4 4.1 %copy.18 = f32[2,1,8,2,256,64]{4,3,2,5,0,1:T(2,128)} copy(f32[2,1,8,2,256,64]{4,3,5,2,0,1:T(2,128)} %bitcast.54) | data formatting | bytes 4194304 | tf_op jit(solution)/shard_map/transpose | solution.py:60
  137.6 3.9 %reshape.75 = f32[2,4096,64]{1,2,0:T(8,128)} reshape(f32[2,1,8,2,256,64]{4,3,2,5,0,1:T(2,128)} %copy.18) | data formatting | bytes 4194304 | tf_op jit(solution)/shard_map/reshape | solution.py:60
  141.5 0.0 reduce-scatter.2.cloned.1.call-update
  141.5 60.0 %reduce-scatter.2.cloned.1.call-done = f32[2,256,64]{1,2,0:T(8,128)} async-done(((f32[2,4096,64]{1,2,0:T(8,128)}), f32[2,256,64]{1,2,0:T(8,128)}) %reduce-scatter.2.cloned.1.call-update) | async-done | bytes 131088 | tf_op jit(solution)/shard_map/reduce_scatter | solution.py:63
  (7 shorter events, 0.0 us)
Async XLA Ops:
  6.5 111.2 %copy-start = (bf16[1,4,16,128,128]{4,3,2,1,0:T(8,128)(2,1)S(1)}, bf16[1,4,16,128,128]{4,3,2,1,0:T(8,128)(2,1)}, u32[]{:S(2)}) copy-start(bf16[1,4,16,128,128]{4,3,2,1,0:T(8,128)(2,1)} %param.6) | copy-start | bytes 6291460
  6.5 79.1 %all-gather.2.cloned.1.call-start = ((), (), s32[]{:S(2)}) async-start(), calls=%async_computation.1 | async-start | bytes 4718592 | tf_op jit(solution)/shard_map/all_gather | solution.py:38
  7.3 194.2 %reduce-scatter.2.cloned.1.call-start = ((), (), s32[]{:S(2)}) async-start(), calls=%async_computation.2 | async-start | bytes 2228224 | tf_op jit(solution)/shard_map/reduce_scatter | solution.py:63
  88.7 4.0 %collective-permute-start = (bf16[1024,512]{0,1:T(8,128)(2,1)}, bf16[1024,512]{0,1:T(8,128)(2,1)S(1)}, u32[]{:S(2)}, u32[]{:S(2)}) collective-permute-start(bf16[1024,512]{0,1:T(8,128)(2,1)} %get-tuple-element.5), channel_id=1, source_target_pairs={{0,1},{1,0},{2,3},{3,2},{4,5},{5,4},{6,7},{7,6},{8,9},{9,8},{10,11... | collective-permute-start | bytes 3145736 | tf_op jit(solution)/shard_map/ppermute | solution.py:17
  88.7 4.5 %collective-permute-start.1 = (bf16[1024,512]{0,1:T(8,128)(2,1)}, bf16[1024,512]{0,1:T(8,128)(2,1)}, u32[]{:S(2)}, u32[]{:S(2)}) collective-permute-start(bf16[1024,512]{0,1:T(8,128)(2,1)} %get-tuple-element.6), channel_id=1, source_target_pairs={{1,0},{0,1},{3,2},{2,3},{5,4},{4,5},{7,6},{6,7},{9,8},{8,9},{11,10... | collective-permute-start | bytes 3145736 | tf_op jit(solution)/shard_map/ppermute | solution.py:20
  117.8 5.8 %copy-start.1 = (bf16[64,128,512]{2,1,0:T(8,128)(2,1)S(1)}, bf16[64,128,512]{2,1,0:T(8,128)(2,1)}, u32[]{:S(2)}) copy-start(bf16[64,128,512]{2,1,0:T(8,128)(2,1)} %gather_fusion) | copy-start | bytes 25165828
  117.8 6.4 %copy-start.2 = (bf16[1,4,16,128,128]{4,3,2,1,0:T(8,128)(2,1)S(1)}, bf16[1,4,16,128,128]{4,3,2,1,0:T(8,128)(2,1)}, u32[]{:S(2)}) copy-start(bf16[1,4,16,128,128]{4,3,2,1,0:T(8,128)(2,1)} %param.5) | copy-start | bytes 6291460
Sparse Core Ops, SparseCore 0:
  9.5 76.0 all-gather.1
  141.6 59.8 reduce-scatter.1
where the time goes:
time: 209 us; the launch traced here: 208 us
  waiting for transfers between devices  142 us (68%)
  local copies, waits for them, and re-layouts  34.4 us (16%)
  between operations  13.4 us (6%)
  matrix products  9.34 us (4%)
  other arithmetic  8.38 us (4%)
    all_gather x1, waiting for transfers between devices, body(): wide_phi = lax.all_gather(modes, 'mode', axis=1, tiled=True)  78.3 us
    reduce_scatter x1, waiting for transfers between devices, body(): lax.psum_scatter(partial_value, ('dof', 'mode', 'sub'), scatter_dimension...  60 us
    concatenate x1, local copies, waits for them, and re-layouts, extended_2(): block = jnp.concatenate([low, block, high], axis=dim)  8.58 us
    gather x1, local copies, waits for them, and re-layouts, body(): nearby = ext_blocks[local_index]  8.32 us
    concatenate x1, other arithmetic, extended_2(): block = jnp.concatenate([low, block, high], axis=dim)  7.68 us
    dot_general x1, matrix products, body(): jnp.einsum('jkab,jkbn->jan', centrifugal[0], nearby, preferred_element_ty...  4.8 us
  transfers between devices with their start and end apart: 4, of which 4 were waited for; matrix products, arithmetic and copies ran while one was open for 0% of the time, Pallas kernels for 0%

commit v1 on v0

v1 whole, which is shorter than its diff:
```python
import functools
import math

import jax
import jax.numpy as jnp
from jax import lax
from jax.experimental import pallas as pl
from jax.experimental.pallas import tpu as pltpu
from jax.sharding import PartitionSpec as P

HB = 8
X = 2
VMEM_LIMIT = 48 * 1024 * 1024
NT = (((1,), (1,)), ((), ()))


def ring(count):
    forward = [(i, (i + 1) % count) for i in range(count)]
    return forward, [(target, source) for source, target in forward]


def band_kernel(place, gyro, spin, band):
    row = pl.program_id(0)
    slots = gyro.shape[2]
    band[...] = jnp.zeros_like(band)
    for slot in range(slots):
        column = pl.multiple_of(place[row, slot] * 128, 128)
        band[0, 0, :, pl.ds(column, 128)] = gyro[0, 0, slot]
        band[1, 0, :, pl.ds(column, 128)] = spin[0, 0, slot]


def make_band(place, gyroscopic, centrifugal, width):
    _, rows, slots, size, _ = gyroscopic.shape
    block = pl.BlockSpec((1, 1, slots, size, size), lambda j, place: (0, j, 0, 0, 0))
    band = pl.pallas_call(
        band_kernel,
        out_shape=jax.ShapeDtypeStruct((2, rows, size, width), jnp.bfloat16),
        grid_spec=pltpu.PrefetchScalarGridSpec(
            num_scalar_prefetch=1,
            grid=(rows,),
            in_specs=[block, block],
            out_specs=pl.BlockSpec((2, 1, size, width), lambda j, place: (0, j, 0, 0)),
        ),
        compiler_params=pltpu.CompilerParams(vmem_limit_bytes=VMEM_LIMIT),
        name="band",
    )(place, gyroscopic, centrifugal)
    return band.reshape(2 * rows * size, width)


def image_kernel(group, info, own, cross, band, image, centre, lhs):
    offset = pl.multiple_of(info[0] * group, group)
    own_x = info[1]
    width = cross.shape[0]
    lhs[:width, :] = own[:, pl.ds(offset, cross.shape[1])]
    lhs[width:, :] = cross[...]
    image[...] = lax.dot_general(
        lhs[...], band[...], NT, preferred_element_type=jnp.float32
    ).astype(jnp.bfloat16)
    middle = pl.ds(2 * group, group)
    centre[pl.ds(pl.multiple_of(own_x * width, width), width), :] = lhs[:width, middle]
    centre[pl.ds(pl.multiple_of((1 - own_x) * width, width), width), :] = lhs[width:, middle]


def make_image(info, own, cross, band, group):
    width, span = cross.shape
    vmem = pl.BlockSpec(memory_space=pltpu.VMEM)
    return pl.pallas_call(
        functools.partial(image_kernel, group),
        out_shape=(
            jax.ShapeDtypeStruct((2 * width, band.shape[0]), jnp.bfloat16),
            jax.ShapeDtypeStruct((2 * width, group), jnp.bfloat16),
        ),
        in_specs=[pl.BlockSpec(memory_space=pltpu.SMEM), vmem, vmem, vmem],
        out_specs=(vmem, vmem),
        scratch_shapes=[pltpu.VMEM((2 * width, span), jnp.bfloat16)],
        compiler_params=pltpu.CompilerParams(vmem_limit_bytes=VMEM_LIMIT),
        cost_estimate=pl.CostEstimate(
            flops=4 * width * span * band.shape[0],
            bytes_accessed=2 * span * band.shape[0],
            transcendentals=0,
        ),
        name="image",
    )(info, own, cross, band)


def project_kernel(scaling, rows_out, info, *refs):
    images, centres = refs[:4], refs[4:8]
    keep, send, own_rows, stacked = refs[8:]
    pair = centres[0].shape[0]
    total, depth = own_rows.shape
    half = total // 2
    chunk = min(rows_out, pair)
    sub = info[8]
    for slot in range(4):
        start = info[slot] * pair
        for piece in range(pair // chunk):
            first = start + piece * chunk
            target = (
                lax.rem(lax.div(first, rows_out), 2) * half
                + lax.div(first, 2 * rows_out) * rows_out
                + lax.rem(first, rows_out)
            )
            own_rows[pl.ds(pl.multiple_of(target, chunk), chunk), :] = centres[slot][
                piece * chunk : (piece + 1) * chunk, :
            ]
        stacked[pl.ds(pl.multiple_of(info[4 + slot] * pair, pair), pair), :] = images[slot][...]
    mine = pl.ds(pl.multiple_of(sub * half, half), half)
    other = pl.ds(pl.multiple_of((1 - sub) * half, half), half)
    for matrix in range(2):
        part = stacked[:, matrix * depth : (matrix + 1) * depth]
        send[matrix] = (
            lax.dot_general(part, own_rows[other, :], NT, preferred_element_type=jnp.float32)
            * scaling
        ).astype(send.dtype)
        keep[matrix] = (
            lax.dot_general(part, own_rows[mine, :], NT, preferred_element_type=jnp.float32)
            * scaling
        )


def make_projection(info, images, centres, scaling, rows_out):
    pair, depth = centres[0].shape
    total = 4 * pair
    vmem = pl.BlockSpec(memory_space=pltpu.VMEM)
    return pl.pallas_call(
        functools.partial(project_kernel, scaling, rows_out),
        out_shape=(
            jax.ShapeDtypeStruct((2, total, total // 2), jnp.float32),
            jax.ShapeDtypeStruct((2, total, total // 2), jnp.bfloat16),
        ),
        in_specs=[pl.BlockSpec(memory_space=pltpu.SMEM)] + [vmem] * 8,
        out_specs=(vmem, vmem),
        scratch_shapes=[
            pltpu.VMEM((total, depth), jnp.bfloat16),
            pltpu.VMEM((total, images[0].shape[1]), jnp.bfloat16),
        ],
        compiler_params=pltpu.CompilerParams(vmem_limit_bytes=VMEM_LIMIT),
        cost_estimate=pl.CostEstimate(
            flops=4 * total * total * depth, bytes_accessed=4 * total * total, transcendentals=0
        ),
        name="project",
    )(info, *images, *centres)


def body(modes, gyroscopic, centrifugal, pattern):
    mode_count = lax.axis_size("mode")
    dof_count = lax.axis_size("dof")
    sub_count = lax.axis_size("sub")
    unit_count = dof_count * sub_count
    rows_dev = gyroscopic.shape[1]
    block_size = gyroscopic.shape[3]
    per_unit = rows_dev * mode_count
    block_total = unit_count * per_unit
    group = rows_dev * block_size
    total = modes.shape[1] * mode_count
    unit = lax.axis_index(("dof", "sub"))
    sub = lax.axis_index("sub")
    m = lax.axis_index("mode")
    z, x = m // X, m % X
    is_mid = (z == 1) | (z == 2)

    place = jnp.mod(pattern[0] - (unit * per_unit + m * rows_dev) + HB, block_total)
    band = make_band(place, gyroscopic, centrifugal, (rows_dev + 2 * HB) * block_size)

    phi = modes.T
    forward, backward = ring(unit_count)
    rim = HB * block_size
    low = lax.ppermute(phi[:, phi.shape[1] - rim :], ("dof", "sub"), forward)
    high = lax.ppermute(phi[:, :rim], ("dof", "sub"), backward)
    ext = jnp.concatenate([low, phi, high], axis=1)

    def window(array, first, count):
        return lax.dynamic_slice_in_dim(array, first * group, count * group, 1)

    def over_z(array, pairs):
        return lax.ppermute(
            array, "mode", [(s * X + i, t * X + i) for s, t in pairs for i in range(X)]
        )

    def over_x(array):
        return lax.ppermute(array, "mode", [(i, i ^ 1) for i in range(mode_count)])

    near = over_z(window(ext, 2 * (z ^ 1), 6), [(0, 1), (1, 0), (2, 3), (3, 2)])
    inner = over_z(window(ext, jnp.where(z == 1, 4, 0), 8), [(1, 2), (2, 1)])
    cross0 = over_x(window(ext, m ^ 1, 5))
    skip = over_z(window(ext, jnp.where(z == 0, 4, 2), 6), [(0, 2), (3, 1)])
    far = over_z(window(ext, jnp.where(z == 0, 6, 0), 6), [(0, 3), (3, 0)])
    passed = over_z(window(inner, jnp.where(z == 2, 2, 0), 6), [(2, 3), (1, 0)])
    crossA = over_x(window(near, 1 - x, 5))
    slotB = jnp.where(is_mid, window(inner, jnp.where(z == 1, 2, 0), 6), passed)
    crossB = over_x(window(slotB, 1 - x, 5))
    slotC = jnp.where(is_mid, skip, far)
    crossC = over_x(window(slotC, 1 - x, 5))

    pieces = []
    for own, cross, first in ((ext, cross0, m), (near, crossA, x), (slotB, crossB, x), (slotC, crossC, x)):
        info = jnp.stack([first, x]).astype(jnp.int32)
        pieces.append(make_image(info, own, cross, band, group))

    order_b = jnp.where(is_mid, 3, 2)
    order_c = jnp.where(is_mid, 2, 3)
    zero = jnp.zeros_like(z)
    info = jnp.stack(
        [z, z ^ 1, z ^ order_b, z ^ order_c, zero, zero + 1, order_b, order_c, sub]
    ).astype(jnp.int32)
    scaling = 1.0 / math.sqrt(block_total * block_size)
    keep, send = make_projection(
        info, [p[0] for p in pieces], [p[1] for p in pieces], scaling, total // unit_count
    )
    got = lax.ppermute(send, "sub", [(0, 1), (1, 0)])
    chip = keep + got.astype(jnp.float32)
    width = modes.shape[1]
    result = chip[:, :width]
    for j in range(1, mode_count):
        message = chip[:, j * width : (j + 1) * width].astype(jnp.bfloat16)
        arrived = lax.ppermute(message, "mode", [(i, i ^ j) for i in range(mode_count)])
        result = result + arrived.astype(jnp.float32)
    if dof_count > 1:
        result = lax.psum_scatter(result, "dof", scatter_dimension=2, tiled=True)
    return result.transpose(0, 2, 1)


def solution(mesh):
    return jax.shard_map(
        body,
        mesh=mesh,
        in_specs=(
            P(("dof", "sub"), ("parts", "mode")),
            P(("parts", "dof", "sub"), "mode", None, None, None),
            P(("parts", "dof", "sub"), "mode", None, None, None),
            P(("dof", "sub"), "mode", None),
        ),
        out_specs=P("parts", ("dof", "sub"), "mode"),
        check_vma=False,
    )
```

time: 209 us -> 98.7 us (0.47)
  waiting for transfers between devices: 142 us -> 36.5 us
  starting transfers between devices: 0.55 us -> 28.8 us
  local copies, waits for them, and re-layouts: 34.4 us -> 7.48 us
  Pallas kernels: 0 us -> 22.2 us
  between operations: 13.4 us -> 0.19 us
  matrix products: 9.34 us -> 0 us
  other arithmetic: 8.38 us -> 2.96 us
    all_gather x1 -> x0, waiting for transfers between devices: 78.3 us -> none  [body(): wide_phi = lax.all_gather(modes, 'mode', axis=1, tiled=True)]
    reduce_scatter x1 -> x0, waiting for transfers between devices: 60 us -> none  [body(): lax.psum_scatter(partial_value, ('dof', 'mode', 'sub'), scatter_dimension...]
    ppermute x2 -> x19, waiting for transfers between devices: 3.2 us -> 36.5 us  [the longest x5 29.3 us: over_z(): lax.ppermute(array, 'mode', [(s * X + i, t * X + i) for s, t in pairs for...]
    ppermute x2 -> x19, starting transfers between devices: 0.51 us -> 28.8 us  [the longest x7 11.2 us: body(): lax.ppermute(message, 'mode', [(i, i ^ j) for i in range(mode_count)])]
    pallas_call x0 -> x6, Pallas kernels: none -> 22.2 us  [the longest x4 17.2 us: make_image(): pl.pallas_call(functools.partial(image_kernel, group), out_shape=(jax.Sha...]
    dot_general x3 -> x0, matrix products: 9.34 us -> none  [the longest x1 4.8 us: body(): jnp.einsum('jkab,jkbn->jan', centrifugal[0], nearby, preferred_element_ty...]
    concatenate x1 -> x0, local copies, waits for them, and re-layouts: 8.58 us -> none  [extended_2(): block = jnp.concatenate([low, block, high], axis=dim)]
    gather x1 -> x0, local copies, waits for them, and re-layouts: 8.32 us -> none  [body(): nearby = ext_blocks[local_index]]
  transfers between devices with their start and end apart: 4 -> 19, of which waited for: 4 -> 10; matrix products, arithmetic and copies ran while one was open for 0% -> 4% of each run, Pallas kernels for 0% -> 17%
where the time goes in v1:
time: 98.7 us; the launch traced here: 98.2 us
  waiting for transfers between devices  36.5 us (37%)
  starting transfers between devices  28.8 us (29%)
  Pallas kernels  22.2 us (22%)
  local copies, waits for them, and re-layouts  7.48 us (8%)
  other arithmetic  2.96 us (3%)
    ppermute x5, waiting for transfers between devices, over_z(): lax.ppermute(array, 'mode', [(s * X + i, t * X + i) for s, t in pairs for...  29.3 us
    pallas_call x4, Pallas kernels, make_image(): pl.pallas_call(functools.partial(image_kernel, group), out_shape=(jax.Sha...  17.2 us
    ppermute x7, starting transfers between devices, body(): lax.ppermute(message, 'mode', [(i, i ^ j) for i in range(mode_count)])  11.2 us
    ppermute x5, starting transfers between devices, over_z(): lax.ppermute(array, 'mode', [(s * X + i, t * X + i) for s, t in pairs for...  11 us
    ppermute x4, starting transfers between devices, over_x(): return lax.ppermute(array, 'mode', [(i, i ^ 1) for i in range(mode_count)])  5.96 us
    ppermute x7, waiting for transfers between devices, body(): lax.ppermute(message, 'mode', [(i, i ^ j) for i in range(mode_count)])  4.8 us
    pallas_call x1, Pallas kernels, make_band(): pl.pallas_call(band_kernel, out_shape=jax.ShapeDtypeStruct((2, rows, size...  3.68 us
    dynamic_slice x7, local copies, waits for them, and re-layouts, window(): return lax.dynamic_slice_in_dim(array, first * group, count * group, 1)  3.2 us
  transfers between devices with their start and end apart: 19, of which 10 were waited for; matrix products, arithmetic and copies ran while one was open for 4% of the time, Pallas kernels for 17%

profile of v1, /device:TPU:0, one launch (start us, length us, event | category | flops | bytes accessed | tf_op | source)
XLA Modules:
  0.0 98.2 jit_solution(15590931645692082065)
XLA Ops:
  4.1 5.7 %collective-permute-start.8 = (bf16[64,3072]{1,0:T(8,128)(2,1)S(1)}, bf16[64,3072]{1,0:T(8,128)(2,1)S(1)}, u32[]{:S(2)}, u32[]{:S(2)}) collective-permute-start(bf16[64,3072]{1,0:T(8,128)(2,1)S(1)} %get-tuple-element.28), channel_id=1, source_target_pairs={{0,8},{2,10},{12,4},{14,6},{1,9},{3,11},{13,5},{15,7},{16,24},{18,... | collective-permute-start | bytes 1179656 | tf_op jit(solution)/shard_map/ppermute | solution.py:176
  9.8 3.3 %collective-permute-start.9 = (bf16[64,3072]{1,0:T(8,128)(2,1)S(1)}, bf16[64,3072]{1,0:T(8,128)(2,1)S(1)}, u32[]{:S(2)}, u32[]{:S(2)}) collective-permute-start(bf16[64,3072]{1,0:T(8,128)(2,1)S(1)} %get-tuple-element.27), channel_id=1, source_target_pairs={{0,12},{2,14},{12,0},{14,2},{1,13},{3,15},{13,1},{15,3},{16,28},{1... | collective-permute-start | bytes 1179656 | tf_op jit(solution)/shard_map/ppermute | solution.py:176
  14.6 1.5 %collective-permute-start.2 = (bf16[64,2560]{1,0:T(8,128)(2,1)}, bf16[64,2560]{1,0:T(8,128)(2,1)S(1)}, u32[]{:S(2)}, u32[]{:S(2)}) collective-permute-start(bf16[64,2560]{1,0:T(8,128)(2,1)} %constant_dynamic-slice_fusion.8), channel_id=1, source_target_pairs={{0,2},{2,0},{4,6},{6,4},{8,10},{10,8},{12,14},{14,12},{1,3},{3,1},... | collective-permute-start | bytes 983048 | tf_op jit(solution)/shard_map/ppermute | solution.py:181
  16.1 3.1 %collective-permute-done.8 = bf16[64,3072]{1,0:T(8,128)(2,1)S(1)} collective-permute-done((bf16[64,3072]{1,0:T(8,128)(2,1)S(1)}, bf16[64,3072]{1,0:T(8,128)(2,1)S(1)}, u32[]{:S(2)}, u32[]{:S(2)}) %collective-permute-start.8) | collective-permute-done | bytes 393248 | tf_op jit(solution)/shard_map/ppermute | solution.py:176
  19.2 10.3 %collective-permute-done.9 = bf16[64,3072]{1,0:T(8,128)(2,1)S(1)} collective-permute-done((bf16[64,3072]{1,0:T(8,128)(2,1)S(1)}, bf16[64,3072]{1,0:T(8,128)(2,1)S(1)}, u32[]{:S(2)}, u32[]{:S(2)}) %collective-permute-start.9) | collective-permute-done | bytes 393248 | tf_op jit(solution)/shard_map/ppermute | solution.py:176
  31.7 1.5 %collective-permute-start.10 = (bf16[64,2560]{1,0:T(8,128)(2,1)}, bf16[64,2560]{1,0:T(8,128)(2,1)S(1)}, u32[]{:S(2)}, u32[]{:S(2)}) collective-permute-start(bf16[64,2560]{1,0:T(8,128)(2,1)} %constant_dynamic-slice_fusion), channel_id=1, source_target_pairs={{0,2},{2,0},{4,6},{6,4},{8,10},{10,8},{12,14},{14,12},{1,3},{3,1},... | collective-permute-start | bytes 983048 | tf_op jit(solution)/shard_map/ppermute | solution.py:181
  33.2 2.4 %collective-permute-done.3.own = bf16[64,3072]{1,0:T(8,128)(2,1)S(1)} collective-permute-done((bf16[64,3072]{1,0:T(8,128)(2,1)S(1)}, bf16[64,3072]{1,0:T(8,128)(2,1)S(1)}, u32[]{:S(2)}, u32[]{:S(2)}) %collective-permute-start.3) | collective-permute-done | bytes 393248 | tf_op jit(solution)/shard_map/ppermute | solution.py:176
  36.3 1.5 %collective-permute-start.4 = (bf16[64,2560]{1,0:T(8,128)(2,1)}, bf16[64,2560]{1,0:T(8,128)(2,1)S(1)}, u32[]{:S(2)}, u32[]{:S(2)}) collective-permute-start(bf16[64,2560]{1,0:T(8,128)(2,1)} %constant_dynamic-slice_fusion.6), channel_id=1, source_target_pairs={{0,2},{2,0},{4,6},{6,4},{8,10},{10,8},{12,14},{14,12},{1,3},{3,1},... | collective-permute-start | bytes 983048 | tf_op jit(solution)/shard_map/ppermute | solution.py:181
  37.8 13.5 %collective-permute-done.6 = bf16[64,3072]{1,0:T(8,128)(2,1)S(1)} collective-permute-done((bf16[64,3072]{1,0:T(8,128)(2,1)S(1)}, bf16[64,3072]{1,0:T(8,128)(2,1)S(1)}, u32[]{:S(2)}, u32[]{:S(2)}) %collective-permute-start.6) | collective-permute-done | bytes 393248 | tf_op jit(solution)/shard_map/ppermute | solution.py:176
  52.1 1.5 %collective-permute-start.7 = (bf16[64,2560]{1,0:T(8,128)(2,1)}, bf16[64,2560]{1,0:T(8,128)(2,1)S(1)}, u32[]{:S(2)}, u32[]{:S(2)}) collective-permute-start(bf16[64,2560]{1,0:T(8,128)(2,1)} %constant_dynamic-slice_fusion.3), channel_id=1, source_target_pairs={{0,2},{2,0},{4,6},{6,4},{8,10},{10,8},{12,14},{14,12},{1,3},{3,1},... | collective-permute-start | bytes 983048 | tf_op jit(solution)/shard_map/ppermute | solution.py:181
  53.7 1.6 %copy-done = bf16[1,4,16,128,128]{4,3,2,1,0:T(8,128)(2,1)S(1)} copy-done((bf16[1,4,16,128,128]{4,3,2,1,0:T(8,128)(2,1)S(1)}, bf16[1,4,16,128,128]{4,3,2,1,0:T(8,128)(2,1)}, u32[]{:S(2)}) %copy-start) | copy-done | bytes 2097176
  55.3 1.6 %copy-done.1 = bf16[1,4,16,128,128]{4,3,2,1,0:T(8,128)(2,1)S(1)} copy-done((bf16[1,4,16,128,128]{4,3,2,1,0:T(8,128)(2,1)S(1)}, bf16[1,4,16,128,128]{4,3,2,1,0:T(8,128)(2,1)}, u32[]{:S(2)}) %copy-start.1) | copy-done | bytes 2097176
  56.9 3.7 %band.1 = bf16[2,4,128,2560]{3,2,1,0:T(8,128)(2,1)} custom-call(s32[4,16]{1,0:T(4,128)S(1)} %add_select_fusion.place, bf16[1,4,16,128,128]{4,3,2,1,0:T(8,128)(2,1)S(1)} %copy-done, bf16[1,4,16,128,128]{4,3,2,1,0:T(8,128)(2,1)S(1)} %copy-done.1), custom_call_target="tpu_custom_call" | custom-call | tf_op jit(solution)/shard_map/band/pallas_call | solution.py:35
  60.7 4.3 %image.4 = (bf16[128,1024]{1,0:T(8,128)(2,1)S(1)}, bf16[128,512]{1,0:T(8,128)(2,1)S(1)}) custom-call(s32[2]{0:T(128)S(1)} %pad_add_fusion.info, bf16[64,6144]{1,0:T(8,128)(2,1)S(1)} %pad_maximum_fusion.own, bf16[64,2560]{1,0:T(8,128)(2,1)S(1)} %collective-permute-done.2.cross, bf16[1024,2560]{1,0:T(8,128)(2,1)} %bitcast.17), custom_call_target="tpu_custom_call" | custom-call | flops 671088640 | bytes 5242880 | tf_op jit(solution)/shard_map/image/pallas_call | solution.py:67
  65.0 4.3 %image.7 = (bf16[128,1024]{1,0:T(8,128)(2,1)S(1)}, bf16[128,512]{1,0:T(8,128)(2,1)S(1)}) custom-call(s32[2]{0:T(128)S(1)} %pad_add_fusion.1.info, bf16[64,3072]{1,0:T(8,128)(2,1)S(1)} %broadcast_select_fusion.own, bf16[64,2560]{1,0:T(8,128)(2,1)S(1)} %collective-permute-done.10.cross, bf16[1024,2560]{1,0:T(8,128)(2,1)} %bitcast.18), custom_call_target="tpu_custom_call" | custom-call | flops 671088640 | bytes 5242880 | tf_op jit(solution)/shard_map/image/pallas_call | solution.py:67
  69.3 4.3 %image.5 = (bf16[128,1024]{1,0:T(8,128)(2,1)S(1)}, bf16[128,512]{1,0:T(8,128)(2,1)S(1)}) custom-call(s32[2]{0:T(128)S(1)} %pad_add_fusion.1.info, bf16[64,3072]{1,0:T(8,128)(2,1)S(1)} %collective-permute-done.3.own, bf16[64,2560]{1,0:T(8,128)(2,1)S(1)} %collective-permute-done.4.cross, bf16[1024,2560]{1,0:T(8,128)(2,1)} %bitcast.19), custom_call_target="tpu_custom_call" | custom-call | flops 671088640 | bytes 5242880 | tf_op jit(solution)/shard_map/image/pallas_call | solution.py:67
  73.6 4.3 %image.6 = (bf16[128,1024]{1,0:T(8,128)(2,1)S(1)}, bf16[128,512]{1,0:T(8,128)(2,1)S(1)}) custom-call(s32[2]{0:T(128)S(1)} %pad_add_fusion.1.info, bf16[64,3072]{1,0:T(8,128)(2,1)S(1)} %dynamic-slice_select_fusion.own, bf16[64,2560]{1,0:T(8,128)(2,1)S(1)} %collective-permute-done.7.cross, bf16[1024,2560]{1,0:T(8,128)(2,1)} %bitcast.20), custom_call_target="tpu_custom_call" | custom-call | flops 671088640 | bytes 5242880 | tf_op jit(solution)/shard_map/image/pallas_call | solution.py:67
  77.9 1.3 %project.1 = (f32[2,512,256]{2,1,0:T(8,128)S(1)}, bf16[2,512,256]{2,1,0:T(8,128)(2,1)S(1)}) custom-call(s32[9]{0:T(128)S(1)} %stack.51.info, bf16[128,1024]{1,0:T(8,128)(2,1)S(1)} %get-tuple-element.15.refs_0_, bf16[128,1024]{1,0:T(8,128)(2,1)S(1)} %get-tuple-element.16.refs_1_, bf16[128,1024]{1,0:T(8,128)(2,1)S(1)} %get-tuple-element.17.refs_2_, ...), custom_call_target="tpu_custom_call" | custom-call | flops 536870912 | bytes 1048576 | tf_op jit(solution)/shard_map/project/pallas_call | solution.py:125
  79.4 1.9 %collective-permute-done.11 = bf16[2,512,256]{2,1,0:T(8,128)(2,1)S(1)} collective-permute-done((bf16[2,512,256]{2,1,0:T(8,128)(2,1)S(1)}, bf16[2,512,256]{2,1,0:T(8,128)(2,1)S(1)}, u32[]{:S(2)}, u32[]{:S(2)}) %collective-permute-start.11) | collective-permute-done | bytes 524320 | tf_op jit(solution)/shard_map/ppermute | solution.py:210
  82.1 2.9 %collective-permute-start.14 = (bf16[2,64,256]{2,1,0:T(8,128)(2,1)S(1)}, bf16[2,64,256]{2,1,0:T(8,128)(2,1)S(1)}, u32[]{:S(2)}, u32[]{:S(2)}) collective-permute-start(bf16[2,64,256]{2,1,0:T(8,128)(2,1)S(1)} %get-tuple-element.35), channel_id=1, source_target_pairs={{0,6},{2,4},{4,2},{6,0},{8,14},{10,12},{12,10},{14,8},{1,7},{3,5},... | collective-permute-start | bytes 196616 | tf_op jit(solution)/shard_map/ppermute | solution.py:216
  86.1 1.9 %collective-permute-start.16 = (bf16[2,64,256]{2,1,0:T(8,128)(2,1)S(1)}, bf16[2,64,256]{2,1,0:T(8,128)(2,1)S(1)}, u32[]{:S(2)}, u32[]{:S(2)}) collective-permute-start(bf16[2,64,256]{2,1,0:T(8,128)(2,1)S(1)} %get-tuple-element.33), channel_id=1, source_target_pairs={{0,10},{2,8},{4,14},{6,12},{8,2},{10,0},{12,6},{14,4},{1,11},{3,9}... | collective-permute-start | bytes 196616 | tf_op jit(solution)/shard_map/ppermute | solution.py:216
  88.0 2.4 %collective-permute-start.17 = (bf16[2,64,256]{2,1,0:T(8,128)(2,1)S(1)}, bf16[2,64,256]{2,1,0:T(8,128)(2,1)S(1)}, u32[]{:S(2)}, u32[]{:S(2)}) collective-permute-start(bf16[2,64,256]{2,1,0:T(8,128)(2,1)S(1)} %get-tuple-element.32), channel_id=1, source_target_pairs={{0,12},{2,14},{4,8},{6,10},{8,4},{10,6},{12,0},{14,2},{1,13},{3,15... | collective-permute-start | bytes 196616 | tf_op jit(solution)/shard_map/ppermute | solution.py:216
  90.4 2.3 %collective-permute-start.18 = (bf16[2,64,256]{2,1,0:T(8,128)(2,1)S(1)}, bf16[2,64,256]{2,1,0:T(8,128)(2,1)S(1)}, u32[]{:S(2)}, u32[]{:S(2)}) collective-permute-start(bf16[2,64,256]{2,1,0:T(8,128)(2,1)S(1)} %get-tuple-element.31), channel_id=1, source_target_pairs={{0,14},{2,12},{4,10},{6,8},{8,6},{10,4},{12,2},{14,0},{1,15},{3,13... | collective-permute-start | bytes 196616 | tf_op jit(solution)/shard_map/ppermute | solution.py:216
  92.7 2.5 %collective-permute-done.15 = bf16[2,64,256]{2,1,0:T(8,128)(2,1)S(1)} collective-permute-done((bf16[2,64,256]{2,1,0:T(8,128)(2,1)S(1)}, bf16[2,64,256]{2,1,0:T(8,128)(2,1)S(1)}, u32[]{:S(2)}, u32[]{:S(2)}) %collective-permute-start.15) | collective-permute-done | bytes 65568 | tf_op jit(solution)/shard_map/ppermute | solution.py:216
  (42 shorter events, 14.6 us)
Async XLA Ops:
  1.0 1.5 %collective-permute-start = (bf16[64,1024]{1,0:T(8,128)(2,1)S(1)}, bf16[64,1024]{1,0:T(8,128)(2,1)S(1)}, u32[]{:S(2)}, u32[]{:S(2)}) collective-permute-start(bf16[64,1024]{1,0:T(8,128)(2,1)S(1)} %get-tuple-element.37), channel_id=1, source_target_pairs={{0,1},{1,0},{2,3},{3,2},{4,5},{5,4},{6,7},{7,6},{8,9},{9,8},{10,11... | collective-permute-start | bytes 393224 | tf_op jit(solution)/shard_map/ppermute | solution.py:168
  1.5 1.3 %collective-permute-start.1 = (bf16[64,1024]{1,0:T(8,128)(2,1)S(1)}, bf16[64,1024]{1,0:T(8,128)(2,1)S(1)}, u32[]{:S(2)}, u32[]{:S(2)}) collective-permute-start(bf16[64,1024]{1,0:T(8,128)(2,1)S(1)} %get-tuple-element.38), channel_id=1, source_target_pairs={{1,0},{0,1},{3,2},{2,3},{5,4},{4,5},{7,6},{6,7},{9,8},{8,9},{11,10... | collective-permute-start | bytes 393224 | tf_op jit(solution)/shard_map/ppermute | solution.py:169
  4.1 15.2 %collective-permute-start.8 = (bf16[64,3072]{1,0:T(8,128)(2,1)S(1)}, bf16[64,3072]{1,0:T(8,128)(2,1)S(1)}, u32[]{:S(2)}, u32[]{:S(2)}) collective-permute-start(bf16[64,3072]{1,0:T(8,128)(2,1)S(1)} %get-tuple-element.28), channel_id=1, source_target_pairs={{0,8},{2,10},{12,4},{14,6},{1,9},{3,11},{13,5},{15,7},{16,24},{18,... | collective-permute-start | bytes 1179656 | tf_op jit(solution)/shard_map/ppermute | solution.py:176
  9.8 19.7 %collective-permute-start.9 = (bf16[64,3072]{1,0:T(8,128)(2,1)S(1)}, bf16[64,3072]{1,0:T(8,128)(2,1)S(1)}, u32[]{:S(2)}, u32[]{:S(2)}) collective-permute-start(bf16[64,3072]{1,0:T(8,128)(2,1)S(1)} %get-tuple-element.27), channel_id=1, source_target_pairs={{0,12},{2,14},{12,0},{14,2},{1,13},{3,15},{13,1},{15,3},{16,28},{1... | collective-permute-start | bytes 1179656 | tf_op jit(solution)/shard_map/ppermute | solution.py:176
  13.1 16.5 %collective-permute-start.5 = (bf16[64,4096]{1,0:T(8,128)(2,1)S(1)}, bf16[64,4096]{1,0:T(8,128)(2,1)S(1)}, u32[]{:S(2)}, u32[]{:S(2)}) collective-permute-start(bf16[64,4096]{1,0:T(8,128)(2,1)S(1)} %constant_dynamic-slice_fusion.5), channel_id=1, source_target_pairs={{4,8},{6,10},{8,4},{10,6},{5,9},{7,11},{9,5},{11,7},{20,24},{22,26... | collective-permute-start | bytes 1572872 | tf_op jit(solution)/shard_map/ppermute | solution.py:176
  13.8 21.7 %collective-permute-start.3 = (bf16[64,3072]{1,0:T(8,128)(2,1)S(1)}, bf16[64,3072]{1,0:T(8,128)(2,1)S(1)}, u32[]{:S(2)}, u32[]{:S(2)}) collective-permute-start(bf16[64,3072]{1,0:T(8,128)(2,1)S(1)} %get-tuple-element.29), channel_id=1, source_target_pairs={{0,4},{2,6},{4,0},{6,2},{8,12},{10,14},{12,8},{14,10},{1,5},{3,7},... | collective-permute-start | bytes 1179656 | tf_op jit(solution)/shard_map/ppermute | solution.py:176
  14.6 46.1 %collective-permute-start.2 = (bf16[64,2560]{1,0:T(8,128)(2,1)}, bf16[64,2560]{1,0:T(8,128)(2,1)S(1)}, u32[]{:S(2)}, u32[]{:S(2)}) collective-permute-start(bf16[64,2560]{1,0:T(8,128)(2,1)} %constant_dynamic-slice_fusion.8), channel_id=1, source_target_pairs={{0,2},{2,0},{4,6},{6,4},{8,10},{10,8},{12,14},{14,12},{1,3},{3,1},... | collective-permute-start | bytes 983048 | tf_op jit(solution)/shard_map/ppermute | solution.py:181
  29.6 21.6 %collective-permute-start.6 = (bf16[64,3072]{1,0:T(8,128)(2,1)S(1)}, bf16[64,3072]{1,0:T(8,128)(2,1)S(1)}, u32[]{:S(2)}, u32[]{:S(2)}) collective-permute-start(bf16[64,3072]{1,0:T(8,128)(2,1)S(1)} %constant_dynamic-slice_fusion.4), channel_id=1, source_target_pairs={{8,12},{10,14},{4,0},{6,2},{9,13},{11,15},{5,1},{7,3},{24,28},{26,... | collective-permute-start | bytes 1179656 | tf_op jit(solution)/shard_map/ppermute | solution.py:176
  31.7 33.3 %collective-permute-start.10 = (bf16[64,2560]{1,0:T(8,128)(2,1)}, bf16[64,2560]{1,0:T(8,128)(2,1)S(1)}, u32[]{:S(2)}, u32[]{:S(2)}) collective-permute-start(bf16[64,2560]{1,0:T(8,128)(2,1)} %constant_dynamic-slice_fusion), channel_id=1, source_target_pairs={{0,2},{2,0},{4,6},{6,4},{8,10},{10,8},{12,14},{14,12},{1,3},{3,1},... | collective-permute-start | bytes 983048 | tf_op jit(solution)/shard_map/ppermute | solution.py:181
  36.3 33.0 %collective-permute-start.4 = (bf16[64,2560]{1,0:T(8,128)(2,1)}, bf16[64,2560]{1,0:T(8,128)(2,1)S(1)}, u32[]{:S(2)}, u32[]{:S(2)}) collective-permute-start(bf16[64,2560]{1,0:T(8,128)(2,1)} %constant_dynamic-slice_fusion.6), channel_id=1, source_target_pairs={{0,2},{2,0},{4,6},{6,4},{8,10},{10,8},{12,14},{14,12},{1,3},{3,1},... | collective-permute-start | bytes 983048 | tf_op jit(solution)/shard_map/ppermute | solution.py:181
  52.1 21.5 %collective-permute-start.7 = (bf16[64,2560]{1,0:T(8,128)(2,1)}, bf16[64,2560]{1,0:T(8,128)(2,1)S(1)}, u32[]{:S(2)}, u32[]{:S(2)}) collective-permute-start(bf16[64,2560]{1,0:T(8,128)(2,1)} %constant_dynamic-slice_fusion.3), channel_id=1, source_target_pairs={{0,2},{2,0},{4,6},{6,4},{8,10},{10,8},{12,14},{14,12},{1,3},{3,1},... | collective-permute-start | bytes 983048 | tf_op jit(solution)/shard_map/ppermute | solution.py:181
  53.7 1.6 %copy-start = (bf16[1,4,16,128,128]{4,3,2,1,0:T(8,128)(2,1)S(1)}, bf16[1,4,16,128,128]{4,3,2,1,0:T(8,128)(2,1)}, u32[]{:S(2)}) copy-start(bf16[1,4,16,128,128]{4,3,2,1,0:T(8,128)(2,1)} %gyro.1) | copy-start | bytes 6291460
  55.3 1.6 %copy-start.1 = (bf16[1,4,16,128,128]{4,3,2,1,0:T(8,128)(2,1)S(1)}, bf16[1,4,16,128,128]{4,3,2,1,0:T(8,128)(2,1)}, u32[]{:S(2)}) copy-start(bf16[1,4,16,128,128]{4,3,2,1,0:T(8,128)(2,1)} %spin.1) | copy-start | bytes 6291460
  79.3 2.0 %collective-permute-start.11 = (bf16[2,512,256]{2,1,0:T(8,128)(2,1)S(1)}, bf16[2,512,256]{2,1,0:T(8,128)(2,1)S(1)}, u32[]{:S(2)}, u32[]{:S(2)}) collective-permute-start(bf16[2,512,256]{2,1,0:T(8,128)(2,1)S(1)} %get-tuple-element.24), channel_id=1, source_target_pairs={{0,1},{1,0},{2,3},{3,2},{4,5},{5,4},{6,7},{7,6},{8,9},{9,8},{10,11... | collective-permute-start | bytes 1572872 | tf_op jit(solution)/shard_map/ppermute | solution.py:210
  81.5 6.5 %collective-permute-start.12 = (bf16[2,64,256]{2,1,0:T(8,128)(2,1)S(1)}, bf16[2,64,256]{2,1,0:T(8,128)(2,1)S(1)}, u32[]{:S(2)}, u32[]{:S(2)}) collective-permute-start(bf16[2,64,256]{2,1,0:T(8,128)(2,1)S(1)} %get-tuple-element.30), channel_id=1, source_target_pairs={{0,2},{2,0},{4,6},{6,4},{8,10},{10,8},{12,14},{14,12},{1,3},{3,1},... | collective-permute-start | bytes 196616 | tf_op jit(solution)/shard_map/ppermute | solution.py:216
  82.1 8.3 %collective-permute-start.13 = (bf16[2,64,256]{2,1,0:T(8,128)(2,1)S(1)}, bf16[2,64,256]{2,1,0:T(8,128)(2,1)S(1)}, u32[]{:S(2)}, u32[]{:S(2)}) collective-permute-start(bf16[2,64,256]{2,1,0:T(8,128)(2,1)S(1)} %get-tuple-element.36), channel_id=1, source_target_pairs={{0,4},{2,6},{4,0},{6,2},{8,12},{10,14},{12,8},{14,10},{1,5},{3,7},... | collective-permute-start | bytes 196616 | tf_op jit(solution)/shard_map/ppermute | solution.py:216
  82.1 10.6 %collective-permute-start.14 = (bf16[2,64,256]{2,1,0:T(8,128)(2,1)S(1)}, bf16[2,64,256]{2,1,0:T(8,128)(2,1)S(1)}, u32[]{:S(2)}, u32[]{:S(2)}) collective-permute-start(bf16[2,64,256]{2,1,0:T(8,128)(2,1)S(1)} %get-tuple-element.35), channel_id=1, source_target_pairs={{0,6},{2,4},{4,2},{6,0},{8,14},{10,12},{12,10},{14,8},{1,7},{3,5},... | collective-permute-start | bytes 196616 | tf_op jit(solution)/shard_map/ppermute | solution.py:216
  85.0 10.1 %collective-permute-start.15 = (bf16[2,64,256]{2,1,0:T(8,128)(2,1)S(1)}, bf16[2,64,256]{2,1,0:T(8,128)(2,1)S(1)}, u32[]{:S(2)}, u32[]{:S(2)}) collective-permute-start(bf16[2,64,256]{2,1,0:T(8,128)(2,1)S(1)} %get-tuple-element.34), channel_id=1, source_target_pairs={{0,8},{2,10},{4,12},{6,14},{8,0},{10,2},{12,4},{14,6},{1,9},{3,11}... | collective-permute-start | bytes 196616 | tf_op jit(solution)/shard_map/ppermute | solution.py:216
  86.1 10.2 %collective-permute-start.16 = (bf16[2,64,256]{2,1,0:T(8,128)(2,1)S(1)}, bf16[2,64,256]{2,1,0:T(8,128)(2,1)S(1)}, u32[]{:S(2)}, u32[]{:S(2)}) collective-permute-start(bf16[2,64,256]{2,1,0:T(8,128)(2,1)S(1)} %get-tuple-element.33), channel_id=1, source_target_pairs={{0,10},{2,8},{4,14},{6,12},{8,2},{10,0},{12,6},{14,4},{1,11},{3,9}... | collective-permute-start | bytes 196616 | tf_op jit(solution)/shard_map/ppermute | solution.py:216
  88.0 8.3 %collective-permute-start.17 = (bf16[2,64,256]{2,1,0:T(8,128)(2,1)S(1)}, bf16[2,64,256]{2,1,0:T(8,128)(2,1)S(1)}, u32[]{:S(2)}, u32[]{:S(2)}) collective-permute-start(bf16[2,64,256]{2,1,0:T(8,128)(2,1)S(1)} %get-tuple-element.32), channel_id=1, source_target_pairs={{0,12},{2,14},{4,8},{6,10},{8,4},{10,6},{12,0},{14,2},{1,13},{3,15... | collective-permute-start | bytes 196616 | tf_op jit(solution)/shard_map/ppermute | solution.py:216
  90.4 7.1 %collective-permute-start.18 = (bf16[2,64,256]{2,1,0:T(8,128)(2,1)S(1)}, bf16[2,64,256]{2,1,0:T(8,128)(2,1)S(1)}, u32[]{:S(2)}, u32[]{:S(2)}) collective-permute-start(bf16[2,64,256]{2,1,0:T(8,128)(2,1)S(1)} %get-tuple-element.31), channel_id=1, source_target_pairs={{0,14},{2,12},{4,10},{6,8},{8,6},{10,4},{12,2},{14,0},{1,15},{3,13... | collective-permute-start | bytes 196616 | tf_op jit(solution)/shard_map/ppermute | solution.py:216

commit v2 on v0

v2 whole, which is shorter than its diff:
```python
import functools
import math

import jax
import jax.numpy as jnp
from jax import lax
from jax.experimental import pallas as pl
from jax.experimental.pallas import tpu as pltpu
from jax.sharding import PartitionSpec as P

HB = 8
X = 2
VMEM_LIMIT = 24 * 1024 * 1024
NT = (((1,), (1,)), ((), ()))
VMEM = pl.BlockSpec(memory_space=pltpu.VMEM)
ANY = pl.BlockSpec(memory_space=pl.ANY)


def params():
    return pltpu.CompilerParams(vmem_limit_bytes=VMEM_LIMIT)


def ring(count):
    forward = [(i, (i + 1) % count) for i in range(count)]
    return forward, [(target, source) for source, target in forward]


def place_in_mode():
    m = lax.axis_index("mode")
    return m, lax.div(m, X), lax.rem(m, X)


def inside(z):
    return (z == 1) | (z == 2)


def aligned(index, size):
    return pl.multiple_of(index * size, size)


def band_kernel(per_unit, block_total, pattern, gyro, spin, _, band):
    row = pl.program_id(0)
    slots, size = gyro.shape[2:4]
    unit = lax.axis_index(("dof", "sub"))
    base = unit * per_unit + lax.axis_index("mode") * pl.num_programs(0) - HB
    band[...] = jnp.zeros_like(band)
    for slot in range(slots):
        column = lax.rem(pattern[0, row, slot] - base + block_total, block_total)
        where = pl.ds(aligned(column, size), size)
        band[0, 0, :, where] = gyro[0, 0, slot]
        band[1, 0, :, where] = spin[0, 0, slot]


def make_band(pattern, gyroscopic, centrifugal, after, width, per_unit, block_total):
    _, rows, slots, size, _ = gyroscopic.shape
    block = pl.BlockSpec((1, 1, slots, size, size), lambda j: (0, j, 0, 0, 0))
    band = pl.pallas_call(
        functools.partial(band_kernel, per_unit, block_total),
        out_shape=jax.ShapeDtypeStruct((2, rows, size, width), jnp.bfloat16),
        grid=(rows,),
        in_specs=[pl.BlockSpec(memory_space=pltpu.SMEM), block, block, ANY],
        out_specs=pl.BlockSpec((2, 1, size, width), lambda j: (0, j, 0, 0)),
        compiler_params=params(),
        cost_estimate=pl.CostEstimate(flops=0, bytes_accessed=2**23, transcendentals=0),
        name="band",
    )(pattern, gyroscopic, centrifugal, after)
    return band.reshape(2 * rows * size, width)


def first_kernel(group, phi, low, high, ext, inner, near, cross, own):
    m, z, _ = place_in_mode()
    rim = low.shape[1]
    ext[:, :rim] = low[...]
    ext[:, rim : rim + phi.shape[1]] = phi[...]
    ext[:, rim + phi.shape[1] :] = high[...]

    def cut(out, start):
        out[...] = ext[:, pl.ds(aligned(start, group), out.shape[1])]

    cut(inner, jnp.where(z == 1, 4, 0))
    cut(near, 2 * (z + 1 - 2 * lax.rem(z, 2)))
    cut(cross, m + 1 - 2 * lax.rem(m, 2))
    cut(own, m)


def second_kernel(group, ext, inner, near, _, passed, cross, own, skip, far):
    _, z, x = place_in_mode()

    def cut(out, source, start):
        out[...] = source[:, pl.ds(aligned(start, group), out.shape[1])]

    cut(passed, inner, jnp.where(z == 2, 2, 0))
    cut(skip, ext, jnp.where(z == 0, 4, 2))
    cut(far, ext, jnp.where(z == 0, 6, 0))
    cut(cross, near, 1 - x)
    cut(own, near, x)


def choose_kernel(group, shift, middle, corner, *refs):
    cross, own = refs[-2:]
    _, z, x = place_in_mode()

    def cut(source, start):
        cross[...] = source[:, pl.ds(aligned(start + 1 - x, group), cross.shape[1])]
        own[...] = source[:, pl.ds(aligned(start + x, group), own.shape[1])]

    @pl.when(inside(z))
    def _():
        cut(middle, jnp.where(z == 1, shift, 0))

    @pl.when(jnp.logical_not(inside(z)))
    def _():
        cut(corner, 0)


def cutting(kernel, widths, name, *operands, after=()):
    rows = operands[0].shape[0]
    return pl.pallas_call(
        kernel,
        out_shape=[jax.ShapeDtypeStruct((rows, w), jnp.bfloat16) for w in widths],
        in_specs=[VMEM] * len(operands) + [ANY] * len(after),
        out_specs=[VMEM] * len(widths),
        compiler_params=params(),
        name=name,
    )(*operands, *after)


def fill(lhs, centre, pieces, middle):
    width = pieces[0].shape[0]
    _, _, x = place_in_mode()
    for slot in range(len(pieces) // 2):
        for side in range(2):
            first = (2 * slot + side) * width
            piece = pieces[2 * slot + side]
            lhs[first : first + width, :] = piece[...]
            chip = lax.rem(x + side, 2)
            centre[slot, pl.ds(aligned(chip, width), width), :] = piece[:, middle]


def image_kernel(middle, *refs):
    pieces, (band, image, centre, lhs) = refs[:4], refs[4:]
    fill(lhs, centre, pieces, middle)
    image[...] = lax.dot_general(
        lhs[...], band[...], NT, preferred_element_type=jnp.float32
    ).astype(jnp.bfloat16)


def make_image(pieces, band, group):
    width, span = pieces[0].shape
    return pl.pallas_call(
        functools.partial(image_kernel, slice(2 * group, 3 * group)),
        out_shape=(
            jax.ShapeDtypeStruct((4 * width, band.shape[0]), jnp.bfloat16),
            jax.ShapeDtypeStruct((2, 2 * width, group), jnp.bfloat16),
        ),
        in_specs=[VMEM] * 5,
        out_specs=(VMEM, VMEM),
        scratch_shapes=[pltpu.VMEM((4 * width, span), jnp.bfloat16)],
        compiler_params=params(),
        cost_estimate=pl.CostEstimate(
            flops=8 * width * span * band.shape[0], bytes_accessed=2**22, transcendentals=0
        ),
        name="image",
    )(*pieces, band)


def project_kernel(middle, scaling, rows_out, *refs):
    pieces, (band, image, centre) = refs[:4], refs[4:7]
    keep, send, own_rows, stacked, late, lhs = refs[7:]
    _, z, _ = place_in_mode()
    pair = centre.shape[1]
    total, depth = own_rows.shape
    half = total // 2
    chunk = min(rows_out, pair)
    fill(lhs, late, pieces, middle)
    late_image = lax.dot_general(
        lhs[...], band[...], NT, preferred_element_type=jnp.float32
    ).astype(jnp.bfloat16)
    near = z + 1 - 2 * lax.rem(z, 2)
    third = jnp.where(inside(z), 3 - z, lax.rem(z + 2, 4))
    last = jnp.where(inside(z), lax.rem(z + 2, 4), 3 - z)
    third_at = jnp.where(inside(z), 3, 2)
    stacked[: 2 * pair, :] = image[...]
    stacked[pl.ds(aligned(third_at, pair), pair), :] = late_image[:pair]
    stacked[pl.ds(aligned(5 - third_at, pair), pair), :] = late_image[pair:]
    for slot, chip_row in enumerate((z, near, third, last)):
        source = (centre, late)[slot // 2]
        for piece in range(pair // chunk):
            first = chip_row * pair + piece * chunk
            target = (
                lax.rem(lax.div(first, rows_out), 2) * half
                + lax.div(first, 2 * rows_out) * rows_out
                + lax.rem(first, rows_out)
            )
            own_rows[pl.ds(pl.multiple_of(target, chunk), chunk), :] = source[
                slot % 2, piece * chunk : (piece + 1) * chunk, :
            ]
    sub = lax.axis_index("sub")
    for matrix in range(2):
        part = stacked[:, matrix * depth : (matrix + 1) * depth]
        for out, side in ((send, 1 - sub), (keep, sub)):
            out[matrix] = (
                lax.dot_general(
                    part,
                    own_rows[pl.ds(aligned(side, half), half), :],
                    NT,
                    preferred_element_type=jnp.float32,
                )
                * scaling
            )


def make_projection(pieces, band, image, centre, group, scaling, rows_out):
    width, span = pieces[0].shape
    total = 8 * width
    part = jax.ShapeDtypeStruct((2, total, total // 2), jnp.float32)
    return pl.pallas_call(
        functools.partial(
            project_kernel, slice(2 * group, 3 * group), scaling, rows_out
        ),
        out_shape=(part, part),
        in_specs=[VMEM] * 7,
        out_specs=(VMEM, VMEM),
        scratch_shapes=[
            pltpu.VMEM((total, group), jnp.bfloat16),
            pltpu.VMEM((total, image.shape[1]), jnp.bfloat16),
            pltpu.VMEM(centre.shape, jnp.bfloat16),
            pltpu.VMEM((4 * width, span), jnp.bfloat16),
        ],
        compiler_params=params(),
        cost_estimate=pl.CostEstimate(
            flops=4 * total * total * group, bytes_accessed=2**22, transcendentals=0
        ),
        name="project",
    )(*pieces, band, image, centre)


def body(modes, gyroscopic, centrifugal, pattern):
    mode_count = lax.axis_size("mode")
    dof_count = lax.axis_size("dof")
    sub_count = lax.axis_size("sub")
    unit_count = dof_count * sub_count
    rows_dev = gyroscopic.shape[1]
    block_size = gyroscopic.shape[3]
    per_unit = rows_dev * mode_count
    block_total = unit_count * per_unit
    group = rows_dev * block_size
    width = modes.shape[1]
    total = width * mode_count

    def over_z(array, pairs):
        return lax.ppermute(
            array, "mode", [(s * X + i, t * X + i) for s, t in pairs for i in range(X)]
        )

    def over_x(array):
        return lax.ppermute(array, "mode", [(i, i ^ 1) for i in range(mode_count)])

    phi = modes.T
    forward, backward = ring(unit_count)
    rim = HB * block_size
    low = lax.ppermute(phi[:, phi.shape[1] - rim :], ("dof", "sub"), forward)
    high = lax.ppermute(phi[:, :rim], ("dof", "sub"), backward)

    w5, w6, w8 = 5 * group, 6 * group, 8 * group
    ext, inner_w, near_w, cross0_w, own0 = cutting(
        functools.partial(first_kernel, group),
        (phi.shape[1] + 2 * rim, w8, w6, w5, w5),
        "first",
        phi,
        low,
        high,
    )
    inner = over_z(inner_w, [(1, 2), (2, 1)])
    near = over_z(near_w, [(0, 1), (1, 0), (2, 3), (3, 2)])
    cross0 = over_x(cross0_w)
    band = make_band(pattern, gyroscopic, centrifugal, own0, w5, per_unit, block_total)

    passed_w, crossA_w, ownA, skip_w, far_w = cutting(
        functools.partial(second_kernel, group),
        (w6, w5, w5, w6, w6),
        "second",
        ext,
        inner,
        near,
        after=(band,),
    )
    passed = over_z(passed_w, [(2, 3), (1, 0)])
    skip = over_z(skip_w, [(0, 2), (3, 1)])
    far = over_z(far_w, [(0, 3), (3, 0)])
    crossA = over_x(crossA_w)
    image, centre = make_image((own0, cross0, ownA, crossA), band, group)

    crossB_w, ownB = cutting(
        functools.partial(choose_kernel, group, 2), (w5, w5), "third", inner, passed
    )
    crossB = over_x(crossB_w)
    crossC_w, ownC = cutting(
        functools.partial(choose_kernel, group, 0), (w5, w5), "fourth", skip, far, after=(image,)
    )
    crossC = over_x(crossC_w)

    scaling = 1.0 / math.sqrt(block_total * block_size)
    keep, send = make_projection(
        (ownB, crossB, ownC, crossC), band, image, centre, group, scaling, total // unit_count
    )
    got = lax.ppermute(send, "sub", [(0, 1), (1, 0)])
    chip = keep + got
    result = chip[:, :width]
    for j in range(mode_count - 1, 0, -1):
        message = chip[:, j * width : (j + 1) * width].astype(jnp.bfloat16)
        arrived = lax.ppermute(message, "mode", [(i, i ^ j) for i in range(mode_count)])
        result = result + arrived.astype(jnp.float32)
    if dof_count > 1:
        result = lax.psum_scatter(result, "dof", scatter_dimension=2, tiled=True)
    return result.transpose(0, 2, 1)


def solution(mesh):
    return jax.shard_map(
        body,
        mesh=mesh,
        in_specs=(
            P(("dof", "sub"), ("parts", "mode")),
            P(("parts", "dof", "sub"), "mode", None, None, None),
            P(("parts", "dof", "sub"), "mode", None, None, None),
            P(("dof", "sub"), "mode", None),
        ),
        out_specs=P("parts", ("dof", "sub"), "mode"),
        check_vma=False,
    )
```

time: 209 us -> 77.8 us (0.37)
  waiting for transfers between devices: 142 us -> 33 us
  starting transfers between devices: 0.55 us -> 31.5 us
  local copies, waits for them, and re-layouts: 34.4 us -> 5.92 us
  between operations: 13.4 us -> 0.13 us
  matrix products: 9.34 us -> 0 us
  other arithmetic: 8.38 us -> 0.91 us
  Pallas kernels: 0 us -> 6.05 us
    all_gather x1 -> x0, waiting for transfers between devices: 78.3 us -> none  [body(): wide_phi = lax.all_gather(modes, 'mode', axis=1, tiled=True)]
    reduce_scatter x1 -> x0, waiting for transfers between devices: 60 us -> none  [body(): lax.psum_scatter(partial_value, ('dof', 'mode', 'sub'), scatter_dimension...]
    ppermute x2 -> x19, starting transfers between devices: 0.51 us -> 31.5 us  [the longest x5 17 us: over_z(): lax.ppermute(array, 'mode', [(s * X + i, t * X + i) for s, t in pairs for...]
    ppermute x2 -> x19, waiting for transfers between devices: 3.2 us -> 33 us  [the longest x5 14.4 us: over_z(): lax.ppermute(array, 'mode', [(s * X + i, t * X + i) for s, t in pairs for...]
    dot_general x3 -> x0, matrix products: 9.34 us -> none  [the longest x1 4.8 us: body(): jnp.einsum('jkab,jkbn->jan', centrifugal[0], nearby, preferred_element_ty...]
    concatenate x1 -> x0, local copies, waits for them, and re-layouts: 8.58 us -> none  [extended_2(): block = jnp.concatenate([low, block, high], axis=dim)]
    gather x1 -> x0, local copies, waits for them, and re-layouts: 8.32 us -> none  [body(): nearby = ext_blocks[local_index]]
    concatenate x1 -> x0, other arithmetic: 7.68 us -> none  [extended_2(): block = jnp.concatenate([low, block, high], axis=dim)]
  transfers between devices with their start and end apart: 4 -> 19, of which waited for: 4 -> 11; matrix products, arithmetic and copies ran while one was open for 0% -> 0% of each run, Pallas kernels for 0% -> 5%
where the time goes in v2:
time: 77.8 us; the launch traced here: 77.5 us
  waiting for transfers between devices  33 us (42%)
  starting transfers between devices  31.5 us (40%)
  Pallas kernels  6.05 us (8%)
  local copies, waits for them, and re-layouts  5.92 us (8%)
  other arithmetic  0.91 us (1%)
    ppermute x5, starting transfers between devices, over_z(): lax.ppermute(array, 'mode', [(s * X + i, t * X + i) for s, t in pairs for...  17 us
    ppermute x5, waiting for transfers between devices, over_z(): lax.ppermute(array, 'mode', [(s * X + i, t * X + i) for s, t in pairs for...  14.4 us
    ppermute x7, starting transfers between devices, body(): lax.ppermute(message, 'mode', [(i, i ^ j) for i in range(mode_count)])  9.6 us
    ppermute x4, waiting for transfers between devices, over_x(): return lax.ppermute(array, 'mode', [(i, i ^ 1) for i in range(mode_count)])  7.4 us
    ppermute x7, waiting for transfers between devices, body(): lax.ppermute(message, 'mode', [(i, i ^ j) for i in range(mode_count)])  7.28 us
    unnamed x8, local copies, waits for them, and re-layouts  4.9 us
    ppermute x4, starting transfers between devices, over_x(): return lax.ppermute(array, 'mode', [(i, i ^ 1) for i in range(mode_count)])  4.25 us
    ppermute x1, waiting for transfers between devices, body(): got = lax.ppermute(send, 'sub', [(0, 1), (1, 0)])  2.65 us
  transfers between devices with their start and end apart: 19, of which 11 were waited for; matrix products, arithmetic and copies ran while one was open for 0% of the time, Pallas kernels for 5%

profile of v2, /device:TPU:0, one launch (start us, length us, event | category | flops | bytes accessed | tf_op | source)
XLA Modules:
  0.0 77.5 jit_solution(8545520695961077942)
XLA Ops:
  4.8 5.6 %collective-permute-start.3 = (bf16[64,3072]{1,0:T(8,128)(2,1)S(1)}, bf16[64,3072]{1,0:T(8,128)(2,1)S(1)}, u32[]{:S(2)}, u32[]{:S(2)}) collective-permute-start(bf16[64,3072]{1,0:T(8,128)(2,1)S(1)} %get-tuple-element.25), channel_id=1, source_target_pairs={{0,4},{2,6},{4,0},{6,2},{8,12},{10,14},{12,8},{14,10},{1,5},{3,7},... | collective-permute-start | bytes 1179656 | tf_op jit(solution)/shard_map/ppermute | solution.py:252
  10.4 1.5 %collective-permute-start.8 = (bf16[64,2560]{1,0:T(8,128)(2,1)S(1)}, bf16[64,2560]{1,0:T(8,128)(2,1)S(1)}, u32[]{:S(2)}, u32[]{:S(2)}) collective-permute-start(bf16[64,2560]{1,0:T(8,128)(2,1)S(1)} %get-tuple-element.32), channel_id=1, source_target_pairs={{0,2},{2,0},{4,6},{6,4},{8,10},{10,8},{12,14},{14,12},{1,3},{3,1},... | collective-permute-start | bytes 983048 | tf_op jit(solution)/shard_map/ppermute | solution.py:257
  11.9 1.6 %copy-done = bf16[1,4,16,128,128]{4,3,2,1,0:T(8,128)(2,1)S(1)} copy-done((bf16[1,4,16,128,128]{4,3,2,1,0:T(8,128)(2,1)S(1)}, bf16[1,4,16,128,128]{4,3,2,1,0:T(8,128)(2,1)}, u32[]{:S(2)}) %copy-start) | copy-done | bytes 2097176
  13.5 1.6 %copy-done.1 = bf16[1,4,16,128,128]{4,3,2,1,0:T(8,128)(2,1)S(1)} copy-done((bf16[1,4,16,128,128]{4,3,2,1,0:T(8,128)(2,1)S(1)}, bf16[1,4,16,128,128]{4,3,2,1,0:T(8,128)(2,1)}, u32[]{:S(2)}) %copy-start.1) | copy-done | bytes 2097176
  15.7 2.0 %band.1 = bf16[2,4,128,2560]{3,2,1,0:T(8,128)(2,1)S(1)} custom-call(s32[1,4,16]{2,1,0:T(4,128)S(1)} %copy-done.3, bf16[1,4,16,128,128]{4,3,2,1,0:T(8,128)(2,1)S(1)} %copy-done, bf16[1,4,16,128,128]{4,3,2,1,0:T(8,128)(2,1)S(1)} %copy-done.1, bf16[64,2560]{1,0:T(8,128)(2,1)S(1)} %get-tuple-element.26._.refs_0_), custom_call_target="tpu_custom_call" | custom-call | bytes 8388608 | tf_op jit(solution)/shard_map/band/pallas_call | solution.py:57
  17.8 1.9 %collective-permute-done.3.near = bf16[64,3072]{1,0:T(8,128)(2,1)S(1)} collective-permute-done((bf16[64,3072]{1,0:T(8,128)(2,1)S(1)}, bf16[64,3072]{1,0:T(8,128)(2,1)S(1)}, u32[]{:S(2)}, u32[]{:S(2)}) %collective-permute-start.3) | collective-permute-done | bytes 393248 | tf_op jit(solution)/shard_map/ppermute | solution.py:252
  19.8 1.6 %collective-permute-start.9 = (bf16[64,2560]{1,0:T(8,128)(2,1)S(1)}, bf16[64,2560]{1,0:T(8,128)(2,1)S(1)}, u32[]{:S(2)}, u32[]{:S(2)}) collective-permute-start(bf16[64,2560]{1,0:T(8,128)(2,1)S(1)} %get-tuple-element.34), channel_id=1, source_target_pairs={{0,2},{2,0},{4,6},{6,4},{8,10},{10,8},{12,14},{14,12},{1,3},{3,1},... | collective-permute-start | bytes 983048 | tf_op jit(solution)/shard_map/ppermute | solution.py:257
  21.4 1.3 %collective-permute-start.4 = (bf16[64,3072]{1,0:T(8,128)(2,1)S(1)}, bf16[64,3072]{1,0:T(8,128)(2,1)S(1)}, u32[]{:S(2)}, u32[]{:S(2)}) collective-permute-start(bf16[64,3072]{1,0:T(8,128)(2,1)S(1)} %get-tuple-element.27), channel_id=1, source_target_pairs={{8,12},{10,14},{4,0},{6,2},{9,13},{11,15},{5,1},{7,3},{24,28},{26,... | collective-permute-start | bytes 1179656 | tf_op jit(solution)/shard_map/ppermute | solution.py:252
  22.7 6.1 %collective-permute-start.6 = (bf16[64,3072]{1,0:T(8,128)(2,1)S(1)}, bf16[64,3072]{1,0:T(8,128)(2,1)S(1)}, u32[]{:S(2)}, u32[]{:S(2)}) collective-permute-start(bf16[64,3072]{1,0:T(8,128)(2,1)S(1)} %get-tuple-element.30), channel_id=1, source_target_pairs={{0,8},{2,10},{12,4},{14,6},{1,9},{3,11},{13,5},{15,7},{16,24},{18,... | collective-permute-start | bytes 1179656 | tf_op jit(solution)/shard_map/ppermute | solution.py:252
  28.8 3.3 %collective-permute-start.7 = (bf16[64,3072]{1,0:T(8,128)(2,1)S(1)}, bf16[64,3072]{1,0:T(8,128)(2,1)S(1)}, u32[]{:S(2)}, u32[]{:S(2)}) collective-permute-start(bf16[64,3072]{1,0:T(8,128)(2,1)S(1)} %get-tuple-element.31), channel_id=1, source_target_pairs={{0,12},{2,14},{12,0},{14,2},{1,13},{3,15},{13,1},{15,3},{16,28},{1... | collective-permute-start | bytes 1179656 | tf_op jit(solution)/shard_map/ppermute | solution.py:252
  32.1 1.6 %image.1 = (bf16[256,1024]{1,0:T(8,128)(2,1)S(1)}, bf16[2,128,512]{2,1,0:T(8,128)(2,1)S(1)}) custom-call(bf16[64,2560]{1,0:T(8,128)(2,1)S(1)} %get-tuple-element.26._.refs_0_, bf16[64,2560]{1,0:T(8,128)(2,1)S(1)} %collective-permute-done.8.refs_1_, bf16[64,2560]{1,0:T(8,128)(2,1)S(1)} %get-tuple-element.33.refs_2_, ...), custom_call_target="tpu_custom_call" | custom-call | flops 1342177280 | bytes 4194304 | tf_op jit(solution)/shard_map/image/pallas_call | solution.py:150
  35.0 3.4 %collective-permute-done.6.middle = bf16[64,3072]{1,0:T(8,128)(2,1)S(1)} collective-permute-done((bf16[64,3072]{1,0:T(8,128)(2,1)S(1)}, bf16[64,3072]{1,0:T(8,128)(2,1)S(1)}, u32[]{:S(2)}, u32[]{:S(2)}) %collective-permute-start.6) | collective-permute-done | bytes 393248 | tf_op jit(solution)/shard_map/ppermute | solution.py:252
  38.3 8.4 %collective-permute-done.7.corner = bf16[64,3072]{1,0:T(8,128)(2,1)S(1)} collective-permute-done((bf16[64,3072]{1,0:T(8,128)(2,1)S(1)}, bf16[64,3072]{1,0:T(8,128)(2,1)S(1)}, u32[]{:S(2)}, u32[]{:S(2)}) %collective-permute-start.7) | collective-permute-done | bytes 393248 | tf_op jit(solution)/shard_map/ppermute | solution.py:252
  47.4 7.4 %collective-permute-done.10.refs_3_ = bf16[64,2560]{1,0:T(8,128)(2,1)S(1)} collective-permute-done((bf16[64,2560]{1,0:T(8,128)(2,1)S(1)}, bf16[64,2560]{1,0:T(8,128)(2,1)S(1)}, u32[]{:S(2)}, u32[]{:S(2)}) %collective-permute-start.10) | collective-permute-done | bytes 327712 | tf_op jit(solution)/shard_map/ppermute | solution.py:257
  54.8 2.1 %project.1 = (f32[2,512,256]{2,1,0:T(8,128)S(1)}, f32[2,512,256]{2,1,0:T(8,128)S(1)}) custom-call(bf16[64,2560]{1,0:T(8,128)(2,1)S(1)} %get-tuple-element.28.refs_0_, bf16[64,2560]{1,0:T(8,128)(2,1)S(1)} %collective-permute-done.5.refs_1_, bf16[64,2560]{1,0:T(8,128)(2,1)S(1)} %get-tuple-element.36.refs_2_, ...), custom_call_target="tpu_custom_call" | custom-call | flops 536870912 | bytes 4194304 | tf_op jit(solution)/shard_map/project/pallas_call | solution.py:217
  57.0 2.6 %collective-permute-done.11 = f32[2,512,256]{2,1,0:T(8,128)S(1)} collective-permute-done((f32[2,512,256]{2,1,0:T(8,128)S(1)}, f32[2,512,256]{2,1,0:T(8,128)S(1)}, u32[]{:S(2)}, u32[]{:S(2)}) %collective-permute-start.11) | collective-permute-done | bytes 1048608 | tf_op jit(solution)/shard_map/ppermute | solution.py:307
  59.9 2.5 %collective-permute-start.12 = (bf16[2,64,256]{2,1,0:T(8,128)(2,1)S(1)}, bf16[2,64,256]{2,1,0:T(8,128)(2,1)S(1)}, u32[]{:S(2)}, u32[]{:S(2)}) collective-permute-start(bf16[2,64,256]{2,1,0:T(8,128)(2,1)S(1)} %get-tuple-element.43), channel_id=1, source_target_pairs={{0,14},{2,12},{4,10},{6,8},{8,6},{10,4},{12,2},{14,0},{1,15},{3,13... | collective-permute-start | bytes 196616 | tf_op jit(solution)/shard_map/ppermute | solution.py:312
  62.4 1.5 %collective-permute-start.18 = (bf16[2,64,256]{2,1,0:T(8,128)(2,1)S(1)}, bf16[2,64,256]{2,1,0:T(8,128)(2,1)S(1)}, u32[]{:S(2)}, u32[]{:S(2)}) collective-permute-start(bf16[2,64,256]{2,1,0:T(8,128)(2,1)S(1)} %get-tuple-element.44), channel_id=1, source_target_pairs={{0,2},{2,0},{4,6},{6,4},{8,10},{10,8},{12,14},{14,12},{1,3},{3,1},... | collective-permute-start | bytes 196616 | tf_op jit(solution)/shard_map/ppermute | solution.py:312
  63.9 2.0 %collective-permute-start.16 = (bf16[2,64,256]{2,1,0:T(8,128)(2,1)S(1)}, bf16[2,64,256]{2,1,0:T(8,128)(2,1)S(1)}, u32[]{:S(2)}, u32[]{:S(2)}) collective-permute-start(bf16[2,64,256]{2,1,0:T(8,128)(2,1)S(1)} %get-tuple-element.46), channel_id=1, source_target_pairs={{0,6},{2,4},{4,2},{6,0},{8,14},{10,12},{12,10},{14,8},{1,7},{3,5},... | collective-permute-start | bytes 196616 | tf_op jit(solution)/shard_map/ppermute | solution.py:312
  65.9 1.6 %collective-permute-done.12 = bf16[2,64,256]{2,1,0:T(8,128)(2,1)S(1)} collective-permute-done((bf16[2,64,256]{2,1,0:T(8,128)(2,1)S(1)}, bf16[2,64,256]{2,1,0:T(8,128)(2,1)S(1)}, u32[]{:S(2)}, u32[]{:S(2)}) %collective-permute-start.12) | collective-permute-done | bytes 65568 | tf_op jit(solution)/shard_map/ppermute | solution.py:312
  67.5 2.2 %collective-permute-start.14 = (bf16[2,64,256]{2,1,0:T(8,128)(2,1)S(1)}, bf16[2,64,256]{2,1,0:T(8,128)(2,1)S(1)}, u32[]{:S(2)}, u32[]{:S(2)}) collective-permute-start(bf16[2,64,256]{2,1,0:T(8,128)(2,1)S(1)} %get-tuple-element.48), channel_id=1, source_target_pairs={{0,10},{2,8},{4,14},{6,12},{8,2},{10,0},{12,6},{14,4},{1,11},{3,9}... | collective-permute-start | bytes 196616 | tf_op jit(solution)/shard_map/ppermute | solution.py:312
  69.7 1.3 %collective-permute-start.13 = (bf16[2,64,256]{2,1,0:T(8,128)(2,1)S(1)}, bf16[2,64,256]{2,1,0:T(8,128)(2,1)S(1)}, u32[]{:S(2)}, u32[]{:S(2)}) collective-permute-start(bf16[2,64,256]{2,1,0:T(8,128)(2,1)S(1)} %get-tuple-element.49), channel_id=1, source_target_pairs={{0,12},{2,14},{4,8},{6,10},{8,4},{10,6},{12,0},{14,2},{1,13},{3,15... | collective-permute-start | bytes 196616 | tf_op jit(solution)/shard_map/ppermute | solution.py:312
  71.1 3.1 %collective-permute-done.15 = bf16[2,64,256]{2,1,0:T(8,128)(2,1)S(1)} collective-permute-done((bf16[2,64,256]{2,1,0:T(8,128)(2,1)S(1)}, bf16[2,64,256]{2,1,0:T(8,128)(2,1)S(1)}, u32[]{:S(2)}, u32[]{:S(2)}) %collective-permute-start.15) | collective-permute-done | bytes 65568 | tf_op jit(solution)/shard_map/ppermute | solution.py:312
  74.2 2.6 %collective-permute-done.14 = bf16[2,64,256]{2,1,0:T(8,128)(2,1)S(1)} collective-permute-done((bf16[2,64,256]{2,1,0:T(8,128)(2,1)S(1)}, bf16[2,64,256]{2,1,0:T(8,128)(2,1)S(1)}, u32[]{:S(2)}, u32[]{:S(2)}) %collective-permute-start.14) | collective-permute-done | bytes 65568 | tf_op jit(solution)/shard_map/ppermute | solution.py:312
  (33 shorter events, 8.5 us)
Async XLA Ops:
  1.0 1.5 %collective-permute-start.1 = (bf16[64,1024]{1,0:T(8,128)(2,1)S(1)}, bf16[64,1024]{1,0:T(8,128)(2,1)S(1)}, u32[]{:S(2)}, u32[]{:S(2)}) collective-permute-start(bf16[64,1024]{1,0:T(8,128)(2,1)S(1)} %get-tuple-element.50), channel_id=1, source_target_pairs={{1,0},{0,1},{3,2},{2,3},{5,4},{4,5},{7,6},{6,7},{9,8},{8,9},{11,10... | collective-permute-start | bytes 393224 | tf_op jit(solution)/shard_map/ppermute | solution.py:263
  1.5 1.3 %collective-permute-start = (bf16[64,1024]{1,0:T(8,128)(2,1)S(1)}, bf16[64,1024]{1,0:T(8,128)(2,1)S(1)}, u32[]{:S(2)}, u32[]{:S(2)}) collective-permute-start(bf16[64,1024]{1,0:T(8,128)(2,1)S(1)} %get-tuple-element.51), channel_id=1, source_target_pairs={{0,1},{1,0},{2,3},{3,2},{4,5},{5,4},{6,7},{7,6},{8,9},{9,8},{10,11... | collective-permute-start | bytes 393224 | tf_op jit(solution)/shard_map/ppermute | solution.py:262
  2.9 1.0 %copy-start.2 = (bf16[4096,64]{0,1:T(8,128)(2,1)S(1)}, bf16[4096,64]{0,1:T(8,128)(2,1)}, u32[]{:S(2)}) copy-start(bf16[4096,64]{0,1:T(8,128)(2,1)} %param.4) | copy-start | bytes 1572868
  4.1 15.6 %collective-permute-start.2 = (bf16[64,4096]{1,0:T(8,128)(2,1)S(1)}, bf16[64,4096]{1,0:T(8,128)(2,1)S(1)}, u32[]{:S(2)}, u32[]{:S(2)}) collective-permute-start(bf16[64,4096]{1,0:T(8,128)(2,1)S(1)} %get-tuple-element.23), channel_id=1, source_target_pairs={{4,8},{6,10},{8,4},{10,6},{5,9},{7,11},{9,5},{11,7},{20,24},{22,26... | collective-permute-start | bytes 1572872 | tf_op jit(solution)/shard_map/ppermute | solution.py:252
  4.8 14.9 %collective-permute-start.3 = (bf16[64,3072]{1,0:T(8,128)(2,1)S(1)}, bf16[64,3072]{1,0:T(8,128)(2,1)S(1)}, u32[]{:S(2)}, u32[]{:S(2)}) collective-permute-start(bf16[64,3072]{1,0:T(8,128)(2,1)S(1)} %get-tuple-element.25), channel_id=1, source_target_pairs={{0,4},{2,6},{4,0},{6,2},{8,12},{10,14},{12,8},{14,10},{1,5},{3,7},... | collective-permute-start | bytes 1179656 | tf_op jit(solution)/shard_map/ppermute | solution.py:252
  10.4 21.7 %collective-permute-start.8 = (bf16[64,2560]{1,0:T(8,128)(2,1)S(1)}, bf16[64,2560]{1,0:T(8,128)(2,1)S(1)}, u32[]{:S(2)}, u32[]{:S(2)}) collective-permute-start(bf16[64,2560]{1,0:T(8,128)(2,1)S(1)} %get-tuple-element.32), channel_id=1, source_target_pairs={{0,2},{2,0},{4,6},{6,4},{8,10},{10,8},{12,14},{14,12},{1,3},{3,1},... | collective-permute-start | bytes 983048 | tf_op jit(solution)/shard_map/ppermute | solution.py:257
  11.9 1.6 %copy-start = (bf16[1,4,16,128,128]{4,3,2,1,0:T(8,128)(2,1)S(1)}, bf16[1,4,16,128,128]{4,3,2,1,0:T(8,128)(2,1)}, u32[]{:S(2)}) copy-start(bf16[1,4,16,128,128]{4,3,2,1,0:T(8,128)(2,1)} %gyro.1) | copy-start | bytes 6291460
  13.5 1.6 %copy-start.1 = (bf16[1,4,16,128,128]{4,3,2,1,0:T(8,128)(2,1)S(1)}, bf16[1,4,16,128,128]{4,3,2,1,0:T(8,128)(2,1)}, u32[]{:S(2)}) copy-start(bf16[1,4,16,128,128]{4,3,2,1,0:T(8,128)(2,1)} %spin.1) | copy-start | bytes 6291460
  15.0 0.7 copy-start.3
  19.8 12.3 %collective-permute-start.9 = (bf16[64,2560]{1,0:T(8,128)(2,1)S(1)}, bf16[64,2560]{1,0:T(8,128)(2,1)S(1)}, u32[]{:S(2)}, u32[]{:S(2)}) collective-permute-start(bf16[64,2560]{1,0:T(8,128)(2,1)S(1)} %get-tuple-element.34), channel_id=1, source_target_pairs={{0,2},{2,0},{4,6},{6,4},{8,10},{10,8},{12,14},{14,12},{1,3},{3,1},... | collective-permute-start | bytes 983048 | tf_op jit(solution)/shard_map/ppermute | solution.py:257
  21.4 12.9 %collective-permute-start.4 = (bf16[64,3072]{1,0:T(8,128)(2,1)S(1)}, bf16[64,3072]{1,0:T(8,128)(2,1)S(1)}, u32[]{:S(2)}, u32[]{:S(2)}) collective-permute-start(bf16[64,3072]{1,0:T(8,128)(2,1)S(1)} %get-tuple-element.27), channel_id=1, source_target_pairs={{8,12},{10,14},{4,0},{6,2},{9,13},{11,15},{5,1},{7,3},{24,28},{26,... | collective-permute-start | bytes 1179656 | tf_op jit(solution)/shard_map/ppermute | solution.py:252
  22.7 15.7 %collective-permute-start.6 = (bf16[64,3072]{1,0:T(8,128)(2,1)S(1)}, bf16[64,3072]{1,0:T(8,128)(2,1)S(1)}, u32[]{:S(2)}, u32[]{:S(2)}) collective-permute-start(bf16[64,3072]{1,0:T(8,128)(2,1)S(1)} %get-tuple-element.30), channel_id=1, source_target_pairs={{0,8},{2,10},{12,4},{14,6},{1,9},{3,11},{13,5},{15,7},{16,24},{18,... | collective-permute-start | bytes 1179656 | tf_op jit(solution)/shard_map/ppermute | solution.py:252
  28.8 18.0 %collective-permute-start.7 = (bf16[64,3072]{1,0:T(8,128)(2,1)S(1)}, bf16[64,3072]{1,0:T(8,128)(2,1)S(1)}, u32[]{:S(2)}, u32[]{:S(2)}) collective-permute-start(bf16[64,3072]{1,0:T(8,128)(2,1)S(1)} %get-tuple-element.31), channel_id=1, source_target_pairs={{0,12},{2,14},{12,0},{14,2},{1,13},{3,15},{13,1},{15,3},{16,28},{1... | collective-permute-start | bytes 1179656 | tf_op jit(solution)/shard_map/ppermute | solution.py:252
  34.4 13.0 %collective-permute-start.5 = (bf16[64,2560]{1,0:T(8,128)(2,1)S(1)}, bf16[64,2560]{1,0:T(8,128)(2,1)S(1)}, u32[]{:S(2)}, u32[]{:S(2)}) collective-permute-start(bf16[64,2560]{1,0:T(8,128)(2,1)S(1)} %get-tuple-element.29), channel_id=1, source_target_pairs={{0,2},{2,0},{4,6},{6,4},{8,10},{10,8},{12,14},{14,12},{1,3},{3,1},... | collective-permute-start | bytes 983048 | tf_op jit(solution)/shard_map/ppermute | solution.py:257
  46.8 8.0 %collective-permute-start.10 = (bf16[64,2560]{1,0:T(8,128)(2,1)S(1)}, bf16[64,2560]{1,0:T(8,128)(2,1)S(1)}, u32[]{:S(2)}, u32[]{:S(2)}) collective-permute-start(bf16[64,2560]{1,0:T(8,128)(2,1)S(1)} %get-tuple-element.37), channel_id=1, source_target_pairs={{0,2},{2,0},{4,6},{6,4},{8,10},{10,8},{12,14},{14,12},{1,3},{3,1},... | collective-permute-start | bytes 983048 | tf_op jit(solution)/shard_map/ppermute | solution.py:257
  56.9 2.7 %collective-permute-start.11 = (f32[2,512,256]{2,1,0:T(8,128)S(1)}, f32[2,512,256]{2,1,0:T(8,128)S(1)}, u32[]{:S(2)}, u32[]{:S(2)}) collective-permute-start(f32[2,512,256]{2,1,0:T(8,128)S(1)} %get-tuple-element.40), channel_id=1, source_target_pairs={{0,1},{1,0},{2,3},{3,2},{4,5},{5,4},{6,7},{7,6},{8,9},{9,8},{10,11... | collective-permute-start | bytes 3145736 | tf_op jit(solution)/shard_map/ppermute | solution.py:307
  59.9 7.6 %collective-permute-start.12 = (bf16[2,64,256]{2,1,0:T(8,128)(2,1)S(1)}, bf16[2,64,256]{2,1,0:T(8,128)(2,1)S(1)}, u32[]{:S(2)}, u32[]{:S(2)}) collective-permute-start(bf16[2,64,256]{2,1,0:T(8,128)(2,1)S(1)} %get-tuple-element.43), channel_id=1, source_target_pairs={{0,14},{2,12},{4,10},{6,8},{8,6},{10,4},{12,2},{14,0},{1,15},{3,13... | collective-permute-start | bytes 196616 | tf_op jit(solution)/shard_map/ppermute | solution.py:312
  62.4 7.3 %collective-permute-start.18 = (bf16[2,64,256]{2,1,0:T(8,128)(2,1)S(1)}, bf16[2,64,256]{2,1,0:T(8,128)(2,1)S(1)}, u32[]{:S(2)}, u32[]{:S(2)}) collective-permute-start(bf16[2,64,256]{2,1,0:T(8,128)(2,1)S(1)} %get-tuple-element.44), channel_id=1, source_target_pairs={{0,2},{2,0},{4,6},{6,4},{8,10},{10,8},{12,14},{14,12},{1,3},{3,1},... | collective-permute-start | bytes 196616 | tf_op jit(solution)/shard_map/ppermute | solution.py:312
  63.9 7.2 %collective-permute-start.17 = (bf16[2,64,256]{2,1,0:T(8,128)(2,1)S(1)}, bf16[2,64,256]{2,1,0:T(8,128)(2,1)S(1)}, u32[]{:S(2)}, u32[]{:S(2)}) collective-permute-start(bf16[2,64,256]{2,1,0:T(8,128)(2,1)S(1)} %get-tuple-element.45), channel_id=1, source_target_pairs={{0,4},{2,6},{4,0},{6,2},{8,12},{10,14},{12,8},{14,10},{1,5},{3,7},... | collective-permute-start | bytes 196616 | tf_op jit(solution)/shard_map/ppermute | solution.py:312
  63.9 7.2 %collective-permute-start.16 = (bf16[2,64,256]{2,1,0:T(8,128)(2,1)S(1)}, bf16[2,64,256]{2,1,0:T(8,128)(2,1)S(1)}, u32[]{:S(2)}, u32[]{:S(2)}) collective-permute-start(bf16[2,64,256]{2,1,0:T(8,128)(2,1)S(1)} %get-tuple-element.46), channel_id=1, source_target_pairs={{0,6},{2,4},{4,2},{6,0},{8,14},{10,12},{12,10},{14,8},{1,7},{3,5},... | collective-permute-start | bytes 196616 | tf_op jit(solution)/shard_map/ppermute | solution.py:312
  65.9 8.3 %collective-permute-start.15 = (bf16[2,64,256]{2,1,0:T(8,128)(2,1)S(1)}, bf16[2,64,256]{2,1,0:T(8,128)(2,1)S(1)}, u32[]{:S(2)}, u32[]{:S(2)}) collective-permute-start(bf16[2,64,256]{2,1,0:T(8,128)(2,1)S(1)} %get-tuple-element.47), channel_id=1, source_target_pairs={{0,8},{2,10},{4,12},{6,14},{8,0},{10,2},{12,4},{14,6},{1,9},{3,11}... | collective-permute-start | bytes 196616 | tf_op jit(solution)/shard_map/ppermute | solution.py:312
  67.5 9.3 %collective-permute-start.14 = (bf16[2,64,256]{2,1,0:T(8,128)(2,1)S(1)}, bf16[2,64,256]{2,1,0:T(8,128)(2,1)S(1)}, u32[]{:S(2)}, u32[]{:S(2)}) collective-permute-start(bf16[2,64,256]{2,1,0:T(8,128)(2,1)S(1)} %get-tuple-element.48), channel_id=1, source_target_pairs={{0,10},{2,8},{4,14},{6,12},{8,2},{10,0},{12,6},{14,4},{1,11},{3,9}... | collective-permute-start | bytes 196616 | tf_op jit(solution)/shard_map/ppermute | solution.py:312
  69.7 7.0 %collective-permute-start.13 = (bf16[2,64,256]{2,1,0:T(8,128)(2,1)S(1)}, bf16[2,64,256]{2,1,0:T(8,128)(2,1)S(1)}, u32[]{:S(2)}, u32[]{:S(2)}) collective-permute-start(bf16[2,64,256]{2,1,0:T(8,128)(2,1)S(1)} %get-tuple-element.49), channel_id=1, source_target_pairs={{0,12},{2,14},{4,8},{6,10},{8,4},{10,6},{12,0},{14,2},{1,13},{3,15... | collective-permute-start | bytes 196616 | tf_op jit(solution)/shard_map/ppermute | solution.py:312

commit v3 on v2

--- a/solution.py
+++ b/solution.py
@@ -67,50 +67,63 @@
     return band.reshape(2 * rows * size, width)
 
 
-def first_kernel(group, phi, low, high, ext, inner, near, cross, own):
+def rim_kernel(phi, low, high):
+    low[...] = phi[:, phi.shape[1] - low.shape[1] :]
+    high[...] = phi[:, : high.shape[1]]
+
+
+def cut(group, out, source, start):
+    out[...] = source[:, pl.ds(aligned(start, group), out.shape[1])]
+
+
+def first_kernel(group, phi, low, high, ext, inner, far, near, cross, own):
     m, z, _ = place_in_mode()
     rim = low.shape[1]
     ext[:, :rim] = low[...]
     ext[:, rim : rim + phi.shape[1]] = phi[...]
     ext[:, rim + phi.shape[1] :] = high[...]
-
-    def cut(out, start):
-        out[...] = ext[:, pl.ds(aligned(start, group), out.shape[1])]
-
-    cut(inner, jnp.where(z == 1, 4, 0))
-    cut(near, 2 * (z + 1 - 2 * lax.rem(z, 2)))
-    cut(cross, m + 1 - 2 * lax.rem(m, 2))
-    cut(own, m)
-
-
-def second_kernel(group, ext, inner, near, _, passed, cross, own, skip, far):
+    cut(group, inner, ext, jnp.where(z == 1, 4, 0))
+    cut(group, far, ext, jnp.where(z == 0, 6, 0))
+    cut(group, near, ext, 2 * (z + 1 - 2 * lax.rem(z, 2)))
+    cut(group, cross, ext, m + 1 - 2 * lax.rem(m, 2))
+    cut(group, own, ext, m)
+
+
+def near_kernel(group, near, cross, own):
+    _, _, x = place_in_mode()
+    cut(group, cross, near, 1 - x)
+    cut(group, own, near, x)
+
+
+def middle_kernel(group, ext, inner, far, _, passed, skip, cross, own):
     _, z, x = place_in_mode()
-
-    def cut(out, source, start):
-        out[...] = source[:, pl.ds(aligned(start, group), out.shape[1])]
-
-    cut(passed, inner, jnp.where(z == 2, 2, 0))
-    cut(skip, ext, jnp.where(z == 0, 4, 2))
-    cut(far, ext, jnp.where(z == 0, 6, 0))
-    cut(cross, near, 1 - x)
-    cut(own, near, x)
-
-
-def choose_kernel(group, shift, middle, corner, *refs):
-    cross, own = refs[-2:]
-    _, z, x = place_in_mode()
-
-    def cut(source, start):
-        cross[...] = source[:, pl.ds(aligned(start + 1 - x, group), cross.shape[1])]
-        own[...] = source[:, pl.ds(aligned(start + x, group), own.shape[1])]
+    cut(group, passed, inner, jnp.where(z == 2, 2, 0))
+    cut(group, skip, ext, jnp.where(z == 0, 4, 2))
 
     @pl.when(inside(z))
     def _():
-        cut(middle, jnp.where(z == 1, shift, 0))
+        first = jnp.where(z == 1, 2, 0)
+        cut(group, cross, inner, first + 1 - x)
+        cut(group, own, inner, first + x)
 
     @pl.when(jnp.logical_not(inside(z)))
     def _():
-        cut(corner, 0)
+        cut(group, cross, far, 1 - x)
+        cut(group, own, far, x)
+
+
+def last_kernel(group, skip, passed, _, cross, own):
+    _, z, x = place_in_mode()
+
+    @pl.when(inside(z))
+    def _():
+        cut(group, cross, skip, 1 - x)
+        cut(group, own, skip, x)
+
+    @pl.when(jnp.logical_not(inside(z)))
+    def _():
+        cut(group, cross, passed, 1 - x)
+        cut(group, own, passed, x)
 
 
 def cutting(kernel, widths, name, *operands, after=()):
@@ -164,7 +177,7 @@
     )(*pieces, band)
 
 
-def project_kernel(middle, scaling, rows_out, *refs):
+def project_kernel(matrix, middle, scaling, rows_out, *refs):
     pieces, (band, image, centre) = refs[:4], refs[4:7]
     keep, send, own_rows, stacked, late, lhs = refs[7:]
     _, z, _ = place_in_mode()
@@ -172,18 +185,16 @@
     total, depth = own_rows.shape
     half = total // 2
     chunk = min(rows_out, pair)
+    columns = slice(matrix * depth, (matrix + 1) * depth)
     fill(lhs, late, pieces, middle)
     late_image = lax.dot_general(
-        lhs[...], band[...], NT, preferred_element_type=jnp.float32
+        lhs[...], band[columns, :], NT, preferred_element_type=jnp.float32
     ).astype(jnp.bfloat16)
+    stacked[: 2 * pair, :] = image[:, columns]
+    stacked[2 * pair : 3 * pair, :] = late_image[pair:]
+    stacked[3 * pair :, :] = late_image[:pair]
     near = z + 1 - 2 * lax.rem(z, 2)
-    third = jnp.where(inside(z), 3 - z, lax.rem(z + 2, 4))
-    last = jnp.where(inside(z), lax.rem(z + 2, 4), 3 - z)
-    third_at = jnp.where(inside(z), 3, 2)
-    stacked[: 2 * pair, :] = image[...]
-    stacked[pl.ds(aligned(third_at, pair), pair), :] = late_image[:pair]
-    stacked[pl.ds(aligned(5 - third_at, pair), pair), :] = late_image[pair:]
-    for slot, chip_row in enumerate((z, near, third, last)):
+    for slot, chip_row in enumerate((z, near, 3 - z, lax.rem(z + 2, 4))):
         source = (centre, late)[slot // 2]
         for piece in range(pair // chunk):
             first = chip_row * pair + piece * chunk
@@ -196,40 +207,38 @@
                 slot % 2, piece * chunk : (piece + 1) * chunk, :
             ]
     sub = lax.axis_index("sub")
-    for matrix in range(2):
-        part = stacked[:, matrix * depth : (matrix + 1) * depth]
-        for out, side in ((send, 1 - sub), (keep, sub)):
-            out[matrix] = (
-                lax.dot_general(
-                    part,
-                    own_rows[pl.ds(aligned(side, half), half), :],
-                    NT,
-                    preferred_element_type=jnp.float32,
-                )
-                * scaling
+    for out, side in ((send, 1 - sub), (keep, sub)):
+        out[...] = (
+            lax.dot_general(
+                stacked[...],
+                own_rows[pl.ds(aligned(side, half), half), :],
+                NT,
+                preferred_element_type=jnp.float32,
             )
-
-
-def make_projection(pieces, band, image, centre, group, scaling, rows_out):
+            * scaling
+        )
+
+
+def make_projection(matrix, pieces, band, image, centre, group, scaling, rows_out):
     width, span = pieces[0].shape
     total = 8 * width
-    part = jax.ShapeDtypeStruct((2, total, total // 2), jnp.float32)
+    part = jax.ShapeDtypeStruct((total, total // 2), jnp.float32)
     return pl.pallas_call(
         functools.partial(
-            project_kernel, slice(2 * group, 3 * group), scaling, rows_out
+            project_kernel, matrix, slice(2 * group, 3 * group), scaling, rows_out
         ),
         out_shape=(part, part),
         in_specs=[VMEM] * 7,
         out_specs=(VMEM, VMEM),
         scratch_shapes=[
             pltpu.VMEM((total, group), jnp.bfloat16),
-            pltpu.VMEM((total, image.shape[1]), jnp.bfloat16),
+            pltpu.VMEM((total, group), jnp.bfloat16),
             pltpu.VMEM(centre.shape, jnp.bfloat16),
             pltpu.VMEM((4 * width, span), jnp.bfloat16),
         ],
         compiler_params=params(),
         cost_estimate=pl.CostEstimate(
-            flops=4 * total * total * group, bytes_accessed=2**22, transcendentals=0
+            flops=2 * total * total * group, bytes_accessed=2**21, transcendentals=0
         ),
         name="project",
     )(*pieces, band, image, centre)
@@ -259,53 +268,60 @@
     phi = modes.T
     forward, backward = ring(unit_count)
     rim = HB * block_size
-    low = lax.ppermute(phi[:, phi.shape[1] - rim :], ("dof", "sub"), forward)
-    high = lax.ppermute(phi[:, :rim], ("dof", "sub"), backward)
+    low_w, high_w = cutting(rim_kernel, (rim, rim), "rims", phi)
+    low = lax.ppermute(low_w, ("dof", "sub"), forward)
+    high = lax.ppermute(high_w, ("dof", "sub"), backward)
 
     w5, w6, w8 = 5 * group, 6 * group, 8 * group
-    ext, inner_w, near_w, cross0_w, own0 = cutting(
+    ext, inner_w, far_w, near_w, cross0_w, own0 = cutting(
         functools.partial(first_kernel, group),
-        (phi.shape[1] + 2 * rim, w8, w6, w5, w5),
+        (phi.shape[1] + 2 * rim, w8, w6, w6, w5, w5),
         "first",
         phi,
         low,
         high,
     )
     inner = over_z(inner_w, [(1, 2), (2, 1)])
+    far = over_z(far_w, [(0, 3), (3, 0)])
     near = over_z(near_w, [(0, 1), (1, 0), (2, 3), (3, 2)])
     cross0 = over_x(cross0_w)
     band = make_band(pattern, gyroscopic, centrifugal, own0, w5, per_unit, block_total)
 
-    passed_w, crossA_w, ownA, skip_w, far_w = cutting(
-        functools.partial(second_kernel, group),
-        (w6, w5, w5, w6, w6),
-        "second",
+    crossA_w, ownA = cutting(functools.partial(near_kernel, group), (w5, w5), "near", near)
+    crossA = over_x(crossA_w)
+    passed_w, skip_w, crossB_w, ownB = cutting(
+        functools.partial(middle_kernel, group),
+        (w6, w6, w5, w5),
+        "middle",
         ext,
         inner,
-        near,
+        far,
         after=(band,),
     )
     passed = over_z(passed_w, [(2, 3), (1, 0)])
     skip = over_z(skip_w, [(0, 2), (3, 1)])
-    far = over_z(far_w, [(0, 3), (3, 0)])
-    crossA = over_x(crossA_w)
+    crossB = over_x(crossB_w)
     image, centre = make_image((own0, cross0, ownA, crossA), band, group)
-
-    crossB_w, ownB = cutting(
-        functools.partial(choose_kernel, group, 2), (w5, w5), "third", inner, passed
-    )
-    crossB = over_x(crossB_w)
     crossC_w, ownC = cutting(
-        functools.partial(choose_kernel, group, 0), (w5, w5), "fourth", skip, far, after=(image,)
+        functools.partial(last_kernel, group), (w5, w5), "last", skip, passed, after=(image,)
     )
     crossC = over_x(crossC_w)
 
     scaling = 1.0 / math.sqrt(block_total * block_size)
-    keep, send = make_projection(
-        (ownB, crossB, ownC, crossC), band, image, centre, group, scaling, total // unit_count
-    )
-    got = lax.ppermute(send, "sub", [(0, 1), (1, 0)])
-    chip = keep + got
+    sums = []
+    for matrix in range(2):
+        keep, send = make_projection(
+            matrix,
+            (ownB, crossB, ownC, crossC),
+            band,
+            image,
+            centre,
+            group,
+            scaling,
+            total // unit_count,
+        )
+        sums.append(keep + lax.ppermute(send, "sub", [(0, 1), (1, 0)]))
+    chip = jnp.stack(sums)
     result = chip[:, :width]
     for j in range(mode_count - 1, 0, -1):
         message = chip[:, j * width : (j + 1) * width].astype(jnp.bfloat16)

time: 77.8 us -> 75.4 us (0.969)
  waiting for transfers between devices: 33 us -> 28.3 us
  starting transfers between devices: 31.5 us -> 34.4 us
  local copies, waits for them, and re-layouts: 5.92 us -> 4.94 us
    ppermute x7, waiting for transfers between devices: 7.28 us -> 4.79 us  [body(): lax.ppermute(message, 'mode', [(i, i ^ j) for i in range(mode_count)])]
    ppermute x4, starting transfers between devices: 4.25 us -> 6.23 us  [over_x(): return lax.ppermute(array, 'mode', [(i, i ^ 1) for i in range(mode_count)])]
    ppermute x7, starting transfers between devices: 9.6 us -> 11.2 us  [body(): lax.ppermute(message, 'mode', [(i, i ^ j) for i in range(mode_count)])]
    ppermute x5, starting transfers between devices: 17 us -> 15.8 us  [over_z(): lax.ppermute(array, 'mode', [(s * X + i, t * X + i) for s, t in pairs for...]
    ppermute x3 -> x4, waiting for transfers between devices: 3.92 us -> 2.73 us  [the longest x2 1.47 us: body(): sums.append(keep + lax.ppermute(send, 'sub', [(0, 1), (1, 0)]))]
    slice x1 -> x0, local copies, waits for them, and re-layouts: 0.99 us -> none  [body(): high = lax.ppermute(phi[:, :rim], ('dof', 'sub'), backward)]
    ppermute x4, waiting for transfers between devices: 7.4 us -> 6.44 us  [over_x(): return lax.ppermute(array, 'mode', [(i, i ^ 1) for i in range(mode_count)])]
    pallas_call x1 -> x2, Pallas kernels: 2.1 us -> 2.33 us  [make_projection(): pl.pallas_call(functools.partial(project_kernel, matrix, slice(2 * group,...]
  transfers between devices with their start and end apart: 19 -> 20, of which waited for: 11 -> 13; matrix products, arithmetic and copies ran while one was open for 0% -> 0% of each run, Pallas kernels for 5% -> 7%
where the time goes in v3:
time: 75.4 us; the launch traced here: 75 us
  starting transfers between devices  34.4 us (46%)
  waiting for transfers between devices  28.3 us (38%)
  Pallas kernels  6.3 us (8%)
  local copies, waits for them, and re-layouts  4.94 us (7%)
  other arithmetic  0.93 us (1%)
    ppermute x5, starting transfers between devices, over_z(): lax.ppermute(array, 'mode', [(s * X + i, t * X + i) for s, t in pairs for...  15.8 us
    ppermute x5, waiting for transfers between devices, over_z(): lax.ppermute(array, 'mode', [(s * X + i, t * X + i) for s, t in pairs for...  14.3 us
    ppermute x7, starting transfers between devices, body(): lax.ppermute(message, 'mode', [(i, i ^ j) for i in range(mode_count)])  11.2 us
    ppermute x4, waiting for transfers between devices, over_x(): return lax.ppermute(array, 'mode', [(i, i ^ 1) for i in range(mode_count)])  6.44 us
    ppermute x4, starting transfers between devices, over_x(): return lax.ppermute(array, 'mode', [(i, i ^ 1) for i in range(mode_count)])  6.23 us
    unnamed x8, local copies, waits for them, and re-layouts  4.9 us
    ppermute x7, waiting for transfers between devices, body(): lax.ppermute(message, 'mode', [(i, i ^ j) for i in range(mode_count)])  4.79 us
    pallas_call x2, Pallas kernels, make_projection(): pl.pallas_call(functools.partial(project_kernel, matrix, slice(2 * group,...  2.33 us
  transfers between devices with their start and end apart: 20, of which 13 were waited for; matrix products, arithmetic and copies ran while one was open for 0% of the time, Pallas kernels for 7%

profile of v3, /device:TPU:0, one launch (start us, length us, event | category | flops | bytes accessed | tf_op | source)
XLA Modules:
  0.0 75.0 jit_solution(18362050598014920299)
XLA Ops:
  3.8 5.6 %collective-permute-start.8 = (bf16[64,3072]{1,0:T(8,128)(2,1)S(1)}, bf16[64,3072]{1,0:T(8,128)(2,1)S(1)}, u32[]{:S(2)}, u32[]{:S(2)}) collective-permute-start(bf16[64,3072]{1,0:T(8,128)(2,1)S(1)} %get-tuple-element.38), channel_id=1, source_target_pairs={{0,4},{2,6},{4,0},{6,2},{8,12},{10,14},{12,8},{14,10},{1,5},{3,7},... | collective-permute-start | bytes 1179656 | tf_op jit(solution)/shard_map/ppermute | solution.py:261
  9.4 3.2 %collective-permute-start.3 = (bf16[64,3072]{1,0:T(8,128)(2,1)S(1)}, bf16[64,3072]{1,0:T(8,128)(2,1)S(1)}, u32[]{:S(2)}, u32[]{:S(2)}) collective-permute-start(bf16[64,3072]{1,0:T(8,128)(2,1)S(1)} %get-tuple-element.31), channel_id=1, source_target_pairs={{0,12},{2,14},{12,0},{14,2},{1,13},{3,15},{13,1},{15,3},{16,28},{1... | collective-permute-start | bytes 1179656 | tf_op jit(solution)/shard_map/ppermute | solution.py:261
  12.7 1.6 %collective-permute-start.7 = (bf16[64,2560]{1,0:T(8,128)(2,1)S(1)}, bf16[64,2560]{1,0:T(8,128)(2,1)S(1)}, u32[]{:S(2)}, u32[]{:S(2)}) collective-permute-start(bf16[64,2560]{1,0:T(8,128)(2,1)S(1)} %get-tuple-element.37), channel_id=1, source_target_pairs={{0,2},{2,0},{4,6},{6,4},{8,10},{10,8},{12,14},{14,12},{1,3},{3,1},... | collective-permute-start | bytes 983048 | tf_op jit(solution)/shard_map/ppermute | solution.py:266
  14.2 4.7 %collective-permute-done.8.near = bf16[64,3072]{1,0:T(8,128)(2,1)S(1)} collective-permute-done((bf16[64,3072]{1,0:T(8,128)(2,1)S(1)}, bf16[64,3072]{1,0:T(8,128)(2,1)S(1)}, u32[]{:S(2)}, u32[]{:S(2)}) %collective-permute-start.8) | collective-permute-done | bytes 393248 | tf_op jit(solution)/shard_map/ppermute | solution.py:261
  19.0 1.6 %collective-permute-start.9 = (bf16[64,2560]{1,0:T(8,128)(2,1)S(1)}, bf16[64,2560]{1,0:T(8,128)(2,1)S(1)}, u32[]{:S(2)}, u32[]{:S(2)}) collective-permute-start(bf16[64,2560]{1,0:T(8,128)(2,1)S(1)} %get-tuple-element.40), channel_id=1, source_target_pairs={{0,2},{2,0},{4,6},{6,4},{8,10},{10,8},{12,14},{14,12},{1,3},{3,1},... | collective-permute-start | bytes 983048 | tf_op jit(solution)/shard_map/ppermute | solution.py:266
  20.5 1.6 %copy-done.1 = bf16[1,4,16,128,128]{4,3,2,1,0:T(8,128)(2,1)S(1)} copy-done((bf16[1,4,16,128,128]{4,3,2,1,0:T(8,128)(2,1)S(1)}, bf16[1,4,16,128,128]{4,3,2,1,0:T(8,128)(2,1)}, u32[]{:S(2)}) %copy-start.1) | copy-done | bytes 2097176
  22.1 1.6 %copy-done.2 = bf16[1,4,16,128,128]{4,3,2,1,0:T(8,128)(2,1)S(1)} copy-done((bf16[1,4,16,128,128]{4,3,2,1,0:T(8,128)(2,1)S(1)}, bf16[1,4,16,128,128]{4,3,2,1,0:T(8,128)(2,1)}, u32[]{:S(2)}) %copy-start.2) | copy-done | bytes 2097176
  24.4 2.0 %band.1 = bf16[2,4,128,2560]{3,2,1,0:T(8,128)(2,1)S(1)} custom-call(s32[1,4,16]{2,1,0:T(4,128)S(1)} %copy-done.3, bf16[1,4,16,128,128]{4,3,2,1,0:T(8,128)(2,1)S(1)} %copy-done.1, bf16[1,4,16,128,128]{4,3,2,1,0:T(8,128)(2,1)S(1)} %copy-done.2, bf16[64,2560]{1,0:T(8,128)(2,1)S(1)} %get-tuple-element.32._.refs_0_), custom_call_target="tpu_custom_call" | custom-call | bytes 8388608 | tf_op jit(solution)/shard_map/band/pallas_call | solution.py:57
  26.4 1.9 %collective-permute-done.3.far = bf16[64,3072]{1,0:T(8,128)(2,1)S(1)} collective-permute-done((bf16[64,3072]{1,0:T(8,128)(2,1)S(1)}, bf16[64,3072]{1,0:T(8,128)(2,1)S(1)}, u32[]{:S(2)}, u32[]{:S(2)}) %collective-permute-start.3) | collective-permute-done | bytes 393248 | tf_op jit(solution)/shard_map/ppermute | solution.py:261
  28.5 4.9 %collective-permute-start.5 = (bf16[64,3072]{1,0:T(8,128)(2,1)S(1)}, bf16[64,3072]{1,0:T(8,128)(2,1)S(1)}, u32[]{:S(2)}, u32[]{:S(2)}) collective-permute-start(bf16[64,3072]{1,0:T(8,128)(2,1)S(1)} %get-tuple-element.35), channel_id=1, source_target_pairs={{0,8},{2,10},{12,4},{14,6},{1,9},{3,11},{13,5},{15,7},{16,24},{18,... | collective-permute-start | bytes 1179656 | tf_op jit(solution)/shard_map/ppermute | solution.py:261
  33.4 1.3 %collective-permute-start.6 = (bf16[64,3072]{1,0:T(8,128)(2,1)S(1)}, bf16[64,3072]{1,0:T(8,128)(2,1)S(1)}, u32[]{:S(2)}, u32[]{:S(2)}) collective-permute-start(bf16[64,3072]{1,0:T(8,128)(2,1)S(1)} %get-tuple-element.36), channel_id=1, source_target_pairs={{8,12},{10,14},{4,0},{6,2},{9,13},{11,15},{5,1},{7,3},{24,28},{26,... | collective-permute-start | bytes 1179656 | tf_op jit(solution)/shard_map/ppermute | solution.py:261
  34.7 1.6 %collective-permute-start.4 = (bf16[64,2560]{1,0:T(8,128)(2,1)S(1)}, bf16[64,2560]{1,0:T(8,128)(2,1)S(1)}, u32[]{:S(2)}, u32[]{:S(2)}) collective-permute-start(bf16[64,2560]{1,0:T(8,128)(2,1)S(1)} %get-tuple-element.34), channel_id=1, source_target_pairs={{0,2},{2,0},{4,6},{6,4},{8,10},{10,8},{12,14},{14,12},{1,3},{3,1},... | collective-permute-start | bytes 983048 | tf_op jit(solution)/shard_map/ppermute | solution.py:266
  36.3 1.6 %image.1 = (bf16[256,1024]{1,0:T(8,128)(2,1)S(1)}, bf16[2,128,512]{2,1,0:T(8,128)(2,1)S(1)}) custom-call(bf16[64,2560]{1,0:T(8,128)(2,1)S(1)} %get-tuple-element.32._.refs_0_, bf16[64,2560]{1,0:T(8,128)(2,1)S(1)} %collective-permute-done.7.refs_1_, bf16[64,2560]{1,0:T(8,128)(2,1)S(1)} %get-tuple-element.39.refs_2_, ...), custom_call_target="tpu_custom_call" | custom-call | flops 1342177280 | bytes 4194304 | tf_op jit(solution)/shard_map/image/pallas_call | solution.py:163
  37.8 3.6 %collective-permute-done.5.skip = bf16[64,3072]{1,0:T(8,128)(2,1)S(1)} collective-permute-done((bf16[64,3072]{1,0:T(8,128)(2,1)S(1)}, bf16[64,3072]{1,0:T(8,128)(2,1)S(1)}, u32[]{:S(2)}, u32[]{:S(2)}) %collective-permute-start.5) | collective-permute-done | bytes 393248 | tf_op jit(solution)/shard_map/ppermute | solution.py:261
  41.4 4.1 %collective-permute-done.6.passed = bf16[64,3072]{1,0:T(8,128)(2,1)S(1)} collective-permute-done((bf16[64,3072]{1,0:T(8,128)(2,1)S(1)}, bf16[64,3072]{1,0:T(8,128)(2,1)S(1)}, u32[]{:S(2)}, u32[]{:S(2)}) %collective-permute-start.6) | collective-permute-done | bytes 393248 | tf_op jit(solution)/shard_map/ppermute | solution.py:261
  45.6 1.6 %collective-permute-start.10 = (bf16[64,2560]{1,0:T(8,128)(2,1)S(1)}, bf16[64,2560]{1,0:T(8,128)(2,1)S(1)}, u32[]{:S(2)}, u32[]{:S(2)}) collective-permute-start(bf16[64,2560]{1,0:T(8,128)(2,1)S(1)} %get-tuple-element.43), channel_id=1, source_target_pairs={{0,2},{2,0},{4,6},{6,4},{8,10},{10,8},{12,14},{14,12},{1,3},{3,1},... | collective-permute-start | bytes 983048 | tf_op jit(solution)/shard_map/ppermute | solution.py:266
  47.2 6.4 %collective-permute-done.10.refs_3_ = bf16[64,2560]{1,0:T(8,128)(2,1)S(1)} collective-permute-done((bf16[64,2560]{1,0:T(8,128)(2,1)S(1)}, bf16[64,2560]{1,0:T(8,128)(2,1)S(1)}, u32[]{:S(2)}, u32[]{:S(2)}) %collective-permute-start.10) | collective-permute-done | bytes 327712 | tf_op jit(solution)/shard_map/ppermute | solution.py:266
  56.8 1.3 %collective-permute-done.12 = f32[512,256]{1,0:T(8,128)S(1)} collective-permute-done((f32[512,256]{1,0:T(8,128)S(1)}, f32[512,256]{1,0:T(8,128)S(1)}, u32[]{:S(2)}, u32[]{:S(2)}) %collective-permute-start.12) | collective-permute-done | bytes 524320 | tf_op jit(solution)/shard_map/ppermute | solution.py:323
  58.3 2.4 %collective-permute-start.13 = (bf16[2,64,256]{2,1,0:T(8,128)(2,1)S(1)}, bf16[2,64,256]{2,1,0:T(8,128)(2,1)S(1)}, u32[]{:S(2)}, u32[]{:S(2)}) collective-permute-start(bf16[2,64,256]{2,1,0:T(8,128)(2,1)S(1)} %get-tuple-element.49), channel_id=1, source_target_pairs={{0,14},{2,12},{4,10},{6,8},{8,6},{10,4},{12,2},{14,0},{1,15},{3,13... | collective-permute-start | bytes 196616 | tf_op jit(solution)/shard_map/ppermute | solution.py:328
  60.7 2.5 %collective-permute-start.14 = (bf16[2,64,256]{2,1,0:T(8,128)(2,1)S(1)}, bf16[2,64,256]{2,1,0:T(8,128)(2,1)S(1)}, u32[]{:S(2)}, u32[]{:S(2)}) collective-permute-start(bf16[2,64,256]{2,1,0:T(8,128)(2,1)S(1)} %get-tuple-element.55), channel_id=1, source_target_pairs={{0,12},{2,14},{4,8},{6,10},{8,4},{10,6},{12,0},{14,2},{1,13},{3,15... | collective-permute-start | bytes 196616 | tf_op jit(solution)/shard_map/ppermute | solution.py:328
  63.1 2.9 %collective-permute-start.16 = (bf16[2,64,256]{2,1,0:T(8,128)(2,1)S(1)}, bf16[2,64,256]{2,1,0:T(8,128)(2,1)S(1)}, u32[]{:S(2)}, u32[]{:S(2)}) collective-permute-start(bf16[2,64,256]{2,1,0:T(8,128)(2,1)S(1)} %get-tuple-element.53), channel_id=1, source_target_pairs={{0,8},{2,10},{4,12},{6,14},{8,0},{10,2},{12,4},{14,6},{1,9},{3,11}... | collective-permute-start | bytes 196616 | tf_op jit(solution)/shard_map/ppermute | solution.py:328
  66.0 3.0 %collective-permute-start.18 = (bf16[2,64,256]{2,1,0:T(8,128)(2,1)S(1)}, bf16[2,64,256]{2,1,0:T(8,128)(2,1)S(1)}, u32[]{:S(2)}, u32[]{:S(2)}) collective-permute-start(bf16[2,64,256]{2,1,0:T(8,128)(2,1)S(1)} %get-tuple-element.51), channel_id=1, source_target_pairs={{0,4},{2,6},{4,0},{6,2},{8,12},{10,14},{12,8},{14,10},{1,5},{3,7},... | collective-permute-start | bytes 196616 | tf_op jit(solution)/shard_map/ppermute | solution.py:328
  69.5 1.6 %collective-permute-done.15 = bf16[2,64,256]{2,1,0:T(8,128)(2,1)S(1)} collective-permute-done((bf16[2,64,256]{2,1,0:T(8,128)(2,1)S(1)}, bf16[2,64,256]{2,1,0:T(8,128)(2,1)S(1)}, u32[]{:S(2)}, u32[]{:S(2)}) %collective-permute-start.15) | collective-permute-done | bytes 65568 | tf_op jit(solution)/shard_map/ppermute | solution.py:328
  71.1 1.4 %collective-permute-done.16 = bf16[2,64,256]{2,1,0:T(8,128)(2,1)S(1)} collective-permute-done((bf16[2,64,256]{2,1,0:T(8,128)(2,1)S(1)}, bf16[2,64,256]{2,1,0:T(8,128)(2,1)S(1)}, u32[]{:S(2)}, u32[]{:S(2)}) %collective-permute-start.16) | collective-permute-done | bytes 65568 | tf_op jit(solution)/shard_map/ppermute | solution.py:328
  (38 shorter events, 11.0 us)
Async XLA Ops:
  0.0 1.0 %copy-start = (bf16[4096,64]{0,1:T(8,128)(2,1)S(1)}, bf16[4096,64]{0,1:T(8,128)(2,1)}, u32[]{:S(2)}) copy-start(bf16[4096,64]{0,1:T(8,128)(2,1)} %param.4) | copy-start | bytes 1572868
  1.1 1.5 %collective-permute-start = (bf16[64,1024]{1,0:T(8,128)(2,1)S(1)}, bf16[64,1024]{1,0:T(8,128)(2,1)S(1)}, u32[]{:S(2)}, u32[]{:S(2)}) collective-permute-start(bf16[64,1024]{1,0:T(8,128)(2,1)S(1)} %get-tuple-element.27), channel_id=1, source_target_pairs={{0,1},{1,0},{2,3},{3,2},{4,5},{5,4},{6,7},{7,6},{8,9},{9,8},{10,11... | collective-permute-start | bytes 393224 | tf_op jit(solution)/shard_map/ppermute | solution.py:272
  1.6 1.3 %collective-permute-start.1 = (bf16[64,1024]{1,0:T(8,128)(2,1)S(1)}, bf16[64,1024]{1,0:T(8,128)(2,1)S(1)}, u32[]{:S(2)}, u32[]{:S(2)}) collective-permute-start(bf16[64,1024]{1,0:T(8,128)(2,1)S(1)} %get-tuple-element.28), channel_id=1, source_target_pairs={{1,0},{0,1},{3,2},{2,3},{5,4},{4,5},{7,6},{6,7},{9,8},{8,9},{11,10... | collective-permute-start | bytes 393224 | tf_op jit(solution)/shard_map/ppermute | solution.py:273
  3.1 25.2 %collective-permute-start.2 = (bf16[64,4096]{1,0:T(8,128)(2,1)S(1)}, bf16[64,4096]{1,0:T(8,128)(2,1)S(1)}, u32[]{:S(2)}, u32[]{:S(2)}) collective-permute-start(bf16[64,4096]{1,0:T(8,128)(2,1)S(1)} %get-tuple-element.30), channel_id=1, source_target_pairs={{4,8},{6,10},{8,4},{10,6},{5,9},{7,11},{9,5},{11,7},{20,24},{22,26... | collective-permute-start | bytes 1572872 | tf_op jit(solution)/shard_map/ppermute | solution.py:261
  3.8 15.1 %collective-permute-start.8 = (bf16[64,3072]{1,0:T(8,128)(2,1)S(1)}, bf16[64,3072]{1,0:T(8,128)(2,1)S(1)}, u32[]{:S(2)}, u32[]{:S(2)}) collective-permute-start(bf16[64,3072]{1,0:T(8,128)(2,1)S(1)} %get-tuple-element.38), channel_id=1, source_target_pairs={{0,4},{2,6},{4,0},{6,2},{8,12},{10,14},{12,8},{14,10},{1,5},{3,7},... | collective-permute-start | bytes 1179656 | tf_op jit(solution)/shard_map/ppermute | solution.py:261
  9.4 18.9 %collective-permute-start.3 = (bf16[64,3072]{1,0:T(8,128)(2,1)S(1)}, bf16[64,3072]{1,0:T(8,128)(2,1)S(1)}, u32[]{:S(2)}, u32[]{:S(2)}) collective-permute-start(bf16[64,3072]{1,0:T(8,128)(2,1)S(1)} %get-tuple-element.31), channel_id=1, source_target_pairs={{0,12},{2,14},{12,0},{14,2},{1,13},{3,15},{13,1},{15,3},{16,28},{1... | collective-permute-start | bytes 1179656 | tf_op jit(solution)/shard_map/ppermute | solution.py:261
  12.7 23.6 %collective-permute-start.7 = (bf16[64,2560]{1,0:T(8,128)(2,1)S(1)}, bf16[64,2560]{1,0:T(8,128)(2,1)S(1)}, u32[]{:S(2)}, u32[]{:S(2)}) collective-permute-start(bf16[64,2560]{1,0:T(8,128)(2,1)S(1)} %get-tuple-element.37), channel_id=1, source_target_pairs={{0,2},{2,0},{4,6},{6,4},{8,10},{10,8},{12,14},{14,12},{1,3},{3,1},... | collective-permute-start | bytes 983048 | tf_op jit(solution)/shard_map/ppermute | solution.py:266
  19.0 17.3 %collective-permute-start.9 = (bf16[64,2560]{1,0:T(8,128)(2,1)S(1)}, bf16[64,2560]{1,0:T(8,128)(2,1)S(1)}, u32[]{:S(2)}, u32[]{:S(2)}) collective-permute-start(bf16[64,2560]{1,0:T(8,128)(2,1)S(1)} %get-tuple-element.40), channel_id=1, source_target_pairs={{0,2},{2,0},{4,6},{6,4},{8,10},{10,8},{12,14},{14,12},{1,3},{3,1},... | collective-permute-start | bytes 983048 | tf_op jit(solution)/shard_map/ppermute | solution.py:266
  20.5 1.6 %copy-start.1 = (bf16[1,4,16,128,128]{4,3,2,1,0:T(8,128)(2,1)S(1)}, bf16[1,4,16,128,128]{4,3,2,1,0:T(8,128)(2,1)}, u32[]{:S(2)}) copy-start(bf16[1,4,16,128,128]{4,3,2,1,0:T(8,128)(2,1)} %gyro.1) | copy-start | bytes 6291460
  22.1 1.6 %copy-start.2 = (bf16[1,4,16,128,128]{4,3,2,1,0:T(8,128)(2,1)S(1)}, bf16[1,4,16,128,128]{4,3,2,1,0:T(8,128)(2,1)}, u32[]{:S(2)}) copy-start(bf16[1,4,16,128,128]{4,3,2,1,0:T(8,128)(2,1)} %spin.1) | copy-start | bytes 6291460
  23.7 0.7 copy-start.3
  28.5 13.0 %collective-permute-start.5 = (bf16[64,3072]{1,0:T(8,128)(2,1)S(1)}, bf16[64,3072]{1,0:T(8,128)(2,1)S(1)}, u32[]{:S(2)}, u32[]{:S(2)}) collective-permute-start(bf16[64,3072]{1,0:T(8,128)(2,1)S(1)} %get-tuple-element.35), channel_id=1, source_target_pairs={{0,8},{2,10},{12,4},{14,6},{1,9},{3,11},{13,5},{15,7},{16,24},{18,... | collective-permute-start | bytes 1179656 | tf_op jit(solution)/shard_map/ppermute | solution.py:261
  33.4 12.2 %collective-permute-start.6 = (bf16[64,3072]{1,0:T(8,128)(2,1)S(1)}, bf16[64,3072]{1,0:T(8,128)(2,1)S(1)}, u32[]{:S(2)}, u32[]{:S(2)}) collective-permute-start(bf16[64,3072]{1,0:T(8,128)(2,1)S(1)} %get-tuple-element.36), channel_id=1, source_target_pairs={{8,12},{10,14},{4,0},{6,2},{9,13},{11,15},{5,1},{7,3},{24,28},{26,... | collective-permute-start | bytes 1179656 | tf_op jit(solution)/shard_map/ppermute | solution.py:261
  34.7 12.5 %collective-permute-start.4 = (bf16[64,2560]{1,0:T(8,128)(2,1)S(1)}, bf16[64,2560]{1,0:T(8,128)(2,1)S(1)}, u32[]{:S(2)}, u32[]{:S(2)}) collective-permute-start(bf16[64,2560]{1,0:T(8,128)(2,1)S(1)} %get-tuple-element.34), channel_id=1, source_target_pairs={{0,2},{2,0},{4,6},{6,4},{8,10},{10,8},{12,14},{14,12},{1,3},{3,1},... | collective-permute-start | bytes 983048 | tf_op jit(solution)/shard_map/ppermute | solution.py:266
  45.6 8.0 %collective-permute-start.10 = (bf16[64,2560]{1,0:T(8,128)(2,1)S(1)}, bf16[64,2560]{1,0:T(8,128)(2,1)S(1)}, u32[]{:S(2)}, u32[]{:S(2)}) collective-permute-start(bf16[64,2560]{1,0:T(8,128)(2,1)S(1)} %get-tuple-element.43), channel_id=1, source_target_pairs={{0,2},{2,0},{4,6},{6,4},{8,10},{10,8},{12,14},{14,12},{1,3},{3,1},... | collective-permute-start | bytes 983048 | tf_op jit(solution)/shard_map/ppermute | solution.py:266
  54.8 2.0 %collective-permute-start.11 = (f32[512,256]{1,0:T(8,128)S(1)}, f32[512,256]{1,0:T(8,128)S(1)}, u32[]{:S(2)}, u32[]{:S(2)}) collective-permute-start(f32[512,256]{1,0:T(8,128)S(1)} %get-tuple-element.46), channel_id=1, source_target_pairs={{0,1},{1,0},{2,3},{3,2},{4,5},{5,4},{6,7},{7,6},{8,9},{9,8},{10,11... | collective-permute-start | bytes 1572872 | tf_op jit(solution)/shard_map/ppermute | solution.py:323
  56.0 2.1 %collective-permute-start.12 = (f32[512,256]{1,0:T(8,128)S(1)}, f32[512,256]{1,0:T(8,128)S(1)}, u32[]{:S(2)}, u32[]{:S(2)}) collective-permute-start(f32[512,256]{1,0:T(8,128)S(1)} %get-tuple-element.48), channel_id=1, source_target_pairs={{0,1},{1,0},{2,3},{3,2},{4,5},{5,4},{6,7},{7,6},{8,9},{9,8},{10,11... | collective-permute-start | bytes 1572872 | tf_op jit(solution)/shard_map/ppermute | solution.py:323
  58.3 7.7 %collective-permute-start.13 = (bf16[2,64,256]{2,1,0:T(8,128)(2,1)S(1)}, bf16[2,64,256]{2,1,0:T(8,128)(2,1)S(1)}, u32[]{:S(2)}, u32[]{:S(2)}) collective-permute-start(bf16[2,64,256]{2,1,0:T(8,128)(2,1)S(1)} %get-tuple-element.49), channel_id=1, source_target_pairs={{0,14},{2,12},{4,10},{6,8},{8,6},{10,4},{12,2},{14,0},{1,15},{3,13... | collective-permute-start | bytes 196616 | tf_op jit(solution)/shard_map/ppermute | solution.py:328
  60.7 8.3 %collective-permute-start.14 = (bf16[2,64,256]{2,1,0:T(8,128)(2,1)S(1)}, bf16[2,64,256]{2,1,0:T(8,128)(2,1)S(1)}, u32[]{:S(2)}, u32[]{:S(2)}) collective-permute-start(bf16[2,64,256]{2,1,0:T(8,128)(2,1)S(1)} %get-tuple-element.55), channel_id=1, source_target_pairs={{0,12},{2,14},{4,8},{6,10},{8,4},{10,6},{12,0},{14,2},{1,13},{3,15... | collective-permute-start | bytes 196616 | tf_op jit(solution)/shard_map/ppermute | solution.py:328
  63.1 8.0 %collective-permute-start.15 = (bf16[2,64,256]{2,1,0:T(8,128)(2,1)S(1)}, bf16[2,64,256]{2,1,0:T(8,128)(2,1)S(1)}, u32[]{:S(2)}, u32[]{:S(2)}) collective-permute-start(bf16[2,64,256]{2,1,0:T(8,128)(2,1)S(1)} %get-tuple-element.54), channel_id=1, source_target_pairs={{0,10},{2,8},{4,14},{6,12},{8,2},{10,0},{12,6},{14,4},{1,11},{3,9}... | collective-permute-start | bytes 196616 | tf_op jit(solution)/shard_map/ppermute | solution.py:328
  63.1 9.5 %collective-permute-start.16 = (bf16[2,64,256]{2,1,0:T(8,128)(2,1)S(1)}, bf16[2,64,256]{2,1,0:T(8,128)(2,1)S(1)}, u32[]{:S(2)}, u32[]{:S(2)}) collective-permute-start(bf16[2,64,256]{2,1,0:T(8,128)(2,1)S(1)} %get-tuple-element.53), channel_id=1, source_target_pairs={{0,8},{2,10},{4,12},{6,14},{8,0},{10,2},{12,4},{14,6},{1,9},{3,11}... | collective-permute-start | bytes 196616 | tf_op jit(solution)/shard_map/ppermute | solution.py:328
  66.0 7.6 %collective-permute-start.17 = (bf16[2,64,256]{2,1,0:T(8,128)(2,1)S(1)}, bf16[2,64,256]{2,1,0:T(8,128)(2,1)S(1)}, u32[]{:S(2)}, u32[]{:S(2)}) collective-permute-start(bf16[2,64,256]{2,1,0:T(8,128)(2,1)S(1)} %get-tuple-element.52), channel_id=1, source_target_pairs={{0,6},{2,4},{4,2},{6,0},{8,14},{10,12},{12,10},{14,8},{1,7},{3,5},... | collective-permute-start | bytes 196616 | tf_op jit(solution)/shard_map/ppermute | solution.py:328
  66.0 8.3 %collective-permute-start.18 = (bf16[2,64,256]{2,1,0:T(8,128)(2,1)S(1)}, bf16[2,64,256]{2,1,0:T(8,128)(2,1)S(1)}, u32[]{:S(2)}, u32[]{:S(2)}) collective-permute-start(bf16[2,64,256]{2,1,0:T(8,128)(2,1)S(1)} %get-tuple-element.51), channel_id=1, source_target_pairs={{0,4},{2,6},{4,0},{6,2},{8,12},{10,14},{12,8},{14,10},{1,5},{3,7},... | collective-permute-start | bytes 196616 | tf_op jit(solution)/shard_map/ppermute | solution.py:328
  69.0 5.3 %collective-permute-start.19 = (bf16[2,64,256]{2,1,0:T(8,128)(2,1)S(1)}, bf16[2,64,256]{2,1,0:T(8,128)(2,1)S(1)}, u32[]{:S(2)}, u32[]{:S(2)}) collective-permute-start(bf16[2,64,256]{2,1,0:T(8,128)(2,1)S(1)} %get-tuple-element.50), channel_id=1, source_target_pairs={{0,2},{2,0},{4,6},{6,4},{8,10},{10,8},{12,14},{14,12},{1,3},{3,1},... | collective-permute-start | bytes 196616 | tf_op jit(solution)/shard_map/ppermute | solution.py:328

commit v4 on v3

v4 whole, which is shorter than its diff:
```python
import functools
import math

import jax
import jax.numpy as jnp
from jax import lax
from jax.experimental import pallas as pl
from jax.experimental.pallas import tpu as pltpu
from jax.sharding import PartitionSpec as P

HB = 8
X = 2
EARLY = 48
VMEM_LIMIT = 24 * 1024 * 1024
NT = (((1,), (1,)), ((), ()))
VMEM = pl.BlockSpec(memory_space=pltpu.VMEM)
ANY = pl.BlockSpec(memory_space=pl.ANY)


def params():
    return pltpu.CompilerParams(vmem_limit_bytes=VMEM_LIMIT)


def ring(count):
    forward = [(i, (i + 1) % count) for i in range(count)]
    return forward, [(target, source) for source, target in forward]


def place_in_mode():
    m = lax.axis_index("mode")
    return m, lax.div(m, X), lax.rem(m, X)


def ahead(z):
    return lax.rem(3 * (z + 1), 5) - 1


def behind(z):
    return lax.rem(2 * (z + 1), 5) - 1


def aligned(index, size):
    return pl.multiple_of(index * size, size)


def band_kernel(per_unit, block_total, pattern, gyro, spin, _, band):
    row = pl.program_id(0)
    slots, size = gyro.shape[2:4]
    unit = lax.axis_index(("dof", "sub"))
    base = unit * per_unit + lax.axis_index("mode") * pl.num_programs(0) - HB
    band[...] = jnp.zeros_like(band)
    for slot in range(slots):
        column = lax.rem(pattern[0, row, slot] - base + block_total, block_total)
        where = pl.ds(aligned(column, size), size)
        band[0, 0, :, where] = gyro[0, 0, slot]
        band[1, 0, :, where] = spin[0, 0, slot]


def make_band(pattern, gyroscopic, centrifugal, after, width, per_unit, block_total):
    _, rows, slots, size, _ = gyroscopic.shape
    block = pl.BlockSpec((1, 1, slots, size, size), lambda j: (0, j, 0, 0, 0))
    band = pl.pallas_call(
        functools.partial(band_kernel, per_unit, block_total),
        out_shape=jax.ShapeDtypeStruct((2, rows, size, width), jnp.bfloat16),
        grid=(rows,),
        in_specs=[pl.BlockSpec(memory_space=pltpu.SMEM), block, block, ANY],
        out_specs=pl.BlockSpec((2, 1, size, width), lambda j: (0, j, 0, 0)),
        compiler_params=params(),
        cost_estimate=pl.CostEstimate(flops=0, bytes_accessed=2**23, transcendentals=0),
        name="band",
    )(pattern, gyroscopic, centrifugal, after)
    return band.reshape(2 * rows * size, width)


def rim_kernel(phi, low, high):
    low[...] = phi[:, phi.shape[1] - low.shape[1] :]
    high[...] = phi[:, : high.shape[1]]


def cut(group, out, source, start):
    out[...] = source[:, pl.ds(aligned(start, group), out.shape[1])]


def first_kernel(group, phi, low, high, ext, to_ahead, to_behind, cross, own):
    m, z, _ = place_in_mode()
    rim = low.shape[1]
    ext[:, :rim] = low[...]
    ext[:, rim : rim + phi.shape[1]] = phi[...]
    ext[:, rim + phi.shape[1] :] = high[...]
    cut(group, to_ahead, ext, 2 * ahead(z))
    cut(group, to_behind, ext, 2 * behind(z))
    cut(group, cross, ext, m + 1 - 2 * lax.rem(m, 2))
    cut(group, own, ext, m)


def parted_kernel(group, got, *refs):
    cross, own = refs[-2:]
    _, _, x = place_in_mode()
    cut(group, cross, got, 1 - x)
    cut(group, own, got, x)


def onward_kernel(group, rows, got, ext, *refs):
    cross, own, out = refs[-3:]
    _, z, x = place_in_mode()
    cut(group, cross, got, 1 - x)
    cut(group, own, got, x)
    out[...] = ext[rows, pl.ds(aligned(2 * (3 - z), group), out.shape[1])]


def cutting(kernel, shapes, name, *operands, after=()):
    return pl.pallas_call(
        kernel,
        out_shape=[jax.ShapeDtypeStruct(shape, jnp.bfloat16) for shape in shapes],
        in_specs=[VMEM] * len(operands) + [ANY] * len(after),
        out_specs=[VMEM] * len(shapes),
        compiler_params=params(),
        name=name,
    )(*operands, *after)


def fill(lhs, centre, slots, middle):
    _, _, x = place_in_mode()
    width = centre.shape[1] // 2
    for slot, sides in enumerate(slots):
        for side, chunks in enumerate(sides):
            chip = aligned(lax.rem(x + side, 2), width)
            at = 0
            for chunk in chunks:
                first = (2 * slot + side) * width + at
                count = chunk.shape[0]
                lhs[first : first + count, :] = chunk[...]
                centre[slot, pl.ds(pl.multiple_of(chip + at, 16), count), :] = chunk[:, middle]
                at += count


def regroup(layout, refs):
    refs = iter(refs)
    return [[[next(refs) for _ in range(chunks)] for _ in range(2)] for chunks in layout]


def image_kernel(layout, middle, *refs):
    band, image, centre, lhs = refs[-4:]
    fill(lhs, centre, regroup(layout, refs[:-4]), middle)
    image[...] = lax.dot_general(
        lhs[...], band[...], NT, preferred_element_type=jnp.float32
    ).astype(jnp.bfloat16)


def flat(slots):
    layout = [len(sides[0]) for sides in slots]
    return layout, [chunk for sides in slots for chunks in sides for chunk in chunks]


def make_image(slots, band, group, width):
    layout, pieces = flat(slots)
    span = pieces[0].shape[1]
    return pl.pallas_call(
        functools.partial(image_kernel, layout, slice(2 * group, 3 * group)),
        out_shape=(
            jax.ShapeDtypeStruct((4 * width, band.shape[0]), jnp.bfloat16),
            jax.ShapeDtypeStruct((2, 2 * width, group), jnp.bfloat16),
        ),
        in_specs=[VMEM] * (len(pieces) + 1),
        out_specs=(VMEM, VMEM),
        scratch_shapes=[pltpu.VMEM((4 * width, span), jnp.bfloat16)],
        compiler_params=params(),
        cost_estimate=pl.CostEstimate(
            flops=8 * width * span * band.shape[0], bytes_accessed=2**22, transcendentals=0
        ),
        name="image",
    )(*pieces, band)


def project_kernel(matrix, layout, middle, scaling, rows_out, *refs):
    keep, send, own_rows, stacked, late, lhs = refs[-6:]
    band, image, centre = refs[-9:-6]
    _, z, _ = place_in_mode()
    pair = centre.shape[1]
    total, depth = own_rows.shape
    half = total // 2
    chunk = min(rows_out, pair)
    columns = slice(matrix * depth, (matrix + 1) * depth)
    fill(lhs, late, regroup(layout, refs[:-9]), middle)
    stacked[: 2 * pair, :] = image[:, columns]
    stacked[2 * pair :, :] = lax.dot_general(
        lhs[...], band[columns, :], NT, preferred_element_type=jnp.float32
    ).astype(jnp.bfloat16)
    for slot, chip_row in enumerate((z, behind(z), ahead(z), 3 - z)):
        source = (centre, late)[slot // 2]
        for piece in range(pair // chunk):
            first = chip_row * pair + piece * chunk
            target = (
                lax.rem(lax.div(first, rows_out), 2) * half
                + lax.div(first, 2 * rows_out) * rows_out
                + lax.rem(first, rows_out)
            )
            own_rows[pl.ds(pl.multiple_of(target, chunk), chunk), :] = source[
                slot % 2, piece * chunk : (piece + 1) * chunk, :
            ]
    sub = lax.axis_index("sub")
    for out, side in ((send, 1 - sub), (keep, sub)):
        out[...] = (
            lax.dot_general(
                stacked[...],
                own_rows[pl.ds(aligned(side, half), half), :],
                NT,
                preferred_element_type=jnp.float32,
            )
            * scaling
        )


def make_projection(matrix, slots, band, image, centre, group, scaling, rows_out):
    layout, pieces = flat(slots)
    total = 2 * image.shape[0]
    part = jax.ShapeDtypeStruct((total, total // 2), jnp.float32)
    return pl.pallas_call(
        functools.partial(
            project_kernel, matrix, layout, slice(2 * group, 3 * group), scaling, rows_out
        ),
        out_shape=(part, part),
        in_specs=[VMEM] * (len(pieces) + 3),
        out_specs=(VMEM, VMEM),
        scratch_shapes=[
            pltpu.VMEM((total, group), jnp.bfloat16),
            pltpu.VMEM((total, group), jnp.bfloat16),
            pltpu.VMEM(centre.shape, jnp.bfloat16),
            pltpu.VMEM((total // 2, pieces[0].shape[1]), jnp.bfloat16),
        ],
        compiler_params=params(),
        cost_estimate=pl.CostEstimate(
            flops=2 * total * total * group, bytes_accessed=2**21, transcendentals=0
        ),
        name="project",
    )(*pieces, band, image, centre)


def body(modes, gyroscopic, centrifugal, pattern):
    mode_count = lax.axis_size("mode")
    dof_count = lax.axis_size("dof")
    sub_count = lax.axis_size("sub")
    unit_count = dof_count * sub_count
    rows_dev = gyroscopic.shape[1]
    block_size = gyroscopic.shape[3]
    per_unit = rows_dev * mode_count
    block_total = unit_count * per_unit
    group = rows_dev * block_size
    width = modes.shape[1]
    total = width * mode_count

    def move(array, to):
        target, flip = to
        pairs = [(i, target(i // X) * X + (i % X ^ flip)) for i in range(mode_count)]
        return lax.ppermute(array, "mode", pairs)

    def to_ahead(z):
        return 3 * (z + 1) % 5 - 1

    def to_behind(z):
        return 2 * (z + 1) % 5 - 1

    def to_far(z):
        return 3 - z

    def to_same(z):
        return z

    phi = modes.T
    forward, backward = ring(unit_count)
    rim = HB * block_size
    low_w, high_w = cutting(rim_kernel, [(width, rim)] * 2, "rims", phi)
    low = lax.ppermute(low_w, ("dof", "sub"), forward)
    high = lax.ppermute(high_w, ("dof", "sub"), backward)

    w5, w6 = 5 * group, 6 * group
    ext, ahead_w, behind_w, cross0_w, own0 = cutting(
        functools.partial(first_kernel, group),
        [(width, w) for w in (phi.shape[1] + 2 * rim, w6, w6, w5, w5)],
        "first",
        phi,
        low,
        high,
    )
    gotA = move(ahead_w, (to_ahead, 0))
    gotB = move(behind_w, (to_behind, 0))
    cross0 = move(cross0_w, (to_same, 1))
    band = make_band(pattern, gyroscopic, centrifugal, own0, w5, per_unit, block_total)

    early = EARLY
    crossA_w, ownA, far1_w = cutting(
        functools.partial(onward_kernel, group, slice(0, early)),
        [(width, w5), (width, w5), (early, w6)],
        "onward",
        gotA,
        ext,
        after=(band,),
    )
    far1 = move(far1_w, (to_far, 0))
    crossA = move(crossA_w, (to_same, 1))
    crossB_w, ownB, far2_w = cutting(
        functools.partial(onward_kernel, group, slice(early, width)),
        [(width, w5), (width, w5), (width - early, w6)],
        "onward",
        gotB,
        ext,
        after=(crossA_w,),
    )
    far2 = move(far2_w, (to_far, 0))
    crossB = move(crossB_w, (to_same, 1))
    image, centre = make_image(
        [([own0], [cross0]), ([ownA], [crossA])], band, group, width
    )
    crossC1_w, ownC1 = cutting(
        functools.partial(parted_kernel, group), [(early, w5)] * 2, "parted", far1, after=(image,)
    )
    crossC1 = move(crossC1_w, (to_same, 1))
    crossC2_w, ownC2 = cutting(
        functools.partial(parted_kernel, group), [(width - early, w5)] * 2, "parted", far2
    )
    crossC2 = move(crossC2_w, (to_same, 1))

    scaling = 1.0 / math.sqrt(block_total * block_size)
    sums = []
    for matrix in range(2):
        keep, send = make_projection(
            matrix,
            [([ownB], [crossB]), ([ownC1, ownC2], [crossC1, crossC2])],
            band,
            image,
            centre,
            group,
            scaling,
            total // unit_count,
        )
        sums.append(keep + lax.ppermute(send, "sub", [(0, 1), (1, 0)]))
    chip = jnp.stack(sums)
    result = chip[:, :width]
    for slot, to in ((3, to_far), (2, to_ahead), (1, to_behind), (0, to_same)):
        for flip in range(X):
            if slot == 0 and flip == 0:
                continue
            first = (slot * X + flip) * width
            message = chip[:, first : first + width].astype(jnp.bfloat16)
            result = result + move(message, (to, flip)).astype(jnp.float32)
    if dof_count > 1:
        result = lax.psum_scatter(result, "dof", scatter_dimension=2, tiled=True)
    return result.transpose(0, 2, 1)


def solution(mesh):
    return jax.shard_map(
        body,
        mesh=mesh,
        in_specs=(
            P(("dof", "sub"), ("parts", "mode")),
            P(("parts", "dof", "sub"), "mode", None, None, None),
            P(("parts", "dof", "sub"), "mode", None, None, None),
            P(("dof", "sub"), "mode", None),
        ),
        out_specs=P("parts", ("dof", "sub"), "mode"),
        check_vma=False,
    )
```

time: 75.4 us -> 71.7 us (0.951)
  waiting for transfers between devices: 28.3 us -> 25.8 us
  starting transfers between devices: 34.4 us -> 33.5 us
    ppermute x16, waiting for transfers between devices: 25.6 us -> 23 us  [move(): return lax.ppermute(array, 'mode', pairs)]
    ppermute x16, starting transfers between devices: 33.2 us -> 32.3 us  [move(): return lax.ppermute(array, 'mode', pairs)]
    pallas_call x8 -> x9, Pallas kernels: 4.27 us -> 4.18 us  [the longest x2 2.29 us: make_projection(): pl.pallas_call(functools.partial(project_kernel, matrix, layout, slice(2...]
  transfers between devices with their start and end apart: 20 -> 20, of which waited for: 13 -> 11; matrix products, arithmetic and copies ran while one was open for 0% -> 0% of each run, Pallas kernels for 7% -> 7%
where the time goes in v4:
time: 71.7 us; the launch traced here: 71.5 us
  starting transfers between devices  33.5 us (47%)
  waiting for transfers between devices  25.8 us (36%)
  Pallas kernels  6.21 us (9%)
  local copies, waits for them, and re-layouts  4.94 us (7%)
  other arithmetic  0.92 us (1%)
    ppermute x16, starting transfers between devices, move(): return lax.ppermute(array, 'mode', pairs)  32.3 us
    ppermute x16, waiting for transfers between devices, move(): return lax.ppermute(array, 'mode', pairs)  23 us
    unnamed x8, local copies, waits for them, and re-layouts  4.9 us
    pallas_call x2, Pallas kernels, make_projection(): pl.pallas_call(functools.partial(project_kernel, matrix, layout, slice(2...  2.29 us
    pallas_call x1, Pallas kernels, make_band(): pl.pallas_call(functools.partial(band_kernel, per_unit, block_total), out...  2.03 us
    pallas_call x1, Pallas kernels, make_image(): pl.pallas_call(functools.partial(image_kernel, layout, slice(2 * group, 3...  1.57 us
    ppermute x2, waiting for transfers between devices, body(): sums.append(keep + lax.ppermute(send, 'sub', [(0, 1), (1, 0)]))  1.47 us
  transfers between devices with their start and end apart: 20, of which 11 were waited for; matrix products, arithmetic and copies ran while one was open for 0% of the time, Pallas kernels for 7%

profile of v4, /device:TPU:0, one launch (start us, length us, event | category | flops | bytes accessed | tf_op | source)
XLA Modules:
  0.0 71.5 jit_solution(6676934778621489737)
XLA Ops:
  3.1 3.8 %collective-permute-start.3 = (bf16[64,3072]{1,0:T(8,128)(2,1)S(1)}, bf16[64,3072]{1,0:T(8,128)(2,1)S(1)}, u32[]{:S(2)}, u32[]{:S(2)}) collective-permute-start(bf16[64,3072]{1,0:T(8,128)(2,1)S(1)} %get-tuple-element.32), channel_id=1, source_target_pairs={{0,8},{2,10},{4,0},{6,2},{8,12},{10,14},{12,4},{14,6},{1,9},{3,11}... | collective-permute-start | bytes 1179656 | tf_op jit(solution)/shard_map/ppermute | solution.py:255
  6.9 1.5 %collective-permute-start.6 = (bf16[64,2560]{1,0:T(8,128)(2,1)S(1)}, bf16[64,2560]{1,0:T(8,128)(2,1)S(1)}, u32[]{:S(2)}, u32[]{:S(2)}) collective-permute-start(bf16[64,2560]{1,0:T(8,128)(2,1)S(1)} %get-tuple-element.38), channel_id=1, source_target_pairs={{0,2},{2,0},{4,6},{6,4},{8,10},{10,8},{12,14},{14,12},{1,3},{3,1},... | collective-permute-start | bytes 983048 | tf_op jit(solution)/shard_map/ppermute | solution.py:255
  8.4 1.6 %copy-done.1 = bf16[1,4,16,128,128]{4,3,2,1,0:T(8,128)(2,1)S(1)} copy-done((bf16[1,4,16,128,128]{4,3,2,1,0:T(8,128)(2,1)S(1)}, bf16[1,4,16,128,128]{4,3,2,1,0:T(8,128)(2,1)}, u32[]{:S(2)}) %copy-start.1) | copy-done | bytes 2097176
  10.0 1.6 %copy-done.2 = bf16[1,4,16,128,128]{4,3,2,1,0:T(8,128)(2,1)S(1)} copy-done((bf16[1,4,16,128,128]{4,3,2,1,0:T(8,128)(2,1)S(1)}, bf16[1,4,16,128,128]{4,3,2,1,0:T(8,128)(2,1)}, u32[]{:S(2)}) %copy-start.2) | copy-done | bytes 2097176
  12.3 2.0 %band.1 = bf16[2,4,128,2560]{3,2,1,0:T(8,128)(2,1)S(1)} custom-call(s32[1,4,16]{2,1,0:T(4,128)S(1)} %copy-done.3, bf16[1,4,16,128,128]{4,3,2,1,0:T(8,128)(2,1)S(1)} %copy-done.1, bf16[1,4,16,128,128]{4,3,2,1,0:T(8,128)(2,1)S(1)} %copy-done.2, bf16[64,2560]{1,0:T(8,128)(2,1)S(1)} %get-tuple-element.33._.refs_0_), custom_call_target="tpu_custom_call" | custom-call | bytes 8388608 | tf_op jit(solution)/shard_map/band/pallas_call | solution.py:62
  14.3 2.1 %collective-permute-done.3.got = bf16[64,3072]{1,0:T(8,128)(2,1)S(1)} collective-permute-done((bf16[64,3072]{1,0:T(8,128)(2,1)S(1)}, bf16[64,3072]{1,0:T(8,128)(2,1)S(1)}, u32[]{:S(2)}, u32[]{:S(2)}) %collective-permute-start.3) | collective-permute-done | bytes 393248 | tf_op jit(solution)/shard_map/ppermute | solution.py:255
  16.5 1.6 %collective-permute-start.7 = (bf16[64,2560]{1,0:T(8,128)(2,1)S(1)}, bf16[64,2560]{1,0:T(8,128)(2,1)S(1)}, u32[]{:S(2)}, u32[]{:S(2)}) collective-permute-start(bf16[64,2560]{1,0:T(8,128)(2,1)S(1)} %get-tuple-element.34.refs_0_), channel_id=1, source_target_pairs={{0,2},{2,0},{4,6},{6,4},{8,10},{10,8},{12,14},{14,12},{1,3},{3,1},... | collective-permute-start | bytes 983048 | tf_op jit(solution)/shard_map/ppermute | solution.py:255
  18.0 3.0 %collective-permute-start.5 = (bf16[48,3072]{1,0:T(8,128)(2,1)S(1)}, bf16[48,3072]{1,0:T(8,128)(2,1)S(1)}, u32[]{:S(2)}, u32[]{:S(2)}) collective-permute-start(bf16[48,3072]{1,0:T(8,128)(2,1)S(1)} %get-tuple-element.37), channel_id=1, source_target_pairs={{0,12},{2,14},{4,8},{6,10},{8,4},{10,6},{12,0},{14,2},{1,13},{3,15... | collective-permute-start | bytes 884744 | tf_op jit(solution)/shard_map/ppermute | solution.py:255
  21.0 5.7 %collective-permute-done.2.got = bf16[64,3072]{1,0:T(8,128)(2,1)S(1)} collective-permute-done((bf16[64,3072]{1,0:T(8,128)(2,1)S(1)}, bf16[64,3072]{1,0:T(8,128)(2,1)S(1)}, u32[]{:S(2)}, u32[]{:S(2)}) %collective-permute-start.2) | collective-permute-done | bytes 393248 | tf_op jit(solution)/shard_map/ppermute | solution.py:255
  26.7 1.6 %collective-permute-start.4 = (bf16[64,2560]{1,0:T(8,128)(2,1)S(1)}, bf16[64,2560]{1,0:T(8,128)(2,1)S(1)}, u32[]{:S(2)}, u32[]{:S(2)}) collective-permute-start(bf16[64,2560]{1,0:T(8,128)(2,1)S(1)} %get-tuple-element.36), channel_id=1, source_target_pairs={{0,2},{2,0},{4,6},{6,4},{8,10},{10,8},{12,14},{14,12},{1,3},{3,1},... | collective-permute-start | bytes 983048 | tf_op jit(solution)/shard_map/ppermute | solution.py:255
  28.3 1.6 %image.1 = (bf16[256,1024]{1,0:T(8,128)(2,1)S(1)}, bf16[2,128,512]{2,1,0:T(8,128)(2,1)S(1)}) custom-call(bf16[64,2560]{1,0:T(8,128)(2,1)S(1)} %get-tuple-element.33._.refs_0_, bf16[64,2560]{1,0:T(8,128)(2,1)S(1)} %collective-permute-done.6.refs_1_, bf16[64,2560]{1,0:T(8,128)(2,1)S(1)} %get-tuple-element.39.refs_2_, ...), custom_call_target="tpu_custom_call" | custom-call | flops 1342177280 | bytes 4194304 | tf_op jit(solution)/shard_map/image/pallas_call | solution.py:158
  29.9 2.6 %collective-permute-done.5.got = bf16[48,3072]{1,0:T(8,128)(2,1)S(1)} collective-permute-done((bf16[48,3072]{1,0:T(8,128)(2,1)S(1)}, bf16[48,3072]{1,0:T(8,128)(2,1)S(1)}, u32[]{:S(2)}, u32[]{:S(2)}) %collective-permute-start.5) | collective-permute-done | bytes 294944 | tf_op jit(solution)/shard_map/ppermute | solution.py:255
  32.5 1.6 %collective-permute-start.9 = (bf16[48,2560]{1,0:T(8,128)(2,1)S(1)}, bf16[48,2560]{1,0:T(8,128)(2,1)S(1)}, u32[]{:S(2)}, u32[]{:S(2)}) collective-permute-start(bf16[48,2560]{1,0:T(8,128)(2,1)S(1)} %get-tuple-element.44), channel_id=1, source_target_pairs={{0,2},{2,0},{4,6},{6,4},{8,10},{10,8},{12,14},{14,12},{1,3},{3,1},... | collective-permute-start | bytes 737288 | tf_op jit(solution)/shard_map/ppermute | solution.py:255
  34.1 2.5 %collective-permute-start.8 = (bf16[16,3072]{1,0:T(8,128)(2,1)S(1)}, bf16[16,3072]{1,0:T(8,128)(2,1)S(1)}, u32[]{:S(2)}, u32[]{:S(2)}) collective-permute-start(bf16[16,3072]{1,0:T(8,128)(2,1)S(1)} %get-tuple-element.42), channel_id=1, source_target_pairs={{0,12},{2,14},{4,8},{6,10},{8,4},{10,6},{12,0},{14,2},{1,13},{3,15... | collective-permute-start | bytes 294920 | tf_op jit(solution)/shard_map/ppermute | solution.py:255
  36.5 4.0 %collective-permute-done.8.got = bf16[16,3072]{1,0:T(8,128)(2,1)S(1)} collective-permute-done((bf16[16,3072]{1,0:T(8,128)(2,1)S(1)}, bf16[16,3072]{1,0:T(8,128)(2,1)S(1)}, u32[]{:S(2)}, u32[]{:S(2)}) %collective-permute-start.8) | collective-permute-done | bytes 98336 | tf_op jit(solution)/shard_map/ppermute | solution.py:255
  41.2 3.9 %collective-permute-done.10.refs_5_ = bf16[16,2560]{1,0:T(8,128)(2,1)S(1)} collective-permute-done((bf16[16,2560]{1,0:T(8,128)(2,1)S(1)}, bf16[16,2560]{1,0:T(8,128)(2,1)S(1)}, u32[]{:S(2)}, u32[]{:S(2)}) %collective-permute-start.10) | collective-permute-done | bytes 81952 | tf_op jit(solution)/shard_map/ppermute | solution.py:255
  45.1 1.1 %project.3 = (f32[512,256]{1,0:T(8,128)S(1)}, f32[512,256]{1,0:T(8,128)S(1)}) custom-call(bf16[64,2560]{1,0:T(8,128)(2,1)S(1)} %get-tuple-element.35.refs_0_, bf16[64,2560]{1,0:T(8,128)(2,1)S(1)} %collective-permute-done.4.refs_1_, bf16[48,2560]{1,0:T(8,128)(2,1)S(1)} %get-tuple-element.41.refs_2_, bf16[16,2560]{1,0:T(8,128)(2,1)S(1)} %get-tuple-element.43.refs_3_, ...), custom_call_target="tpu_custom_call" | custom-call | flops 268435456 | bytes 2097152 | tf_op jit(solution)/shard_map/project/pallas_call | solution.py:218
  46.3 1.1 %project.2 = (f32[512,256]{1,0:T(8,128)S(1)}, f32[512,256]{1,0:T(8,128)S(1)}) custom-call(bf16[64,2560]{1,0:T(8,128)(2,1)S(1)} %get-tuple-element.35.refs_0_, bf16[64,2560]{1,0:T(8,128)(2,1)S(1)} %collective-permute-done.4.refs_1_, bf16[48,2560]{1,0:T(8,128)(2,1)S(1)} %get-tuple-element.41.refs_2_, bf16[16,2560]{1,0:T(8,128)(2,1)S(1)} %get-tuple-element.43.refs_3_, ...), custom_call_target="tpu_custom_call" | custom-call | flops 268435456 | bytes 2097152 | tf_op jit(solution)/shard_map/project/pallas_call | solution.py:218
  48.3 1.3 %collective-permute-done.11 = f32[512,256]{1,0:T(8,128)S(1)} collective-permute-done((f32[512,256]{1,0:T(8,128)S(1)}, f32[512,256]{1,0:T(8,128)S(1)}, u32[]{:S(2)}, u32[]{:S(2)}) %collective-permute-start.11) | collective-permute-done | bytes 524320 | tf_op jit(solution)/shard_map/ppermute | solution.py:336
  50.4 7.9 %collective-permute-start.18 = (bf16[2,64,256]{2,1,0:T(8,128)(2,1)S(1)}, bf16[2,64,256]{2,1,0:T(8,128)(2,1)S(1)}, u32[]{:S(2)}, u32[]{:S(2)}) collective-permute-start(bf16[2,64,256]{2,1,0:T(8,128)(2,1)S(1)} %get-tuple-element.53), channel_id=1, source_target_pairs={{0,6},{2,4},{4,14},{6,12},{8,2},{10,0},{12,10},{14,8},{1,7},{3,5},... | collective-permute-start | bytes 196616 | tf_op jit(solution)/shard_map/ppermute | solution.py:255
  58.3 2.9 %collective-permute-start.16 = (bf16[2,64,256]{2,1,0:T(8,128)(2,1)S(1)}, bf16[2,64,256]{2,1,0:T(8,128)(2,1)S(1)}, u32[]{:S(2)}, u32[]{:S(2)}) collective-permute-start(bf16[2,64,256]{2,1,0:T(8,128)(2,1)S(1)} %get-tuple-element.55), channel_id=1, source_target_pairs={{0,10},{2,8},{4,2},{6,0},{8,14},{10,12},{12,6},{14,4},{1,11},{3,9}... | collective-permute-start | bytes 196616 | tf_op jit(solution)/shard_map/ppermute | solution.py:255
  61.3 3.3 %collective-permute-start.14 = (bf16[2,64,256]{2,1,0:T(8,128)(2,1)S(1)}, bf16[2,64,256]{2,1,0:T(8,128)(2,1)S(1)}, u32[]{:S(2)}, u32[]{:S(2)}) collective-permute-start(bf16[2,64,256]{2,1,0:T(8,128)(2,1)S(1)} %get-tuple-element.57), channel_id=1, source_target_pairs={{0,14},{2,12},{4,10},{6,8},{8,6},{10,4},{12,2},{14,0},{1,15},{3,13... | collective-permute-start | bytes 196616 | tf_op jit(solution)/shard_map/ppermute | solution.py:255
  64.6 1.5 %collective-permute-start.13 = (bf16[2,64,256]{2,1,0:T(8,128)(2,1)S(1)}, bf16[2,64,256]{2,1,0:T(8,128)(2,1)S(1)}, u32[]{:S(2)}, u32[]{:S(2)}) collective-permute-start(bf16[2,64,256]{2,1,0:T(8,128)(2,1)S(1)} %get-tuple-element.51), channel_id=1, source_target_pairs={{0,12},{2,14},{4,8},{6,10},{8,4},{10,6},{12,0},{14,2},{1,13},{3,15... | collective-permute-start | bytes 196616 | tf_op jit(solution)/shard_map/ppermute | solution.py:255
  66.0 3.6 %collective-permute-done.14 = bf16[2,64,256]{2,1,0:T(8,128)(2,1)S(1)} collective-permute-done((bf16[2,64,256]{2,1,0:T(8,128)(2,1)S(1)}, bf16[2,64,256]{2,1,0:T(8,128)(2,1)S(1)}, u32[]{:S(2)}, u32[]{:S(2)}) %collective-permute-start.14) | collective-permute-done | bytes 65568 | tf_op jit(solution)/shard_map/ppermute | solution.py:255
  (39 shorter events, 8.2 us)
Async XLA Ops:
  0.0 1.0 %copy-start = (bf16[4096,64]{0,1:T(8,128)(2,1)S(1)}, bf16[4096,64]{0,1:T(8,128)(2,1)}, u32[]{:S(2)}) copy-start(bf16[4096,64]{0,1:T(8,128)(2,1)} %param.4) | copy-start | bytes 1572868
  1.1 1.5 %collective-permute-start = (bf16[64,1024]{1,0:T(8,128)(2,1)S(1)}, bf16[64,1024]{1,0:T(8,128)(2,1)S(1)}, u32[]{:S(2)}, u32[]{:S(2)}) collective-permute-start(bf16[64,1024]{1,0:T(8,128)(2,1)S(1)} %get-tuple-element.28), channel_id=1, source_target_pairs={{0,1},{1,0},{2,3},{3,2},{4,5},{5,4},{6,7},{7,6},{8,9},{9,8},{10,11... | collective-permute-start | bytes 393224 | tf_op jit(solution)/shard_map/ppermute | solution.py:273
  1.6 1.3 %collective-permute-start.1 = (bf16[64,1024]{1,0:T(8,128)(2,1)S(1)}, bf16[64,1024]{1,0:T(8,128)(2,1)S(1)}, u32[]{:S(2)}, u32[]{:S(2)}) collective-permute-start(bf16[64,1024]{1,0:T(8,128)(2,1)S(1)} %get-tuple-element.29), channel_id=1, source_target_pairs={{1,0},{0,1},{3,2},{2,3},{5,4},{4,5},{7,6},{6,7},{9,8},{8,9},{11,10... | collective-permute-start | bytes 393224 | tf_op jit(solution)/shard_map/ppermute | solution.py:274
  3.1 13.3 %collective-permute-start.3 = (bf16[64,3072]{1,0:T(8,128)(2,1)S(1)}, bf16[64,3072]{1,0:T(8,128)(2,1)S(1)}, u32[]{:S(2)}, u32[]{:S(2)}) collective-permute-start(bf16[64,3072]{1,0:T(8,128)(2,1)S(1)} %get-tuple-element.32), channel_id=1, source_target_pairs={{0,8},{2,10},{4,0},{6,2},{8,12},{10,14},{12,4},{14,6},{1,9},{3,11}... | collective-permute-start | bytes 1179656 | tf_op jit(solution)/shard_map/ppermute | solution.py:255
  6.9 19.8 %collective-permute-start.2 = (bf16[64,3072]{1,0:T(8,128)(2,1)S(1)}, bf16[64,3072]{1,0:T(8,128)(2,1)S(1)}, u32[]{:S(2)}, u32[]{:S(2)}) collective-permute-start(bf16[64,3072]{1,0:T(8,128)(2,1)S(1)} %get-tuple-element.30), channel_id=1, source_target_pairs={{0,4},{2,6},{4,12},{6,14},{8,0},{10,2},{12,8},{14,10},{1,5},{3,7},... | collective-permute-start | bytes 1179656 | tf_op jit(solution)/shard_map/ppermute | solution.py:255
  6.9 21.4 %collective-permute-start.6 = (bf16[64,2560]{1,0:T(8,128)(2,1)S(1)}, bf16[64,2560]{1,0:T(8,128)(2,1)S(1)}, u32[]{:S(2)}, u32[]{:S(2)}) collective-permute-start(bf16[64,2560]{1,0:T(8,128)(2,1)S(1)} %get-tuple-element.38), channel_id=1, source_target_pairs={{0,2},{2,0},{4,6},{6,4},{8,10},{10,8},{12,14},{14,12},{1,3},{3,1},... | collective-permute-start | bytes 983048 | tf_op jit(solution)/shard_map/ppermute | solution.py:255
  8.4 1.6 %copy-start.1 = (bf16[1,4,16,128,128]{4,3,2,1,0:T(8,128)(2,1)S(1)}, bf16[1,4,16,128,128]{4,3,2,1,0:T(8,128)(2,1)}, u32[]{:S(2)}) copy-start(bf16[1,4,16,128,128]{4,3,2,1,0:T(8,128)(2,1)} %gyro.1) | copy-start | bytes 6291460
  10.0 1.6 %copy-start.2 = (bf16[1,4,16,128,128]{4,3,2,1,0:T(8,128)(2,1)S(1)}, bf16[1,4,16,128,128]{4,3,2,1,0:T(8,128)(2,1)}, u32[]{:S(2)}) copy-start(bf16[1,4,16,128,128]{4,3,2,1,0:T(8,128)(2,1)} %spin.1) | copy-start | bytes 6291460
  11.6 0.7 copy-start.3
  16.5 11.8 %collective-permute-start.7 = (bf16[64,2560]{1,0:T(8,128)(2,1)S(1)}, bf16[64,2560]{1,0:T(8,128)(2,1)S(1)}, u32[]{:S(2)}, u32[]{:S(2)}) collective-permute-start(bf16[64,2560]{1,0:T(8,128)(2,1)S(1)} %get-tuple-element.34.refs_0_), channel_id=1, source_target_pairs={{0,2},{2,0},{4,6},{6,4},{8,10},{10,8},{12,14},{14,12},{1,3},{3,1},... | collective-permute-start | bytes 983048 | tf_op jit(solution)/shard_map/ppermute | solution.py:255
  18.0 14.4 %collective-permute-start.5 = (bf16[48,3072]{1,0:T(8,128)(2,1)S(1)}, bf16[48,3072]{1,0:T(8,128)(2,1)S(1)}, u32[]{:S(2)}, u32[]{:S(2)}) collective-permute-start(bf16[48,3072]{1,0:T(8,128)(2,1)S(1)} %get-tuple-element.37), channel_id=1, source_target_pairs={{0,12},{2,14},{4,8},{6,10},{8,4},{10,6},{12,0},{14,2},{1,13},{3,15... | collective-permute-start | bytes 884744 | tf_op jit(solution)/shard_map/ppermute | solution.py:255
  26.7 18.4 %collective-permute-start.4 = (bf16[64,2560]{1,0:T(8,128)(2,1)S(1)}, bf16[64,2560]{1,0:T(8,128)(2,1)S(1)}, u32[]{:S(2)}, u32[]{:S(2)}) collective-permute-start(bf16[64,2560]{1,0:T(8,128)(2,1)S(1)} %get-tuple-element.36), channel_id=1, source_target_pairs={{0,2},{2,0},{4,6},{6,4},{8,10},{10,8},{12,14},{14,12},{1,3},{3,1},... | collective-permute-start | bytes 983048 | tf_op jit(solution)/shard_map/ppermute | solution.py:255
  32.5 12.6 %collective-permute-start.9 = (bf16[48,2560]{1,0:T(8,128)(2,1)S(1)}, bf16[48,2560]{1,0:T(8,128)(2,1)S(1)}, u32[]{:S(2)}, u32[]{:S(2)}) collective-permute-start(bf16[48,2560]{1,0:T(8,128)(2,1)S(1)} %get-tuple-element.44), channel_id=1, source_target_pairs={{0,2},{2,0},{4,6},{6,4},{8,10},{10,8},{12,14},{14,12},{1,3},{3,1},... | collective-permute-start | bytes 737288 | tf_op jit(solution)/shard_map/ppermute | solution.py:255
  34.1 6.5 %collective-permute-start.8 = (bf16[16,3072]{1,0:T(8,128)(2,1)S(1)}, bf16[16,3072]{1,0:T(8,128)(2,1)S(1)}, u32[]{:S(2)}, u32[]{:S(2)}) collective-permute-start(bf16[16,3072]{1,0:T(8,128)(2,1)S(1)} %get-tuple-element.42), channel_id=1, source_target_pairs={{0,12},{2,14},{4,8},{6,10},{8,4},{10,6},{12,0},{14,2},{1,13},{3,15... | collective-permute-start | bytes 294920 | tf_op jit(solution)/shard_map/ppermute | solution.py:255
  40.6 4.5 %collective-permute-start.10 = (bf16[16,2560]{1,0:T(8,128)(2,1)S(1)}, bf16[16,2560]{1,0:T(8,128)(2,1)S(1)}, u32[]{:S(2)}, u32[]{:S(2)}) collective-permute-start(bf16[16,2560]{1,0:T(8,128)(2,1)S(1)} %get-tuple-element.45), channel_id=1, source_target_pairs={{0,2},{2,0},{4,6},{6,4},{8,10},{10,8},{12,14},{14,12},{1,3},{3,1},... | collective-permute-start | bytes 245768 | tf_op jit(solution)/shard_map/ppermute | solution.py:255
  46.3 2.0 %collective-permute-start.12 = (f32[512,256]{1,0:T(8,128)S(1)}, f32[512,256]{1,0:T(8,128)S(1)}, u32[]{:S(2)}, u32[]{:S(2)}) collective-permute-start(f32[512,256]{1,0:T(8,128)S(1)} %get-tuple-element.50), channel_id=1, source_target_pairs={{0,1},{1,0},{2,3},{3,2},{4,5},{5,4},{6,7},{7,6},{8,9},{9,8},{10,11... | collective-permute-start | bytes 1572872 | tf_op jit(solution)/shard_map/ppermute | solution.py:336
  47.5 2.1 %collective-permute-start.11 = (f32[512,256]{1,0:T(8,128)S(1)}, f32[512,256]{1,0:T(8,128)S(1)}, u32[]{:S(2)}, u32[]{:S(2)}) collective-permute-start(f32[512,256]{1,0:T(8,128)S(1)} %get-tuple-element.48), channel_id=1, source_target_pairs={{0,1},{1,0},{2,3},{3,2},{4,5},{5,4},{6,7},{7,6},{8,9},{9,8},{10,11... | collective-permute-start | bytes 1572872 | tf_op jit(solution)/shard_map/ppermute | solution.py:336
  49.8 11.5 %collective-permute-start.19 = (bf16[2,64,256]{2,1,0:T(8,128)(2,1)S(1)}, bf16[2,64,256]{2,1,0:T(8,128)(2,1)S(1)}, u32[]{:S(2)}, u32[]{:S(2)}) collective-permute-start(bf16[2,64,256]{2,1,0:T(8,128)(2,1)S(1)} %get-tuple-element.52), channel_id=1, source_target_pairs={{0,2},{2,0},{4,6},{6,4},{8,10},{10,8},{12,14},{14,12},{1,3},{3,1},... | collective-permute-start | bytes 196616 | tf_op jit(solution)/shard_map/ppermute | solution.py:255
  50.4 14.2 %collective-permute-start.18 = (bf16[2,64,256]{2,1,0:T(8,128)(2,1)S(1)}, bf16[2,64,256]{2,1,0:T(8,128)(2,1)S(1)}, u32[]{:S(2)}, u32[]{:S(2)}) collective-permute-start(bf16[2,64,256]{2,1,0:T(8,128)(2,1)S(1)} %get-tuple-element.53), channel_id=1, source_target_pairs={{0,6},{2,4},{4,14},{6,12},{8,2},{10,0},{12,10},{14,8},{1,7},{3,5},... | collective-permute-start | bytes 196616 | tf_op jit(solution)/shard_map/ppermute | solution.py:255
  58.3 7.8 %collective-permute-start.17 = (bf16[2,64,256]{2,1,0:T(8,128)(2,1)S(1)}, bf16[2,64,256]{2,1,0:T(8,128)(2,1)S(1)}, u32[]{:S(2)}, u32[]{:S(2)}) collective-permute-start(bf16[2,64,256]{2,1,0:T(8,128)(2,1)S(1)} %get-tuple-element.54), channel_id=1, source_target_pairs={{0,4},{2,6},{4,12},{6,14},{8,0},{10,2},{12,8},{14,10},{1,5},{3,7},... | collective-permute-start | bytes 196616 | tf_op jit(solution)/shard_map/ppermute | solution.py:255
  58.3 7.8 %collective-permute-start.16 = (bf16[2,64,256]{2,1,0:T(8,128)(2,1)S(1)}, bf16[2,64,256]{2,1,0:T(8,128)(2,1)S(1)}, u32[]{:S(2)}, u32[]{:S(2)}) collective-permute-start(bf16[2,64,256]{2,1,0:T(8,128)(2,1)S(1)} %get-tuple-element.55), channel_id=1, source_target_pairs={{0,10},{2,8},{4,2},{6,0},{8,14},{10,12},{12,6},{14,4},{1,11},{3,9}... | collective-permute-start | bytes 196616 | tf_op jit(solution)/shard_map/ppermute | solution.py:255
  61.1 4.9 %collective-permute-start.15 = (bf16[2,64,256]{2,1,0:T(8,128)(2,1)S(1)}, bf16[2,64,256]{2,1,0:T(8,128)(2,1)S(1)}, u32[]{:S(2)}, u32[]{:S(2)}) collective-permute-start(bf16[2,64,256]{2,1,0:T(8,128)(2,1)S(1)} %get-tuple-element.56), channel_id=1, source_target_pairs={{0,8},{2,10},{4,0},{6,2},{8,12},{10,14},{12,4},{14,6},{1,9},{3,11}... | collective-permute-start | bytes 196616 | tf_op jit(solution)/shard_map/ppermute | solution.py:255
  61.3 8.4 %collective-permute-start.14 = (bf16[2,64,256]{2,1,0:T(8,128)(2,1)S(1)}, bf16[2,64,256]{2,1,0:T(8,128)(2,1)S(1)}, u32[]{:S(2)}, u32[]{:S(2)}) collective-permute-start(bf16[2,64,256]{2,1,0:T(8,128)(2,1)S(1)} %get-tuple-element.57), channel_id=1, source_target_pairs={{0,14},{2,12},{4,10},{6,8},{8,6},{10,4},{12,2},{14,0},{1,15},{3,13... | collective-permute-start | bytes 196616 | tf_op jit(solution)/shard_map/ppermute | solution.py:255
  64.6 6.2 %collective-permute-start.13 = (bf16[2,64,256]{2,1,0:T(8,128)(2,1)S(1)}, bf16[2,64,256]{2,1,0:T(8,128)(2,1)S(1)}, u32[]{:S(2)}, u32[]{:S(2)}) collective-permute-start(bf16[2,64,256]{2,1,0:T(8,128)(2,1)S(1)} %get-tuple-element.51), channel_id=1, source_target_pairs={{0,12},{2,14},{4,8},{6,10},{8,4},{10,6},{12,0},{14,2},{1,13},{3,15... | collective-permute-start | bytes 196616 | tf_op jit(solution)/shard_map/ppermute | solution.py:255

commit v5 on v4

--- a/solution.py
+++ b/solution.py
@@ -10,7 +10,7 @@
 
 HB = 8
 X = 2
-EARLY = 48
+PIECES = (32, 32)
 VMEM_LIMIT = 24 * 1024 * 1024
 NT = (((1,), (1,)), ((), ()))
 VMEM = pl.BlockSpec(memory_space=pltpu.VMEM)
@@ -72,21 +72,30 @@
     return band.reshape(2 * rows * size, width)
 
 
-def rim_kernel(phi, low, high):
-    low[...] = phi[:, phi.shape[1] - low.shape[1] :]
-    high[...] = phi[:, : high.shape[1]]
-
-
 def cut(group, out, source, start):
     out[...] = source[:, pl.ds(aligned(start, group), out.shape[1])]
 
 
-def first_kernel(group, phi, low, high, ext, to_ahead, to_behind, cross, own):
+def stage_kernel(phi, out):
+    pltpu.sync_copy(phi, out)
+
+
+def stage(phi):
+    return pl.pallas_call(
+        stage_kernel,
+        out_shape=jax.ShapeDtypeStruct(phi.shape, phi.dtype),
+        in_specs=[ANY],
+        out_specs=VMEM,
+        compiler_params=params(),
+        name="stage",
+    )(phi)
+
+
+def first_kernel(group, rim, phi, below, above, ext, to_ahead, to_behind, cross, own):
     m, z, _ = place_in_mode()
-    rim = low.shape[1]
-    ext[:, :rim] = low[...]
+    ext[:, :rim] = below[:, below.shape[1] - rim :]
     ext[:, rim : rim + phi.shape[1]] = phi[...]
-    ext[:, rim + phi.shape[1] :] = high[...]
+    ext[:, rim + phi.shape[1] :] = above[:, :rim]
     cut(group, to_ahead, ext, 2 * ahead(z))
     cut(group, to_behind, ext, 2 * behind(z))
     cut(group, cross, ext, m + 1 - 2 * lax.rem(m, 2))
@@ -100,12 +109,16 @@
     cut(group, own, got, x)
 
 
-def onward_kernel(group, rows, got, ext, *refs):
-    cross, own, out = refs[-3:]
+def onward_kernel(group, got, ext, *refs):
+    cross, own, *far = refs[-2 - len(PIECES) :]
     _, z, x = place_in_mode()
     cut(group, cross, got, 1 - x)
     cut(group, own, got, x)
-    out[...] = ext[rows, pl.ds(aligned(2 * (3 - z), group), out.shape[1])]
+    at = 0
+    for out in far:
+        rows, span = out.shape
+        out[...] = ext[at : at + rows, pl.ds(aligned(2 * (3 - z), group), span)]
+        at += rows
 
 
 def cutting(kernel, shapes, name, *operands, after=()):
@@ -269,63 +282,66 @@
     phi = modes.T
     forward, backward = ring(unit_count)
     rim = HB * block_size
-    low_w, high_w = cutting(rim_kernel, [(width, rim)] * 2, "rims", phi)
-    low = lax.ppermute(low_w, ("dof", "sub"), forward)
-    high = lax.ppermute(high_w, ("dof", "sub"), backward)
+    units = ("dof", "sub")
+    if unit_count == 2:
+        below = above = lax.ppermute(phi, units, forward)
+    else:
+        below = lax.ppermute(phi[:, phi.shape[1] - rim :], units, forward)
+        above = lax.ppermute(phi[:, :rim], units, backward)
 
     w5, w6 = 5 * group, 6 * group
     ext, ahead_w, behind_w, cross0_w, own0 = cutting(
-        functools.partial(first_kernel, group),
+        functools.partial(first_kernel, group, rim),
         [(width, w) for w in (phi.shape[1] + 2 * rim, w6, w6, w5, w5)],
         "first",
-        phi,
-        low,
-        high,
+        stage(phi),
+        below,
+        above,
     )
     gotA = move(ahead_w, (to_ahead, 0))
     gotB = move(behind_w, (to_behind, 0))
     cross0 = move(cross0_w, (to_same, 1))
     band = make_band(pattern, gyroscopic, centrifugal, own0, w5, per_unit, block_total)
 
-    early = EARLY
-    crossA_w, ownA, far1_w = cutting(
-        functools.partial(onward_kernel, group, slice(0, early)),
-        [(width, w5), (width, w5), (early, w6)],
+    crossA_w, ownA, *far_w = cutting(
+        functools.partial(onward_kernel, group),
+        [(width, w5), (width, w5)] + [(rows, w6) for rows in PIECES],
         "onward",
         gotA,
         ext,
         after=(band,),
     )
-    far1 = move(far1_w, (to_far, 0))
+    far = [move(piece, (to_far, 0)) for piece in far_w]
     crossA = move(crossA_w, (to_same, 1))
-    crossB_w, ownB, far2_w = cutting(
-        functools.partial(onward_kernel, group, slice(early, width)),
-        [(width, w5), (width, w5), (width - early, w6)],
-        "onward",
+    crossB_w, ownB = cutting(
+        functools.partial(parted_kernel, group),
+        [(width, w5), (width, w5)],
+        "parted",
         gotB,
-        ext,
         after=(crossA_w,),
     )
-    far2 = move(far2_w, (to_far, 0))
     crossB = move(crossB_w, (to_same, 1))
     image, centre = make_image(
         [([own0], [cross0]), ([ownA], [crossA])], band, group, width
     )
-    crossC1_w, ownC1 = cutting(
-        functools.partial(parted_kernel, group), [(early, w5)] * 2, "parted", far1, after=(image,)
-    )
-    crossC1 = move(crossC1_w, (to_same, 1))
-    crossC2_w, ownC2 = cutting(
-        functools.partial(parted_kernel, group), [(width - early, w5)] * 2, "parted", far2
-    )
-    crossC2 = move(crossC2_w, (to_same, 1))
+    ownC, crossC = [], []
+    for piece in far:
+        cross_w, own = cutting(
+            functools.partial(parted_kernel, group),
+            [(piece.shape[0], w5)] * 2,
+            "parted",
+            piece,
+            after=(image,),
+        )
+        ownC.append(own)
+        crossC.append(move(cross_w, (to_same, 1)))
 
     scaling = 1.0 / math.sqrt(block_total * block_size)
     sums = []
     for matrix in range(2):
         keep, send = make_projection(
             matrix,
-            [([ownB], [crossB]), ([ownC1, ownC2], [crossC1, crossC2])],
+            [([ownB], [crossB]), (ownC, crossC)],
             band,
             image,
             centre,
@@ -336,7 +352,7 @@
         sums.append(keep + lax.ppermute(send, "sub", [(0, 1), (1, 0)]))
     chip = jnp.stack(sums)
     result = chip[:, :width]
-    for slot, to in ((3, to_far), (2, to_ahead), (1, to_behind), (0, to_same)):
+    for slot, to in ((0, to_same), (1, to_behind), (2, to_ahead), (3, to_far)):
         for flip in range(X):
             if slot == 0 and flip == 0:
                 continue

time: 71.7 us -> 66.6 us (0.929)
  starting transfers between devices: 33.5 us -> 30.4 us
  local copies, waits for them, and re-layouts: 4.94 us -> 2.85 us
    ppermute x16, starting transfers between devices: 32.3 us -> 29.3 us  [move(): return lax.ppermute(array, 'mode', pairs)]
    unnamed x8, local copies, waits for them, and re-layouts: 4.9 us -> 2.82 us
    ppermute x16, waiting for transfers between devices: 23 us -> 24 us  [move(): return lax.ppermute(array, 'mode', pairs)]
    ppermute x2 -> x1, waiting for transfers between devices: 1.27 us -> 0.49 us  [body(): below = above = lax.ppermute(phi, units, forward)]
  transfers between devices with their start and end apart: 20 -> 19, of which waited for: 11 -> 13; matrix products, arithmetic and copies ran while one was open for 0% -> 0% of each run, Pallas kernels for 7% -> 7%
where the time goes in v5:
time: 66.6 us; the launch traced here: 66.4 us
  starting transfers between devices  30.4 us (46%)
  waiting for transfers between devices  25.9 us (39%)
  Pallas kernels  6.21 us (9%)
  local copies, waits for them, and re-layouts  2.85 us (4%)
  other arithmetic  0.92 us (1%)
    ppermute x16, starting transfers between devices, move(): return lax.ppermute(array, 'mode', pairs)  29.3 us
    ppermute x16, waiting for transfers between devices, move(): return lax.ppermute(array, 'mode', pairs)  24 us
    unnamed x8, local copies, waits for them, and re-layouts  2.82 us
    pallas_call x2, Pallas kernels, make_projection(): pl.pallas_call(functools.partial(project_kernel, matrix, layout, slice(2...  2.28 us
    pallas_call x1, Pallas kernels, make_band(): pl.pallas_call(functools.partial(band_kernel, per_unit, block_total), out...  2.03 us
    pallas_call x1, Pallas kernels, make_image(): pl.pallas_call(functools.partial(image_kernel, layout, slice(2 * group, 3...  1.55 us
    ppermute x2, waiting for transfers between devices, body(): sums.append(keep + lax.ppermute(send, 'sub', [(0, 1), (1, 0)]))  1.47 us
  transfers between devices with their start and end apart: 19, of which 13 were waited for; matrix products, arithmetic and copies ran while one was open for 0% of the time, Pallas kernels for 7%

profile of v5, /device:TPU:0, one launch (start us, length us, event | category | flops | bytes accessed | tf_op | source)
XLA Modules:
  0.0 66.4 jit_solution(10641112573511962951)
XLA Ops:
  0.5 1.2 %copy-done.2 = bf16[4096,64]{0,1:T(8,128)(2,1)S(1)} copy-done((bf16[4096,64]{0,1:T(8,128)(2,1)S(1)}, bf16[4096,64]{0,1:T(8,128)(2,1)}, u32[]{:S(2)}) %copy-start.2) | copy-done | bytes 524312
  2.4 4.0 %collective-permute-start.2 = (bf16[64,3072]{1,0:T(8,128)(2,1)S(1)}, bf16[64,3072]{1,0:T(8,128)(2,1)S(1)}, u32[]{:S(2)}, u32[]{:S(2)}) collective-permute-start(bf16[64,3072]{1,0:T(8,128)(2,1)S(1)} %get-tuple-element.27), channel_id=1, source_target_pairs={{0,8},{2,10},{4,0},{6,2},{8,12},{10,14},{12,4},{14,6},{1,9},{3,11}... | collective-permute-start | bytes 1179656 | tf_op jit(solution)/shard_map/ppermute | solution.py:268
  6.4 1.5 %collective-permute-start.5 = (bf16[64,2560]{1,0:T(8,128)(2,1)S(1)}, bf16[64,2560]{1,0:T(8,128)(2,1)S(1)}, u32[]{:S(2)}, u32[]{:S(2)}) collective-permute-start(bf16[64,2560]{1,0:T(8,128)(2,1)S(1)} %get-tuple-element.34), channel_id=1, source_target_pairs={{0,2},{2,0},{4,6},{6,4},{8,10},{10,8},{12,14},{14,12},{1,3},{3,1},... | collective-permute-start | bytes 983048 | tf_op jit(solution)/shard_map/ppermute | solution.py:268
  7.9 1.6 %copy-done.1 = bf16[1,4,16,128,128]{4,3,2,1,0:T(8,128)(2,1)S(1)} copy-done((bf16[1,4,16,128,128]{4,3,2,1,0:T(8,128)(2,1)S(1)}, bf16[1,4,16,128,128]{4,3,2,1,0:T(8,128)(2,1)}, u32[]{:S(2)}) %copy-start.1) | copy-done | bytes 2097176
  9.5 2.0 %band.1 = bf16[2,4,128,2560]{3,2,1,0:T(8,128)(2,1)S(1)} custom-call(s32[1,4,16]{2,1,0:T(4,128)S(1)} %copy-done.3, bf16[1,4,16,128,128]{4,3,2,1,0:T(8,128)(2,1)S(1)} %copy-done, bf16[1,4,16,128,128]{4,3,2,1,0:T(8,128)(2,1)S(1)} %copy-done.1, bf16[64,2560]{1,0:T(8,128)(2,1)S(1)} %get-tuple-element.29._.refs_0_), custom_call_target="tpu_custom_call" | custom-call | bytes 8388608 | tf_op jit(solution)/shard_map/band/pallas_call | solution.py:62
  11.5 4.4 %collective-permute-done.2.got = bf16[64,3072]{1,0:T(8,128)(2,1)S(1)} collective-permute-done((bf16[64,3072]{1,0:T(8,128)(2,1)S(1)}, bf16[64,3072]{1,0:T(8,128)(2,1)S(1)}, u32[]{:S(2)}, u32[]{:S(2)}) %collective-permute-start.2) | collective-permute-done | bytes 393248 | tf_op jit(solution)/shard_map/ppermute | solution.py:268
  16.0 1.6 %collective-permute-start.6 = (bf16[64,2560]{1,0:T(8,128)(2,1)S(1)}, bf16[64,2560]{1,0:T(8,128)(2,1)S(1)}, u32[]{:S(2)}, u32[]{:S(2)}) collective-permute-start(bf16[64,2560]{1,0:T(8,128)(2,1)S(1)} %get-tuple-element.30.refs_0_), channel_id=1, source_target_pairs={{0,2},{2,0},{4,6},{6,4},{8,10},{10,8},{12,14},{14,12},{1,3},{3,1},... | collective-permute-start | bytes 983048 | tf_op jit(solution)/shard_map/ppermute | solution.py:268
  17.5 2.7 %collective-permute-start.4 = (bf16[32,3072]{1,0:T(8,128)(2,1)S(1)}, bf16[32,3072]{1,0:T(8,128)(2,1)S(1)}, u32[]{:S(2)}, u32[]{:S(2)}) collective-permute-start(bf16[32,3072]{1,0:T(8,128)(2,1)S(1)} %get-tuple-element.33), channel_id=1, source_target_pairs={{0,12},{2,14},{4,8},{6,10},{8,4},{10,6},{12,0},{14,2},{1,13},{3,15... | collective-permute-start | bytes 589832 | tf_op jit(solution)/shard_map/ppermute | solution.py:268
  21.3 4.8 %collective-permute-done.1.got = bf16[64,3072]{1,0:T(8,128)(2,1)S(1)} collective-permute-done((bf16[64,3072]{1,0:T(8,128)(2,1)S(1)}, bf16[64,3072]{1,0:T(8,128)(2,1)S(1)}, u32[]{:S(2)}, u32[]{:S(2)}) %collective-permute-start.1) | collective-permute-done | bytes 393248 | tf_op jit(solution)/shard_map/ppermute | solution.py:268
  26.2 1.6 %collective-permute-start.3 = (bf16[64,2560]{1,0:T(8,128)(2,1)S(1)}, bf16[64,2560]{1,0:T(8,128)(2,1)S(1)}, u32[]{:S(2)}, u32[]{:S(2)}) collective-permute-start(bf16[64,2560]{1,0:T(8,128)(2,1)S(1)} %get-tuple-element.32), channel_id=1, source_target_pairs={{0,2},{2,0},{4,6},{6,4},{8,10},{10,8},{12,14},{14,12},{1,3},{3,1},... | collective-permute-start | bytes 983048 | tf_op jit(solution)/shard_map/ppermute | solution.py:268
  27.8 1.5 %image.1 = (bf16[256,1024]{1,0:T(8,128)(2,1)S(1)}, bf16[2,128,512]{2,1,0:T(8,128)(2,1)S(1)}) custom-call(bf16[64,2560]{1,0:T(8,128)(2,1)S(1)} %get-tuple-element.29._.refs_0_, bf16[64,2560]{1,0:T(8,128)(2,1)S(1)} %collective-permute-done.5.refs_1_, bf16[64,2560]{1,0:T(8,128)(2,1)S(1)} %get-tuple-element.35.refs_2_, ...), custom_call_target="tpu_custom_call" | custom-call | flops 1342177280 | bytes 4194304 | tf_op jit(solution)/shard_map/image/pallas_call | solution.py:171
  30.5 1.6 %collective-permute-start.8 = (bf16[32,2560]{1,0:T(8,128)(2,1)S(1)}, bf16[32,2560]{1,0:T(8,128)(2,1)S(1)}, u32[]{:S(2)}, u32[]{:S(2)}) collective-permute-start(bf16[32,2560]{1,0:T(8,128)(2,1)S(1)} %get-tuple-element.40), channel_id=1, source_target_pairs={{0,2},{2,0},{4,6},{6,4},{8,10},{10,8},{12,14},{14,12},{1,3},{3,1},... | collective-permute-start | bytes 491528 | tf_op jit(solution)/shard_map/ppermute | solution.py:268
  32.0 1.8 %collective-permute-done.7.got = bf16[32,3072]{1,0:T(8,128)(2,1)S(1)} collective-permute-done((bf16[32,3072]{1,0:T(8,128)(2,1)S(1)}, bf16[32,3072]{1,0:T(8,128)(2,1)S(1)}, u32[]{:S(2)}, u32[]{:S(2)}) %collective-permute-start.7) | collective-permute-done | bytes 196640 | tf_op jit(solution)/shard_map/ppermute | solution.py:268
  33.9 1.6 %collective-permute-start.9 = (bf16[32,2560]{1,0:T(8,128)(2,1)S(1)}, bf16[32,2560]{1,0:T(8,128)(2,1)S(1)}, u32[]{:S(2)}, u32[]{:S(2)}) collective-permute-start(bf16[32,2560]{1,0:T(8,128)(2,1)S(1)} %get-tuple-element.41), channel_id=1, source_target_pairs={{0,2},{2,0},{4,6},{6,4},{8,10},{10,8},{12,14},{14,12},{1,3},{3,1},... | collective-permute-start | bytes 491528 | tf_op jit(solution)/shard_map/ppermute | solution.py:268
  35.4 1.5 %collective-permute-done.3.refs_1_ = bf16[64,2560]{1,0:T(8,128)(2,1)S(1)} collective-permute-done((bf16[64,2560]{1,0:T(8,128)(2,1)S(1)}, bf16[64,2560]{1,0:T(8,128)(2,1)S(1)}, u32[]{:S(2)}, u32[]{:S(2)}) %collective-permute-start.3) | collective-permute-done | bytes 327712 | tf_op jit(solution)/shard_map/ppermute | solution.py:268
  36.9 3.5 %collective-permute-done.8.refs_4_ = bf16[32,2560]{1,0:T(8,128)(2,1)S(1)} collective-permute-done((bf16[32,2560]{1,0:T(8,128)(2,1)S(1)}, bf16[32,2560]{1,0:T(8,128)(2,1)S(1)}, u32[]{:S(2)}, u32[]{:S(2)}) %collective-permute-start.8) | collective-permute-done | bytes 163872 | tf_op jit(solution)/shard_map/ppermute | solution.py:268
  40.4 2.3 %collective-permute-done.9.refs_5_ = bf16[32,2560]{1,0:T(8,128)(2,1)S(1)} collective-permute-done((bf16[32,2560]{1,0:T(8,128)(2,1)S(1)}, bf16[32,2560]{1,0:T(8,128)(2,1)S(1)}, u32[]{:S(2)}, u32[]{:S(2)}) %collective-permute-start.9) | collective-permute-done | bytes 163872 | tf_op jit(solution)/shard_map/ppermute | solution.py:268
  43.9 1.1 %project.2 = (f32[512,256]{1,0:T(8,128)S(1)}, f32[512,256]{1,0:T(8,128)S(1)}) custom-call(bf16[64,2560]{1,0:T(8,128)(2,1)S(1)} %get-tuple-element.31.refs_0_, bf16[64,2560]{1,0:T(8,128)(2,1)S(1)} %collective-permute-done.3.refs_1_, bf16[32,2560]{1,0:T(8,128)(2,1)S(1)} %get-tuple-element.37.refs_2_, bf16[32,2560]{1,0:T(8,128)(2,1)S(1)} %get-tuple-element.39.refs_3_, ...), custom_call_target="tpu_custom_call" | custom-call | flops 268435456 | bytes 2097152 | tf_op jit(solution)/shard_map/project/pallas_call | solution.py:231
  45.9 1.3 %collective-permute-done.10 = f32[512,256]{1,0:T(8,128)S(1)} collective-permute-done((f32[512,256]{1,0:T(8,128)S(1)}, f32[512,256]{1,0:T(8,128)S(1)}, u32[]{:S(2)}, u32[]{:S(2)}) %collective-permute-start.10) | collective-permute-done | bytes 524320 | tf_op jit(solution)/shard_map/ppermute | solution.py:352
  47.4 3.5 %collective-permute-start.18 = (bf16[2,64,256]{2,1,0:T(8,128)(2,1)S(1)}, bf16[2,64,256]{2,1,0:T(8,128)(2,1)S(1)}, u32[]{:S(2)}, u32[]{:S(2)}) collective-permute-start(bf16[2,64,256]{2,1,0:T(8,128)(2,1)S(1)} %get-tuple-element.48), channel_id=1, source_target_pairs={{0,14},{2,12},{4,10},{6,8},{8,6},{10,4},{12,2},{14,0},{1,15},{3,13... | collective-permute-start | bytes 196616 | tf_op jit(solution)/shard_map/ppermute | solution.py:268
  50.8 1.4 %collective-permute-start.17 = (bf16[2,64,256]{2,1,0:T(8,128)(2,1)S(1)}, bf16[2,64,256]{2,1,0:T(8,128)(2,1)S(1)}, u32[]{:S(2)}, u32[]{:S(2)}) collective-permute-start(bf16[2,64,256]{2,1,0:T(8,128)(2,1)S(1)} %get-tuple-element.49), channel_id=1, source_target_pairs={{0,12},{2,14},{4,8},{6,10},{8,4},{10,6},{12,0},{14,2},{1,13},{3,15... | collective-permute-start | bytes 196616 | tf_op jit(solution)/shard_map/ppermute | solution.py:268
  52.2 5.4 %collective-permute-start.16 = (bf16[2,64,256]{2,1,0:T(8,128)(2,1)S(1)}, bf16[2,64,256]{2,1,0:T(8,128)(2,1)S(1)}, u32[]{:S(2)}, u32[]{:S(2)}) collective-permute-start(bf16[2,64,256]{2,1,0:T(8,128)(2,1)S(1)} %get-tuple-element.50), channel_id=1, source_target_pairs={{0,10},{2,8},{4,2},{6,0},{8,14},{10,12},{12,6},{14,4},{1,11},{3,9}... | collective-permute-start | bytes 196616 | tf_op jit(solution)/shard_map/ppermute | solution.py:268
  57.6 2.9 %collective-permute-start.14 = (bf16[2,64,256]{2,1,0:T(8,128)(2,1)S(1)}, bf16[2,64,256]{2,1,0:T(8,128)(2,1)S(1)}, u32[]{:S(2)}, u32[]{:S(2)}) collective-permute-start(bf16[2,64,256]{2,1,0:T(8,128)(2,1)S(1)} %get-tuple-element.52), channel_id=1, source_target_pairs={{0,6},{2,4},{4,14},{6,12},{8,2},{10,0},{12,10},{14,8},{1,7},{3,5},... | collective-permute-start | bytes 196616 | tf_op jit(solution)/shard_map/ppermute | solution.py:268
  61.9 3.2 %collective-permute-done.14 = bf16[2,64,256]{2,1,0:T(8,128)(2,1)S(1)} collective-permute-done((bf16[2,64,256]{2,1,0:T(8,128)(2,1)S(1)}, bf16[2,64,256]{2,1,0:T(8,128)(2,1)S(1)}, u32[]{:S(2)}, u32[]{:S(2)}) %collective-permute-start.14) | collective-permute-done | bytes 65568 | tf_op jit(solution)/shard_map/ppermute | solution.py:268
  (37 shorter events, 8.4 us)
Async XLA Ops:
  0.0 7.9 %copy-start = (bf16[1,4,16,128,128]{4,3,2,1,0:T(8,128)(2,1)S(1)}, bf16[1,4,16,128,128]{4,3,2,1,0:T(8,128)(2,1)}, u32[]{:S(2)}) copy-start(bf16[1,4,16,128,128]{4,3,2,1,0:T(8,128)(2,1)} %gyro.1) | copy-start | bytes 6291460
  0.0 2.2 %collective-permute-start = (bf16[64,4096]{1,0:T(8,128)(2,1)}, bf16[64,4096]{1,0:T(8,128)(2,1)S(1)}, u32[]{:S(2)}, u32[]{:S(2)}) collective-permute-start(bf16[64,4096]{1,0:T(8,128)(2,1)} %bitcast.12), channel_id=1, source_target_pairs={{0,1},{1,0},{2,3},{3,2},{4,5},{5,4},{6,7},{7,6},{8,9},{9,8},{10,11... | collective-permute-start | bytes 1572872 | tf_op jit(solution)/shard_map/ppermute | solution.py:287
  0.5 1.2 %copy-start.2 = (bf16[4096,64]{0,1:T(8,128)(2,1)S(1)}, bf16[4096,64]{0,1:T(8,128)(2,1)}, u32[]{:S(2)}) copy-start(bf16[4096,64]{0,1:T(8,128)(2,1)} %param.4) | copy-start | bytes 1572868
  1.7 6.2 %copy-start.3 = (s32[1,4,16]{2,1,0:T(4,128)S(1)}, s32[1,4,16]{2,1,0:T(4,128)}, u32[]{:S(2)}) copy-start(s32[1,4,16]{2,1,0:T(4,128)} %pattern.1) | copy-start | bytes 772
  2.4 13.5 %collective-permute-start.2 = (bf16[64,3072]{1,0:T(8,128)(2,1)S(1)}, bf16[64,3072]{1,0:T(8,128)(2,1)S(1)}, u32[]{:S(2)}, u32[]{:S(2)}) collective-permute-start(bf16[64,3072]{1,0:T(8,128)(2,1)S(1)} %get-tuple-element.27), channel_id=1, source_target_pairs={{0,8},{2,10},{4,0},{6,2},{8,12},{10,14},{12,4},{14,6},{1,9},{3,11}... | collective-permute-start | bytes 1179656 | tf_op jit(solution)/shard_map/ppermute | solution.py:268
  6.4 19.8 %collective-permute-start.1 = (bf16[64,3072]{1,0:T(8,128)(2,1)S(1)}, bf16[64,3072]{1,0:T(8,128)(2,1)S(1)}, u32[]{:S(2)}, u32[]{:S(2)}) collective-permute-start(bf16[64,3072]{1,0:T(8,128)(2,1)S(1)} %get-tuple-element.26), channel_id=1, source_target_pairs={{0,4},{2,6},{4,12},{6,14},{8,0},{10,2},{12,8},{14,10},{1,5},{3,7},... | collective-permute-start | bytes 1179656 | tf_op jit(solution)/shard_map/ppermute | solution.py:268
  6.4 21.4 %collective-permute-start.5 = (bf16[64,2560]{1,0:T(8,128)(2,1)S(1)}, bf16[64,2560]{1,0:T(8,128)(2,1)S(1)}, u32[]{:S(2)}, u32[]{:S(2)}) collective-permute-start(bf16[64,2560]{1,0:T(8,128)(2,1)S(1)} %get-tuple-element.34), channel_id=1, source_target_pairs={{0,2},{2,0},{4,6},{6,4},{8,10},{10,8},{12,14},{14,12},{1,3},{3,1},... | collective-permute-start | bytes 983048 | tf_op jit(solution)/shard_map/ppermute | solution.py:268
  7.9 1.6 %copy-start.1 = (bf16[1,4,16,128,128]{4,3,2,1,0:T(8,128)(2,1)S(1)}, bf16[1,4,16,128,128]{4,3,2,1,0:T(8,128)(2,1)}, u32[]{:S(2)}) copy-start(bf16[1,4,16,128,128]{4,3,2,1,0:T(8,128)(2,1)} %spin.1) | copy-start | bytes 6291460
  16.0 11.8 %collective-permute-start.6 = (bf16[64,2560]{1,0:T(8,128)(2,1)S(1)}, bf16[64,2560]{1,0:T(8,128)(2,1)S(1)}, u32[]{:S(2)}, u32[]{:S(2)}) collective-permute-start(bf16[64,2560]{1,0:T(8,128)(2,1)S(1)} %get-tuple-element.30.refs_0_), channel_id=1, source_target_pairs={{0,2},{2,0},{4,6},{6,4},{8,10},{10,8},{12,14},{14,12},{1,3},{3,1},... | collective-permute-start | bytes 983048 | tf_op jit(solution)/shard_map/ppermute | solution.py:268
  17.5 12.9 %collective-permute-start.4 = (bf16[32,3072]{1,0:T(8,128)(2,1)S(1)}, bf16[32,3072]{1,0:T(8,128)(2,1)S(1)}, u32[]{:S(2)}, u32[]{:S(2)}) collective-permute-start(bf16[32,3072]{1,0:T(8,128)(2,1)S(1)} %get-tuple-element.33), channel_id=1, source_target_pairs={{0,12},{2,14},{4,8},{6,10},{8,4},{10,6},{12,0},{14,2},{1,13},{3,15... | collective-permute-start | bytes 589832 | tf_op jit(solution)/shard_map/ppermute | solution.py:268
  20.3 13.6 %collective-permute-start.7 = (bf16[32,3072]{1,0:T(8,128)(2,1)S(1)}, bf16[32,3072]{1,0:T(8,128)(2,1)S(1)}, u32[]{:S(2)}, u32[]{:S(2)}) collective-permute-start(bf16[32,3072]{1,0:T(8,128)(2,1)S(1)} %get-tuple-element.38), channel_id=1, source_target_pairs={{0,12},{2,14},{4,8},{6,10},{8,4},{10,6},{12,0},{14,2},{1,13},{3,15... | collective-permute-start | bytes 589832 | tf_op jit(solution)/shard_map/ppermute | solution.py:268
  26.2 10.7 %collective-permute-start.3 = (bf16[64,2560]{1,0:T(8,128)(2,1)S(1)}, bf16[64,2560]{1,0:T(8,128)(2,1)S(1)}, u32[]{:S(2)}, u32[]{:S(2)}) collective-permute-start(bf16[64,2560]{1,0:T(8,128)(2,1)S(1)} %get-tuple-element.32), channel_id=1, source_target_pairs={{0,2},{2,0},{4,6},{6,4},{8,10},{10,8},{12,14},{14,12},{1,3},{3,1},... | collective-permute-start | bytes 983048 | tf_op jit(solution)/shard_map/ppermute | solution.py:268
  30.5 10.0 %collective-permute-start.8 = (bf16[32,2560]{1,0:T(8,128)(2,1)S(1)}, bf16[32,2560]{1,0:T(8,128)(2,1)S(1)}, u32[]{:S(2)}, u32[]{:S(2)}) collective-permute-start(bf16[32,2560]{1,0:T(8,128)(2,1)S(1)} %get-tuple-element.40), channel_id=1, source_target_pairs={{0,2},{2,0},{4,6},{6,4},{8,10},{10,8},{12,14},{14,12},{1,3},{3,1},... | collective-permute-start | bytes 491528 | tf_op jit(solution)/shard_map/ppermute | solution.py:268
  33.9 8.8 %collective-permute-start.9 = (bf16[32,2560]{1,0:T(8,128)(2,1)S(1)}, bf16[32,2560]{1,0:T(8,128)(2,1)S(1)}, u32[]{:S(2)}, u32[]{:S(2)}) collective-permute-start(bf16[32,2560]{1,0:T(8,128)(2,1)S(1)} %get-tuple-element.41), channel_id=1, source_target_pairs={{0,2},{2,0},{4,6},{6,4},{8,10},{10,8},{12,14},{14,12},{1,3},{3,1},... | collective-permute-start | bytes 491528 | tf_op jit(solution)/shard_map/ppermute | solution.py:268
  43.8 2.0 %collective-permute-start.11 = (f32[512,256]{1,0:T(8,128)S(1)}, f32[512,256]{1,0:T(8,128)S(1)}, u32[]{:S(2)}, u32[]{:S(2)}) collective-permute-start(f32[512,256]{1,0:T(8,128)S(1)} %get-tuple-element.46), channel_id=1, source_target_pairs={{0,1},{1,0},{2,3},{3,2},{4,5},{5,4},{6,7},{7,6},{8,9},{9,8},{10,11... | collective-permute-start | bytes 1572872 | tf_op jit(solution)/shard_map/ppermute | solution.py:352
  45.1 2.1 %collective-permute-start.10 = (f32[512,256]{1,0:T(8,128)S(1)}, f32[512,256]{1,0:T(8,128)S(1)}, u32[]{:S(2)}, u32[]{:S(2)}) collective-permute-start(f32[512,256]{1,0:T(8,128)S(1)} %get-tuple-element.44), channel_id=1, source_target_pairs={{0,1},{1,0},{2,3},{3,2},{4,5},{5,4},{6,7},{7,6},{8,9},{9,8},{10,11... | collective-permute-start | bytes 1572872 | tf_op jit(solution)/shard_map/ppermute | solution.py:352
  47.4 13.2 %collective-permute-start.18 = (bf16[2,64,256]{2,1,0:T(8,128)(2,1)S(1)}, bf16[2,64,256]{2,1,0:T(8,128)(2,1)S(1)}, u32[]{:S(2)}, u32[]{:S(2)}) collective-permute-start(bf16[2,64,256]{2,1,0:T(8,128)(2,1)S(1)} %get-tuple-element.48), channel_id=1, source_target_pairs={{0,14},{2,12},{4,10},{6,8},{8,6},{10,4},{12,2},{14,0},{1,15},{3,13... | collective-permute-start | bytes 196616 | tf_op jit(solution)/shard_map/ppermute | solution.py:268
  50.8 9.7 %collective-permute-start.17 = (bf16[2,64,256]{2,1,0:T(8,128)(2,1)S(1)}, bf16[2,64,256]{2,1,0:T(8,128)(2,1)S(1)}, u32[]{:S(2)}, u32[]{:S(2)}) collective-permute-start(bf16[2,64,256]{2,1,0:T(8,128)(2,1)S(1)} %get-tuple-element.49), channel_id=1, source_target_pairs={{0,12},{2,14},{4,8},{6,10},{8,4},{10,6},{12,0},{14,2},{1,13},{3,15... | collective-permute-start | bytes 196616 | tf_op jit(solution)/shard_map/ppermute | solution.py:268
  52.2 9.0 %collective-permute-start.16 = (bf16[2,64,256]{2,1,0:T(8,128)(2,1)S(1)}, bf16[2,64,256]{2,1,0:T(8,128)(2,1)S(1)}, u32[]{:S(2)}, u32[]{:S(2)}) collective-permute-start(bf16[2,64,256]{2,1,0:T(8,128)(2,1)S(1)} %get-tuple-element.50), channel_id=1, source_target_pairs={{0,10},{2,8},{4,2},{6,0},{8,14},{10,12},{12,6},{14,4},{1,11},{3,9}... | collective-permute-start | bytes 196616 | tf_op jit(solution)/shard_map/ppermute | solution.py:268
  57.6 4.3 %collective-permute-start.15 = (bf16[2,64,256]{2,1,0:T(8,128)(2,1)S(1)}, bf16[2,64,256]{2,1,0:T(8,128)(2,1)S(1)}, u32[]{:S(2)}, u32[]{:S(2)}) collective-permute-start(bf16[2,64,256]{2,1,0:T(8,128)(2,1)S(1)} %get-tuple-element.51), channel_id=1, source_target_pairs={{0,8},{2,10},{4,0},{6,2},{8,12},{10,14},{12,4},{14,6},{1,9},{3,11}... | collective-permute-start | bytes 196616 | tf_op jit(solution)/shard_map/ppermute | solution.py:268
  57.6 7.5 %collective-permute-start.14 = (bf16[2,64,256]{2,1,0:T(8,128)(2,1)S(1)}, bf16[2,64,256]{2,1,0:T(8,128)(2,1)S(1)}, u32[]{:S(2)}, u32[]{:S(2)}) collective-permute-start(bf16[2,64,256]{2,1,0:T(8,128)(2,1)S(1)} %get-tuple-element.52), channel_id=1, source_target_pairs={{0,6},{2,4},{4,14},{6,12},{8,2},{10,0},{12,10},{14,8},{1,7},{3,5},... | collective-permute-start | bytes 196616 | tf_op jit(solution)/shard_map/ppermute | solution.py:268
  60.5 5.2 %collective-permute-start.13 = (bf16[2,64,256]{2,1,0:T(8,128)(2,1)S(1)}, bf16[2,64,256]{2,1,0:T(8,128)(2,1)S(1)}, u32[]{:S(2)}, u32[]{:S(2)}) collective-permute-start(bf16[2,64,256]{2,1,0:T(8,128)(2,1)S(1)} %get-tuple-element.53), channel_id=1, source_target_pairs={{0,4},{2,6},{4,12},{6,14},{8,0},{10,2},{12,8},{14,10},{1,5},{3,7},... | collective-permute-start | bytes 196616 | tf_op jit(solution)/shard_map/ppermute | solution.py:268
  60.5 5.2 %collective-permute-start.12 = (bf16[2,64,256]{2,1,0:T(8,128)(2,1)S(1)}, bf16[2,64,256]{2,1,0:T(8,128)(2,1)S(1)}, u32[]{:S(2)}, u32[]{:S(2)}) collective-permute-start(bf16[2,64,256]{2,1,0:T(8,128)(2,1)S(1)} %get-tuple-element.47), channel_id=1, source_target_pairs={{0,2},{2,0},{4,6},{6,4},{8,10},{10,8},{12,14},{14,12},{1,3},{3,1},... | collective-permute-start | bytes 196616 | tf_op jit(solution)/shard_map/ppermute | solution.py:268

commit v6 on v5

--- a/solution.py
+++ b/solution.py
@@ -10,7 +10,7 @@
 
 HB = 8
 X = 2
-PIECES = (32, 32)
+PIECES = (32, 16, 16)
 VMEM_LIMIT = 24 * 1024 * 1024
 NT = (((1,), (1,)), ((), ()))
 VMEM = pl.BlockSpec(memory_space=pltpu.VMEM)
@@ -76,6 +76,26 @@
     out[...] = source[:, pl.ds(aligned(start, group), out.shape[1])]
 
 
+def plain_start(z):
+    return jnp.where(z < 2, 2 * z, 2 * z - 2)
+
+
+def plain_kernel(group, phi, out):
+    _, z, _ = place_in_mode()
+    pltpu.sync_copy(phi.at[:, pl.ds(aligned(plain_start(ahead(z)), group), out.shape[1])], out)
+
+
+def cut_plain(phi, group):
+    return pl.pallas_call(
+        functools.partial(plain_kernel, group),
+        out_shape=jax.ShapeDtypeStruct((phi.shape[0], 4 * group), phi.dtype),
+        in_specs=[ANY],
+        out_specs=VMEM,
+        compiler_params=params(),
+        name="plain",
+    )(phi)
+
+
 def stage_kernel(phi, out):
     pltpu.sync_copy(phi, out)
 
@@ -96,7 +116,8 @@
     ext[:, :rim] = below[:, below.shape[1] - rim :]
     ext[:, rim : rim + phi.shape[1]] = phi[...]
     ext[:, rim + phi.shape[1] :] = above[:, :rim]
-    cut(group, to_ahead, ext, 2 * ahead(z))
+    target = ahead(z)
+    cut(group, to_ahead, ext, jnp.where(target < 2, 2 * target, 2 * target + 4))
     cut(group, to_behind, ext, 2 * behind(z))
     cut(group, cross, ext, m + 1 - 2 * lax.rem(m, 2))
     cut(group, own, ext, m)
@@ -109,11 +130,22 @@
     cut(group, own, got, x)
 
 
-def onward_kernel(group, got, ext, *refs):
+def onward_kernel(group, plain, rim, ext, *refs):
     cross, own, *far = refs[-2 - len(PIECES) :]
     _, z, x = place_in_mode()
-    cut(group, cross, got, 1 - x)
-    cut(group, own, got, x)
+
+    def part(out, first):
+        for lower, order in ((True, (rim, plain)), (False, (plain, rim))):
+            for shift in range(2):
+
+                @pl.when(((z < 2) == lower) & (first == shift))
+                def _():
+                    split = order[0].shape[1] - shift * group
+                    out[:, :split] = order[0][:, shift * group :]
+                    out[:, split:] = order[1][:, : out.shape[1] - split]
+
+    part(cross, 1 - x)
+    part(own, x)
     at = 0
     for out in far:
         rows, span = out.shape
@@ -282,6 +314,7 @@
     phi = modes.T
     forward, backward = ring(unit_count)
     rim = HB * block_size
+    plainA = move(cut_plain(phi, group), (to_ahead, 0))
     units = ("dof", "sub")
     if unit_count == 2:
         below = above = lax.ppermute(phi, units, forward)
@@ -292,7 +325,7 @@
     w5, w6 = 5 * group, 6 * group
     ext, ahead_w, behind_w, cross0_w, own0 = cutting(
         functools.partial(first_kernel, group, rim),
-        [(width, w) for w in (phi.shape[1] + 2 * rim, w6, w6, w5, w5)],
+        [(width, w) for w in (phi.shape[1] + 2 * rim, 2 * group, w6, w5, w5)],
         "first",
         stage(phi),
         below,
@@ -307,6 +340,7 @@
         functools.partial(onward_kernel, group),
         [(width, w5), (width, w5)] + [(rows, w6) for rows in PIECES],
         "onward",
+        plainA,
         gotA,
         ext,
         after=(band,),

time: 66.6 us -> 65.1 us (0.977)
  waiting for transfers between devices: 25.9 us -> 21.1 us
  starting transfers between devices: 30.4 us -> 33.8 us
    ppermute x16 -> x19, waiting for transfers between devices: 24 us -> 19.6 us  [move(): return lax.ppermute(array, 'mode', pairs)]
    ppermute x16 -> x19, starting transfers between devices: 29.3 us -> 32.8 us  [move(): return lax.ppermute(array, 'mode', pairs)]
  transfers between devices with their start and end apart: 19 -> 22, of which waited for: 13 -> 11; matrix products, arithmetic and copies ran while one was open for 0% -> 0% of each run, Pallas kernels for 7% -> 8%
where the time goes in v6:
time: 65.1 us; the launch traced here: 64.9 us
  starting transfers between devices  33.8 us (52%)
  waiting for transfers between devices  21.1 us (32%)
  Pallas kernels  6.26 us (10%)
  local copies, waits for them, and re-layouts  2.67 us (4%)
  other arithmetic  0.92 us (1%)
    ppermute x19, starting transfers between devices, move(): return lax.ppermute(array, 'mode', pairs)  32.8 us
    ppermute x19, waiting for transfers between devices, move(): return lax.ppermute(array, 'mode', pairs)  19.6 us
    unnamed x8, local copies, waits for them, and re-layouts  2.64 us
    pallas_call x2, Pallas kernels, make_projection(): pl.pallas_call(functools.partial(project_kernel, matrix, layout, slice(2...  2.29 us
    pallas_call x1, Pallas kernels, make_band(): pl.pallas_call(functools.partial(band_kernel, per_unit, block_total), out...  2.03 us
    pallas_call x1, Pallas kernels, make_image(): pl.pallas_call(functools.partial(image_kernel, layout, slice(2 * group, 3...  1.55 us
    ppermute x2, waiting for transfers between devices, body(): sums.append(keep + lax.ppermute(send, 'sub', [(0, 1), (1, 0)]))  1.47 us
  transfers between devices with their start and end apart: 22, of which 11 were waited for; matrix products, arithmetic and copies ran while one was open for 0% of the time, Pallas kernels for 8%

profile of v6, /device:TPU:0, one launch (start us, length us, event | category | flops | bytes accessed | tf_op | source)
XLA Modules:
  0.0 64.9 jit_solution(17842641314443750892)
XLA Ops:
  0.5 1.0 %copy-done = bf16[4096,64]{0,1:T(8,128)(2,1)S(1)} copy-done((bf16[4096,64]{0,1:T(8,128)(2,1)S(1)}, bf16[4096,64]{0,1:T(8,128)(2,1)}, u32[]{:S(2)}) %copy-start) | copy-done | bytes 524312
  1.5 3.6 %collective-permute-start.2 = (bf16[64,2048]{1,0:T(8,128)(2,1)S(1)}, bf16[64,2048]{1,0:T(8,128)(2,1)S(1)}, u32[]{:S(2)}, u32[]{:S(2)}) collective-permute-start(bf16[64,2048]{1,0:T(8,128)(2,1)S(1)} %plain.1), channel_id=1, source_target_pairs={{0,8},{2,10},{4,0},{6,2},{8,12},{10,14},{12,4},{14,6},{1,9},{3,11}... | collective-permute-start | bytes 786440 | tf_op jit(solution)/shard_map/ppermute | solution.py:300
  5.4 1.6 %collective-permute-start.3 = (bf16[64,1024]{1,0:T(8,128)(2,1)S(1)}, bf16[64,1024]{1,0:T(8,128)(2,1)S(1)}, u32[]{:S(2)}, u32[]{:S(2)}) collective-permute-start(bf16[64,1024]{1,0:T(8,128)(2,1)S(1)} %get-tuple-element.30), channel_id=1, source_target_pairs={{0,8},{2,10},{4,0},{6,2},{8,12},{10,14},{12,4},{14,6},{1,9},{3,11}... | collective-permute-start | bytes 393224 | tf_op jit(solution)/shard_map/ppermute | solution.py:300
  7.4 1.5 %collective-permute-start.6 = (bf16[64,2560]{1,0:T(8,128)(2,1)S(1)}, bf16[64,2560]{1,0:T(8,128)(2,1)S(1)}, u32[]{:S(2)}, u32[]{:S(2)}) collective-permute-start(bf16[64,2560]{1,0:T(8,128)(2,1)S(1)} %get-tuple-element.37), channel_id=1, source_target_pairs={{0,2},{2,0},{4,6},{6,4},{8,10},{10,8},{12,14},{14,12},{1,3},{3,1},... | collective-permute-start | bytes 983048 | tf_op jit(solution)/shard_map/ppermute | solution.py:300
  8.9 1.6 %copy-done.2 = bf16[1,4,16,128,128]{4,3,2,1,0:T(8,128)(2,1)S(1)} copy-done((bf16[1,4,16,128,128]{4,3,2,1,0:T(8,128)(2,1)S(1)}, bf16[1,4,16,128,128]{4,3,2,1,0:T(8,128)(2,1)}, u32[]{:S(2)}) %copy-start.2) | copy-done | bytes 2097176
  10.5 2.0 %band.1 = bf16[2,4,128,2560]{3,2,1,0:T(8,128)(2,1)S(1)} custom-call(s32[1,4,16]{2,1,0:T(4,128)S(1)} %copy-done.3, bf16[1,4,16,128,128]{4,3,2,1,0:T(8,128)(2,1)S(1)} %copy-done.1, bf16[1,4,16,128,128]{4,3,2,1,0:T(8,128)(2,1)S(1)} %copy-done.2, bf16[64,2560]{1,0:T(8,128)(2,1)S(1)} %get-tuple-element.32._.refs_0_), custom_call_target="tpu_custom_call" | custom-call | bytes 8388608 | tf_op jit(solution)/shard_map/band/pallas_call | solution.py:62
  12.6 2.1 %collective-permute-done.3.rim = bf16[64,1024]{1,0:T(8,128)(2,1)S(1)} collective-permute-done((bf16[64,1024]{1,0:T(8,128)(2,1)S(1)}, bf16[64,1024]{1,0:T(8,128)(2,1)S(1)}, u32[]{:S(2)}, u32[]{:S(2)}) %collective-permute-start.3) | collective-permute-done | bytes 131104 | tf_op jit(solution)/shard_map/ppermute | solution.py:300
  14.7 1.6 %collective-permute-start.7 = (bf16[64,2560]{1,0:T(8,128)(2,1)S(1)}, bf16[64,2560]{1,0:T(8,128)(2,1)S(1)}, u32[]{:S(2)}, u32[]{:S(2)}) collective-permute-start(bf16[64,2560]{1,0:T(8,128)(2,1)S(1)} %get-tuple-element.33.refs_0_), channel_id=1, source_target_pairs={{0,2},{2,0},{4,6},{6,4},{8,10},{10,8},{12,14},{14,12},{1,3},{3,1},... | collective-permute-start | bytes 983048 | tf_op jit(solution)/shard_map/ppermute | solution.py:300
  16.3 3.2 %collective-permute-start.5 = (bf16[32,3072]{1,0:T(8,128)(2,1)S(1)}, bf16[32,3072]{1,0:T(8,128)(2,1)S(1)}, u32[]{:S(2)}, u32[]{:S(2)}) collective-permute-start(bf16[32,3072]{1,0:T(8,128)(2,1)S(1)} %get-tuple-element.36), channel_id=1, source_target_pairs={{0,12},{2,14},{4,8},{6,10},{8,4},{10,6},{12,0},{14,2},{1,13},{3,15... | collective-permute-start | bytes 589832 | tf_op jit(solution)/shard_map/ppermute | solution.py:300
  19.5 5.5 %collective-permute-done.1.got = bf16[64,3072]{1,0:T(8,128)(2,1)S(1)} collective-permute-done((bf16[64,3072]{1,0:T(8,128)(2,1)S(1)}, bf16[64,3072]{1,0:T(8,128)(2,1)S(1)}, u32[]{:S(2)}, u32[]{:S(2)}) %collective-permute-start.1) | collective-permute-done | bytes 393248 | tf_op jit(solution)/shard_map/ppermute | solution.py:300
  25.0 1.6 %collective-permute-start.4 = (bf16[64,2560]{1,0:T(8,128)(2,1)S(1)}, bf16[64,2560]{1,0:T(8,128)(2,1)S(1)}, u32[]{:S(2)}, u32[]{:S(2)}) collective-permute-start(bf16[64,2560]{1,0:T(8,128)(2,1)S(1)} %get-tuple-element.35), channel_id=1, source_target_pairs={{0,2},{2,0},{4,6},{6,4},{8,10},{10,8},{12,14},{14,12},{1,3},{3,1},... | collective-permute-start | bytes 983048 | tf_op jit(solution)/shard_map/ppermute | solution.py:300
  26.5 2.5 %collective-permute-start.8 = (bf16[16,3072]{1,0:T(8,128)(2,1)S(1)}, bf16[16,3072]{1,0:T(8,128)(2,1)S(1)}, u32[]{:S(2)}, u32[]{:S(2)}) collective-permute-start(bf16[16,3072]{1,0:T(8,128)(2,1)S(1)} %get-tuple-element.41), channel_id=1, source_target_pairs={{0,12},{2,14},{4,8},{6,10},{8,4},{10,6},{12,0},{14,2},{1,13},{3,15... | collective-permute-start | bytes 294920 | tf_op jit(solution)/shard_map/ppermute | solution.py:300
  29.0 1.3 %collective-permute-start.9 = (bf16[16,3072]{1,0:T(8,128)(2,1)S(1)}, bf16[16,3072]{1,0:T(8,128)(2,1)S(1)}, u32[]{:S(2)}, u32[]{:S(2)}) collective-permute-start(bf16[16,3072]{1,0:T(8,128)(2,1)S(1)} %get-tuple-element.43), channel_id=1, source_target_pairs={{0,12},{2,14},{4,8},{6,10},{8,4},{10,6},{12,0},{14,2},{1,13},{3,15... | collective-permute-start | bytes 294920 | tf_op jit(solution)/shard_map/ppermute | solution.py:300
  30.4 1.5 %image.1 = (bf16[256,1024]{1,0:T(8,128)(2,1)S(1)}, bf16[2,128,512]{2,1,0:T(8,128)(2,1)S(1)}) custom-call(bf16[64,2560]{1,0:T(8,128)(2,1)S(1)} %get-tuple-element.32._.refs_0_, bf16[64,2560]{1,0:T(8,128)(2,1)S(1)} %collective-permute-done.6.refs_1_, bf16[64,2560]{1,0:T(8,128)(2,1)S(1)} %get-tuple-element.38.refs_2_, ...), custom_call_target="tpu_custom_call" | custom-call | flops 1342177280 | bytes 4194304 | tf_op jit(solution)/shard_map/image/pallas_call | solution.py:203
  34.1 1.3 %collective-permute-done.9.got = bf16[16,3072]{1,0:T(8,128)(2,1)S(1)} collective-permute-done((bf16[16,3072]{1,0:T(8,128)(2,1)S(1)}, bf16[16,3072]{1,0:T(8,128)(2,1)S(1)}, u32[]{:S(2)}, u32[]{:S(2)}) %collective-permute-start.9) | collective-permute-done | bytes 98336 | tf_op jit(solution)/shard_map/ppermute | solution.py:300
  36.1 4.5 %collective-permute-done.11.refs_6_ = bf16[16,2560]{1,0:T(8,128)(2,1)S(1)} collective-permute-done((bf16[16,2560]{1,0:T(8,128)(2,1)S(1)}, bf16[16,2560]{1,0:T(8,128)(2,1)S(1)}, u32[]{:S(2)}, u32[]{:S(2)}) %collective-permute-start.11) | collective-permute-done | bytes 81952 | tf_op jit(solution)/shard_map/ppermute | solution.py:300
  41.5 1.1 %project.3 = (f32[512,256]{1,0:T(8,128)S(1)}, f32[512,256]{1,0:T(8,128)S(1)}) custom-call(bf16[64,2560]{1,0:T(8,128)(2,1)S(1)} %get-tuple-element.34.refs_0_, bf16[64,2560]{1,0:T(8,128)(2,1)S(1)} %collective-permute-done.4.refs_1_, bf16[32,2560]{1,0:T(8,128)(2,1)S(1)} %get-tuple-element.40.refs_2_, bf16[16,2560]{1,0:T(8,128)(2,1)S(1)} %get-tuple-element.42.refs_3_, ...), custom_call_target="tpu_custom_call" | custom-call | flops 268435456 | bytes 2097152 | tf_op jit(solution)/shard_map/project/pallas_call | solution.py:263
  42.7 1.1 %project.2 = (f32[512,256]{1,0:T(8,128)S(1)}, f32[512,256]{1,0:T(8,128)S(1)}) custom-call(bf16[64,2560]{1,0:T(8,128)(2,1)S(1)} %get-tuple-element.34.refs_0_, bf16[64,2560]{1,0:T(8,128)(2,1)S(1)} %collective-permute-done.4.refs_1_, bf16[32,2560]{1,0:T(8,128)(2,1)S(1)} %get-tuple-element.40.refs_2_, bf16[16,2560]{1,0:T(8,128)(2,1)S(1)} %get-tuple-element.42.refs_3_, ...), custom_call_target="tpu_custom_call" | custom-call | flops 268435456 | bytes 2097152 | tf_op jit(solution)/shard_map/project/pallas_call | solution.py:263
  44.7 1.3 %collective-permute-done.13 = f32[512,256]{1,0:T(8,128)S(1)} collective-permute-done((f32[512,256]{1,0:T(8,128)S(1)}, f32[512,256]{1,0:T(8,128)S(1)}, u32[]{:S(2)}, u32[]{:S(2)}) %collective-permute-start.13) | collective-permute-done | bytes 524320 | tf_op jit(solution)/shard_map/ppermute | solution.py:386
  46.1 3.5 %collective-permute-start.21 = (bf16[2,64,256]{2,1,0:T(8,128)(2,1)S(1)}, bf16[2,64,256]{2,1,0:T(8,128)(2,1)S(1)}, u32[]{:S(2)}, u32[]{:S(2)}) collective-permute-start(bf16[2,64,256]{2,1,0:T(8,128)(2,1)S(1)} %get-tuple-element.54), channel_id=1, source_target_pairs={{0,14},{2,12},{4,10},{6,8},{8,6},{10,4},{12,2},{14,0},{1,15},{3,13... | collective-permute-start | bytes 196616 | tf_op jit(solution)/shard_map/ppermute | solution.py:300
  49.6 1.4 %collective-permute-start.20 = (bf16[2,64,256]{2,1,0:T(8,128)(2,1)S(1)}, bf16[2,64,256]{2,1,0:T(8,128)(2,1)S(1)}, u32[]{:S(2)}, u32[]{:S(2)}) collective-permute-start(bf16[2,64,256]{2,1,0:T(8,128)(2,1)S(1)} %get-tuple-element.55), channel_id=1, source_target_pairs={{0,12},{2,14},{4,8},{6,10},{8,4},{10,6},{12,0},{14,2},{1,13},{3,15... | collective-permute-start | bytes 196616 | tf_op jit(solution)/shard_map/ppermute | solution.py:300
  50.9 5.1 %collective-permute-start.19 = (bf16[2,64,256]{2,1,0:T(8,128)(2,1)S(1)}, bf16[2,64,256]{2,1,0:T(8,128)(2,1)S(1)}, u32[]{:S(2)}, u32[]{:S(2)}) collective-permute-start(bf16[2,64,256]{2,1,0:T(8,128)(2,1)S(1)} %get-tuple-element.56), channel_id=1, source_target_pairs={{0,10},{2,8},{4,2},{6,0},{8,14},{10,12},{12,6},{14,4},{1,11},{3,9}... | collective-permute-start | bytes 196616 | tf_op jit(solution)/shard_map/ppermute | solution.py:300
  56.1 2.9 %collective-permute-start.17 = (bf16[2,64,256]{2,1,0:T(8,128)(2,1)S(1)}, bf16[2,64,256]{2,1,0:T(8,128)(2,1)S(1)}, u32[]{:S(2)}, u32[]{:S(2)}) collective-permute-start(bf16[2,64,256]{2,1,0:T(8,128)(2,1)S(1)} %get-tuple-element.58), channel_id=1, source_target_pairs={{0,6},{2,4},{4,14},{6,12},{8,2},{10,0},{12,10},{14,8},{1,7},{3,5},... | collective-permute-start | bytes 196616 | tf_op jit(solution)/shard_map/ppermute | solution.py:300
  60.3 3.2 %collective-permute-done.17 = bf16[2,64,256]{2,1,0:T(8,128)(2,1)S(1)} collective-permute-done((bf16[2,64,256]{2,1,0:T(8,128)(2,1)S(1)}, bf16[2,64,256]{2,1,0:T(8,128)(2,1)S(1)}, u32[]{:S(2)}, u32[]{:S(2)}) %collective-permute-start.17) | collective-permute-done | bytes 65568 | tf_op jit(solution)/shard_map/ppermute | solution.py:300
  (45 shorter events, 8.7 us)
Async XLA Ops:
  0.0 5.2 %collective-permute-start = (bf16[64,4096]{1,0:T(8,128)(2,1)}, bf16[64,4096]{1,0:T(8,128)(2,1)S(1)}, u32[]{:S(2)}, u32[]{:S(2)}) collective-permute-start(bf16[64,4096]{1,0:T(8,128)(2,1)} %bitcast.12), channel_id=1, source_target_pairs={{0,1},{1,0},{2,3},{3,2},{4,5},{5,4},{6,7},{7,6},{8,9},{9,8},{10,11... | collective-permute-start | bytes 1572872 | tf_op jit(solution)/shard_map/ppermute | solution.py:320
  1.5 7.4 %copy-start.1 = (bf16[1,4,16,128,128]{4,3,2,1,0:T(8,128)(2,1)S(1)}, bf16[1,4,16,128,128]{4,3,2,1,0:T(8,128)(2,1)}, u32[]{:S(2)}) copy-start(bf16[1,4,16,128,128]{4,3,2,1,0:T(8,128)(2,1)} %gyro.1) | copy-start | bytes 6291460
  1.5 7.4 %copy-start.3 = (s32[1,4,16]{2,1,0:T(4,128)S(1)}, s32[1,4,16]{2,1,0:T(4,128)}, u32[]{:S(2)}) copy-start(s32[1,4,16]{2,1,0:T(4,128)} %pattern.1) | copy-start | bytes 772
  1.5 11.0 %collective-permute-start.2 = (bf16[64,2048]{1,0:T(8,128)(2,1)S(1)}, bf16[64,2048]{1,0:T(8,128)(2,1)S(1)}, u32[]{:S(2)}, u32[]{:S(2)}) collective-permute-start(bf16[64,2048]{1,0:T(8,128)(2,1)S(1)} %plain.1), channel_id=1, source_target_pairs={{0,8},{2,10},{4,0},{6,2},{8,12},{10,14},{12,4},{14,6},{1,9},{3,11}... | collective-permute-start | bytes 786440 | tf_op jit(solution)/shard_map/ppermute | solution.py:300
  5.4 9.3 %collective-permute-start.3 = (bf16[64,1024]{1,0:T(8,128)(2,1)S(1)}, bf16[64,1024]{1,0:T(8,128)(2,1)S(1)}, u32[]{:S(2)}, u32[]{:S(2)}) collective-permute-start(bf16[64,1024]{1,0:T(8,128)(2,1)S(1)} %get-tuple-element.30), channel_id=1, source_target_pairs={{0,8},{2,10},{4,0},{6,2},{8,12},{10,14},{12,4},{14,6},{1,9},{3,11}... | collective-permute-start | bytes 393224 | tf_op jit(solution)/shard_map/ppermute | solution.py:300
  7.0 17.9 %collective-permute-start.1 = (bf16[64,3072]{1,0:T(8,128)(2,1)S(1)}, bf16[64,3072]{1,0:T(8,128)(2,1)S(1)}, u32[]{:S(2)}, u32[]{:S(2)}) collective-permute-start(bf16[64,3072]{1,0:T(8,128)(2,1)S(1)} %get-tuple-element.29), channel_id=1, source_target_pairs={{0,4},{2,6},{4,12},{6,14},{8,0},{10,2},{12,8},{14,10},{1,5},{3,7},... | collective-permute-start | bytes 1179656 | tf_op jit(solution)/shard_map/ppermute | solution.py:300
  7.4 21.6 %collective-permute-start.6 = (bf16[64,2560]{1,0:T(8,128)(2,1)S(1)}, bf16[64,2560]{1,0:T(8,128)(2,1)S(1)}, u32[]{:S(2)}, u32[]{:S(2)}) collective-permute-start(bf16[64,2560]{1,0:T(8,128)(2,1)S(1)} %get-tuple-element.37), channel_id=1, source_target_pairs={{0,2},{2,0},{4,6},{6,4},{8,10},{10,8},{12,14},{14,12},{1,3},{3,1},... | collective-permute-start | bytes 983048 | tf_op jit(solution)/shard_map/ppermute | solution.py:300
  14.7 15.6 %collective-permute-start.7 = (bf16[64,2560]{1,0:T(8,128)(2,1)S(1)}, bf16[64,2560]{1,0:T(8,128)(2,1)S(1)}, u32[]{:S(2)}, u32[]{:S(2)}) collective-permute-start(bf16[64,2560]{1,0:T(8,128)(2,1)S(1)} %get-tuple-element.33.refs_0_), channel_id=1, source_target_pairs={{0,2},{2,0},{4,6},{6,4},{8,10},{10,8},{12,14},{14,12},{1,3},{3,1},... | collective-permute-start | bytes 983048 | tf_op jit(solution)/shard_map/ppermute | solution.py:300
  16.3 15.6 %collective-permute-start.5 = (bf16[32,3072]{1,0:T(8,128)(2,1)S(1)}, bf16[32,3072]{1,0:T(8,128)(2,1)S(1)}, u32[]{:S(2)}, u32[]{:S(2)}) collective-permute-start(bf16[32,3072]{1,0:T(8,128)(2,1)S(1)} %get-tuple-element.36), channel_id=1, source_target_pairs={{0,12},{2,14},{4,8},{6,10},{8,4},{10,6},{12,0},{14,2},{1,13},{3,15... | collective-permute-start | bytes 589832 | tf_op jit(solution)/shard_map/ppermute | solution.py:300
  25.0 16.5 %collective-permute-start.4 = (bf16[64,2560]{1,0:T(8,128)(2,1)S(1)}, bf16[64,2560]{1,0:T(8,128)(2,1)S(1)}, u32[]{:S(2)}, u32[]{:S(2)}) collective-permute-start(bf16[64,2560]{1,0:T(8,128)(2,1)S(1)} %get-tuple-element.35), channel_id=1, source_target_pairs={{0,2},{2,0},{4,6},{6,4},{8,10},{10,8},{12,14},{14,12},{1,3},{3,1},... | collective-permute-start | bytes 983048 | tf_op jit(solution)/shard_map/ppermute | solution.py:300
  26.5 6.8 %collective-permute-start.8 = (bf16[16,3072]{1,0:T(8,128)(2,1)S(1)}, bf16[16,3072]{1,0:T(8,128)(2,1)S(1)}, u32[]{:S(2)}, u32[]{:S(2)}) collective-permute-start(bf16[16,3072]{1,0:T(8,128)(2,1)S(1)} %get-tuple-element.41), channel_id=1, source_target_pairs={{0,12},{2,14},{4,8},{6,10},{8,4},{10,6},{12,0},{14,2},{1,13},{3,15... | collective-permute-start | bytes 294920 | tf_op jit(solution)/shard_map/ppermute | solution.py:300
  29.0 6.5 %collective-permute-start.9 = (bf16[16,3072]{1,0:T(8,128)(2,1)S(1)}, bf16[16,3072]{1,0:T(8,128)(2,1)S(1)}, u32[]{:S(2)}, u32[]{:S(2)}) collective-permute-start(bf16[16,3072]{1,0:T(8,128)(2,1)S(1)} %get-tuple-element.43), channel_id=1, source_target_pairs={{0,12},{2,14},{4,8},{6,10},{8,4},{10,6},{12,0},{14,2},{1,13},{3,15... | collective-permute-start | bytes 294920 | tf_op jit(solution)/shard_map/ppermute | solution.py:300
  32.0 9.5 %collective-permute-start.10 = (bf16[32,2560]{1,0:T(8,128)(2,1)S(1)}, bf16[32,2560]{1,0:T(8,128)(2,1)S(1)}, u32[]{:S(2)}, u32[]{:S(2)}) collective-permute-start(bf16[32,2560]{1,0:T(8,128)(2,1)S(1)} %get-tuple-element.45), channel_id=1, source_target_pairs={{0,2},{2,0},{4,6},{6,4},{8,10},{10,8},{12,14},{14,12},{1,3},{3,1},... | collective-permute-start | bytes 491528 | tf_op jit(solution)/shard_map/ppermute | solution.py:300
  33.4 7.2 %collective-permute-start.11 = (bf16[16,2560]{1,0:T(8,128)(2,1)S(1)}, bf16[16,2560]{1,0:T(8,128)(2,1)S(1)}, u32[]{:S(2)}, u32[]{:S(2)}) collective-permute-start(bf16[16,2560]{1,0:T(8,128)(2,1)S(1)} %get-tuple-element.46), channel_id=1, source_target_pairs={{0,2},{2,0},{4,6},{6,4},{8,10},{10,8},{12,14},{14,12},{1,3},{3,1},... | collective-permute-start | bytes 245768 | tf_op jit(solution)/shard_map/ppermute | solution.py:300
  35.5 5.9 %collective-permute-start.12 = (bf16[16,2560]{1,0:T(8,128)(2,1)S(1)}, bf16[16,2560]{1,0:T(8,128)(2,1)S(1)}, u32[]{:S(2)}, u32[]{:S(2)}) collective-permute-start(bf16[16,2560]{1,0:T(8,128)(2,1)S(1)} %get-tuple-element.47), channel_id=1, source_target_pairs={{0,2},{2,0},{4,6},{6,4},{8,10},{10,8},{12,14},{14,12},{1,3},{3,1},... | collective-permute-start | bytes 245768 | tf_op jit(solution)/shard_map/ppermute | solution.py:300
  42.6 2.0 %collective-permute-start.14 = (f32[512,256]{1,0:T(8,128)S(1)}, f32[512,256]{1,0:T(8,128)S(1)}, u32[]{:S(2)}, u32[]{:S(2)}) collective-permute-start(f32[512,256]{1,0:T(8,128)S(1)} %get-tuple-element.52), channel_id=1, source_target_pairs={{0,1},{1,0},{2,3},{3,2},{4,5},{5,4},{6,7},{7,6},{8,9},{9,8},{10,11... | collective-permute-start | bytes 1572872 | tf_op jit(solution)/shard_map/ppermute | solution.py:386
  43.8 2.1 %collective-permute-start.13 = (f32[512,256]{1,0:T(8,128)S(1)}, f32[512,256]{1,0:T(8,128)S(1)}, u32[]{:S(2)}, u32[]{:S(2)}) collective-permute-start(f32[512,256]{1,0:T(8,128)S(1)} %get-tuple-element.50), channel_id=1, source_target_pairs={{0,1},{1,0},{2,3},{3,2},{4,5},{5,4},{6,7},{7,6},{8,9},{9,8},{10,11... | collective-permute-start | bytes 1572872 | tf_op jit(solution)/shard_map/ppermute | solution.py:386
  46.1 12.9 %collective-permute-start.21 = (bf16[2,64,256]{2,1,0:T(8,128)(2,1)S(1)}, bf16[2,64,256]{2,1,0:T(8,128)(2,1)S(1)}, u32[]{:S(2)}, u32[]{:S(2)}) collective-permute-start(bf16[2,64,256]{2,1,0:T(8,128)(2,1)S(1)} %get-tuple-element.54), channel_id=1, source_target_pairs={{0,14},{2,12},{4,10},{6,8},{8,6},{10,4},{12,2},{14,0},{1,15},{3,13... | collective-permute-start | bytes 196616 | tf_op jit(solution)/shard_map/ppermute | solution.py:300
  49.6 9.4 %collective-permute-start.20 = (bf16[2,64,256]{2,1,0:T(8,128)(2,1)S(1)}, bf16[2,64,256]{2,1,0:T(8,128)(2,1)S(1)}, u32[]{:S(2)}, u32[]{:S(2)}) collective-permute-start(bf16[2,64,256]{2,1,0:T(8,128)(2,1)S(1)} %get-tuple-element.55), channel_id=1, source_target_pairs={{0,12},{2,14},{4,8},{6,10},{8,4},{10,6},{12,0},{14,2},{1,13},{3,15... | collective-permute-start | bytes 196616 | tf_op jit(solution)/shard_map/ppermute | solution.py:300
  50.9 8.7 %collective-permute-start.19 = (bf16[2,64,256]{2,1,0:T(8,128)(2,1)S(1)}, bf16[2,64,256]{2,1,0:T(8,128)(2,1)S(1)}, u32[]{:S(2)}, u32[]{:S(2)}) collective-permute-start(bf16[2,64,256]{2,1,0:T(8,128)(2,1)S(1)} %get-tuple-element.56), channel_id=1, source_target_pairs={{0,10},{2,8},{4,2},{6,0},{8,14},{10,12},{12,6},{14,4},{1,11},{3,9}... | collective-permute-start | bytes 196616 | tf_op jit(solution)/shard_map/ppermute | solution.py:300
  56.1 4.3 %collective-permute-start.18 = (bf16[2,64,256]{2,1,0:T(8,128)(2,1)S(1)}, bf16[2,64,256]{2,1,0:T(8,128)(2,1)S(1)}, u32[]{:S(2)}, u32[]{:S(2)}) collective-permute-start(bf16[2,64,256]{2,1,0:T(8,128)(2,1)S(1)} %get-tuple-element.57), channel_id=1, source_target_pairs={{0,8},{2,10},{4,0},{6,2},{8,12},{10,14},{12,4},{14,6},{1,9},{3,11}... | collective-permute-start | bytes 196616 | tf_op jit(solution)/shard_map/ppermute | solution.py:300
  56.1 7.5 %collective-permute-start.17 = (bf16[2,64,256]{2,1,0:T(8,128)(2,1)S(1)}, bf16[2,64,256]{2,1,0:T(8,128)(2,1)S(1)}, u32[]{:S(2)}, u32[]{:S(2)}) collective-permute-start(bf16[2,64,256]{2,1,0:T(8,128)(2,1)S(1)} %get-tuple-element.58), channel_id=1, source_target_pairs={{0,6},{2,4},{4,14},{6,12},{8,2},{10,0},{12,10},{14,8},{1,7},{3,5},... | collective-permute-start | bytes 196616 | tf_op jit(solution)/shard_map/ppermute | solution.py:300
  59.0 5.2 %collective-permute-start.16 = (bf16[2,64,256]{2,1,0:T(8,128)(2,1)S(1)}, bf16[2,64,256]{2,1,0:T(8,128)(2,1)S(1)}, u32[]{:S(2)}, u32[]{:S(2)}) collective-permute-start(bf16[2,64,256]{2,1,0:T(8,128)(2,1)S(1)} %get-tuple-element.59), channel_id=1, source_target_pairs={{0,4},{2,6},{4,12},{6,14},{8,0},{10,2},{12,8},{14,10},{1,5},{3,7},... | collective-permute-start | bytes 196616 | tf_op jit(solution)/shard_map/ppermute | solution.py:300
  59.0 5.2 %collective-permute-start.15 = (bf16[2,64,256]{2,1,0:T(8,128)(2,1)S(1)}, bf16[2,64,256]{2,1,0:T(8,128)(2,1)S(1)}, u32[]{:S(2)}, u32[]{:S(2)}) collective-permute-start(bf16[2,64,256]{2,1,0:T(8,128)(2,1)S(1)} %get-tuple-element.53), channel_id=1, source_target_pairs={{0,2},{2,0},{4,6},{6,4},{8,10},{10,8},{12,14},{14,12},{1,3},{3,1},... | collective-permute-start | bytes 196616 | tf_op jit(solution)/shard_map/ppermute | solution.py:300
  (2 other events, 2.6 us)

commit v7 on v6

--- a/solution.py
+++ b/solution.py
@@ -10,7 +10,7 @@
 
 HB = 8
 X = 2
-PIECES = (32, 16, 16)
+PIECES = (32, 32)
 VMEM_LIMIT = 24 * 1024 * 1024
 NT = (((1,), (1,)), ((), ()))
 VMEM = pl.BlockSpec(memory_space=pltpu.VMEM)
@@ -130,26 +130,55 @@
     cut(group, own, got, x)
 
 
+def part(group, out, first, plain, rim):
+    _, z, _ = place_in_mode()
+    for lower, order in ((True, (rim, plain)), (False, (plain, rim))):
+        for shift in range(2):
+
+            @pl.when(((z < 2) == lower) & (first == shift))
+            def _():
+                split = order[0].shape[1] - shift * group
+                out[:, :split] = order[0][:, shift * group :]
+                out[:, split:] = order[1][:, : out.shape[1] - split]
+
+
+def last_kernel(group, at, piece, passed, rim, *refs):
+    cross, own = refs[-2:]
+    _, z, x = place_in_mode()
+    rows = slice(at, at + piece.shape[0])
+    inside = (z == 1) | (z == 2)
+    for here, plain in ((inside, piece), (jnp.logical_not(inside), passed.at[rows, :])):
+
+        @pl.when(here)
+        def _():
+            part(group, cross, 1 - x, plain, rim.at[rows, :])
+            part(group, own, x, plain, rim.at[rows, :])
+
+
 def onward_kernel(group, plain, rim, ext, *refs):
-    cross, own, *far = refs[-2 - len(PIECES) :]
+    cross, own, passed, far_rim, *inner = refs[-4 - len(PIECES) :]
     _, z, x = place_in_mode()
-
-    def part(out, first):
-        for lower, order in ((True, (rim, plain)), (False, (plain, rim))):
-            for shift in range(2):
-
-                @pl.when(((z < 2) == lower) & (first == shift))
-                def _():
-                    split = order[0].shape[1] - shift * group
-                    out[:, :split] = order[0][:, shift * group :]
-                    out[:, split:] = order[1][:, : out.shape[1] - split]
-
-    part(cross, 1 - x)
-    part(own, x)
+    part(group, cross, 1 - x, plain, rim)
+    part(group, own, x, plain, rim)
+    two = 2 * group
+
+    @pl.when(z < 2)
+    def _():
+        passed[:, :two] = rim[...]
+        passed[:, two:] = plain[:, :two]
+
+    @pl.when(z >= 2)
+    def _():
+        passed[:, :two] = plain[:, two:]
+        passed[:, two:] = rim[...]
+
+    target = 3 - z
+    cut(group, far_rim, ext, jnp.where(target < 2, 2 * target, 2 * target + 4))
+    start = aligned(jnp.where(target < 2, 2 * target + 2, 2 * target), group)
     at = 0
-    for out in far:
+    for out in inner:
         rows, span = out.shape
-        out[...] = ext[at : at + rows, pl.ds(aligned(2 * (3 - z), group), span)]
+        out[...] = ext[at : at + rows, pl.ds(start, span)]
         at += rows
 
 
@@ -185,8 +214,10 @@
 
 
 def image_kernel(layout, middle, *refs):
-    band, image, centre, lhs = refs[-4:]
-    fill(lhs, centre, regroup(layout, refs[:-4]), middle)
+    image, centre, lhs = refs[-3:]
+    pieces = 2 * sum(layout)
+    band = refs[pieces]
+    fill(lhs, centre, regroup(layout, refs[:pieces]), middle)
     image[...] = lax.dot_general(
         lhs[...], band[...], NT, preferred_element_type=jnp.float32
     ).astype(jnp.bfloat16)
@@ -197,7 +228,7 @@
     return layout, [chunk for sides in slots for chunks in sides for chunk in chunks]
 
 
-def make_image(slots, band, group, width):
+def make_image(slots, band, group, width, after):
     layout, pieces = flat(slots)
     span = pieces[0].shape[1]
     return pl.pallas_call(
@@ -206,7 +237,7 @@
             jax.ShapeDtypeStruct((4 * width, band.shape[0]), jnp.bfloat16),
             jax.ShapeDtypeStruct((2, 2 * width, group), jnp.bfloat16),
         ),
-        in_specs=[VMEM] * (len(pieces) + 1),
+        in_specs=[VMEM] * (len(pieces) + 1) + [ANY] * len(after),
         out_specs=(VMEM, VMEM),
         scratch_shapes=[pltpu.VMEM((4 * width, span), jnp.bfloat16)],
         compiler_params=params(),
@@ -214,7 +245,7 @@
             flops=8 * width * span * band.shape[0], bytes_accessed=2**22, transcendentals=0
         ),
         name="image",
-    )(*pieces, band)
+    )(*pieces, band, *after)
 
 
 def project_kernel(matrix, layout, middle, scaling, rows_out, *refs):
@@ -308,6 +339,12 @@
     def to_far(z):
         return 3 - z
 
+    def to_near(z):
+        return z ^ 1
+
+    def to_inside(z):
+        return 3 - z if z in (1, 2) else z
+
     def to_same(z):
         return z
 
@@ -336,16 +373,19 @@
     cross0 = move(cross0_w, (to_same, 1))
     band = make_band(pattern, gyroscopic, centrifugal, own0, w5, per_unit, block_total)
 
-    crossA_w, ownA, *far_w = cutting(
+    crossA_w, ownA, passed_w, far_rim_w, *inner_w = cutting(
         functools.partial(onward_kernel, group),
-        [(width, w5), (width, w5)] + [(rows, w6) for rows in PIECES],
+        [(width, w) for w in (w5, w5, 4 * group, 2 * group)]
+        + [(rows, 4 * group) for rows in PIECES],
         "onward",
         plainA,
         gotA,
         ext,
         after=(band,),
     )
-    far = [move(piece, (to_far, 0)) for piece in far_w]
+    far_rim = move(far_rim_w, (to_far, 0))
+    passed = move(passed_w, (to_near, 0))
+    inner = [move(piece, (to_inside, 0)) for piece in inner_w]
     crossA = move(crossA_w, (to_same, 1))
     crossB_w, ownB = cutting(
         functools.partial(parted_kernel, group),
@@ -356,15 +396,17 @@
     )
     crossB = move(crossB_w, (to_same, 1))
     image, centre = make_image(
-        [([own0], [cross0]), ([ownA], [crossA])], band, group, width
+        [([own0], [cross0]), ([ownA], [crossA])], band, group, width, (inner[0],)
     )
     ownC, crossC = [], []
-    for piece in far:
+    for number, piece in enumerate(inner):
         cross_w, own = cutting(
-            functools.partial(parted_kernel, group),
+            functools.partial(last_kernel, group, sum(PIECES[:number])),
             [(piece.shape[0], w5)] * 2,
-            "parted",
+            "last",
             piece,
+            passed,
+            far_rim,
             after=(image,),
         )
         ownC.append(own)

time: 65.1 us -> 64.8 us (level)
  waiting for transfers between devices: 21.1 us -> 17 us
  starting transfers between devices: 33.8 us -> 37.6 us
    ppermute x19, waiting for transfers between devices: 19.6 us -> 15.5 us  [move(): return lax.ppermute(array, 'mode', pairs)]
    ppermute x19, starting transfers between devices: 32.8 us -> 36.5 us  [move(): return lax.ppermute(array, 'mode', pairs)]
  transfers between devices with their start and end apart: 22 -> 22, of which waited for: 11 -> 9; matrix products, arithmetic and copies ran while one was open for 0% -> 0% of each run, Pallas kernels for 8% -> 8%
where the time goes in v7:
time: 64.8 us; the launch traced here: 64.6 us
  starting transfers between devices  37.6 us (58%)
  waiting for transfers between devices  17 us (26%)
  Pallas kernels  6.31 us (10%)
  local copies, waits for them, and re-layouts  2.67 us (4%)
  other arithmetic  0.92 us (1%)
    ppermute x19, starting transfers between devices, move(): return lax.ppermute(array, 'mode', pairs)  36.5 us
    ppermute x19, waiting for transfers between devices, move(): return lax.ppermute(array, 'mode', pairs)  15.5 us
    unnamed x8, local copies, waits for them, and re-layouts  2.64 us
    pallas_call x2, Pallas kernels, make_projection(): pl.pallas_call(functools.partial(project_kernel, matrix, layout, slice(2...  2.29 us
    pallas_call x1, Pallas kernels, make_band(): pl.pallas_call(functools.partial(band_kernel, per_unit, block_total), out...  2.03 us
    pallas_call x1, Pallas kernels, make_image(): pl.pallas_call(functools.partial(image_kernel, layout, slice(2 * group, 3...  1.55 us
    ppermute x2, waiting for transfers between devices, body(): sums.append(keep + lax.ppermute(send, 'sub', [(0, 1), (1, 0)]))  1.47 us
  transfers between devices with their start and end apart: 22, of which 9 were waited for; matrix products, arithmetic and copies ran while one was open for 0% of the time, Pallas kernels for 8%

profile of v7, /device:TPU:0, one launch (start us, length us, event | category | flops | bytes accessed | tf_op | source)
XLA Modules:
  0.0 64.6 jit_solution(8669826655290879688)
XLA Ops:
  1.5 3.6 %collective-permute-start.2 = (bf16[64,2048]{1,0:T(8,128)(2,1)S(1)}, bf16[64,2048]{1,0:T(8,128)(2,1)S(1)}, u32[]{:S(2)}, u32[]{:S(2)}) collective-permute-start(bf16[64,2048]{1,0:T(8,128)(2,1)S(1)} %plain.1), channel_id=1, source_target_pairs={{0,8},{2,10},{4,0},{6,2},{8,12},{10,14},{12,4},{14,6},{1,9},{3,11}... | collective-permute-start | bytes 786440 | tf_op jit(solution)/shard_map/ppermute | solution.py:331
  5.4 1.6 %collective-permute-start.3 = (bf16[64,1024]{1,0:T(8,128)(2,1)S(1)}, bf16[64,1024]{1,0:T(8,128)(2,1)S(1)}, u32[]{:S(2)}, u32[]{:S(2)}) collective-permute-start(bf16[64,1024]{1,0:T(8,128)(2,1)S(1)} %get-tuple-element.29), channel_id=1, source_target_pairs={{0,8},{2,10},{4,0},{6,2},{8,12},{10,14},{12,4},{14,6},{1,9},{3,11}... | collective-permute-start | bytes 393224 | tf_op jit(solution)/shard_map/ppermute | solution.py:331
  7.4 1.5 %collective-permute-start.8 = (bf16[64,2560]{1,0:T(8,128)(2,1)S(1)}, bf16[64,2560]{1,0:T(8,128)(2,1)S(1)}, u32[]{:S(2)}, u32[]{:S(2)}) collective-permute-start(bf16[64,2560]{1,0:T(8,128)(2,1)S(1)} %get-tuple-element.38), channel_id=1, source_target_pairs={{0,2},{2,0},{4,6},{6,4},{8,10},{10,8},{12,14},{14,12},{1,3},{3,1},... | collective-permute-start | bytes 983048 | tf_op jit(solution)/shard_map/ppermute | solution.py:331
  8.9 1.6 %copy-done.2 = bf16[1,4,16,128,128]{4,3,2,1,0:T(8,128)(2,1)S(1)} copy-done((bf16[1,4,16,128,128]{4,3,2,1,0:T(8,128)(2,1)S(1)}, bf16[1,4,16,128,128]{4,3,2,1,0:T(8,128)(2,1)}, u32[]{:S(2)}) %copy-start.2) | copy-done | bytes 2097176
  10.5 2.0 %band.1 = bf16[2,4,128,2560]{3,2,1,0:T(8,128)(2,1)S(1)} custom-call(s32[1,4,16]{2,1,0:T(4,128)S(1)} %copy-done.3, bf16[1,4,16,128,128]{4,3,2,1,0:T(8,128)(2,1)S(1)} %copy-done.1, bf16[1,4,16,128,128]{4,3,2,1,0:T(8,128)(2,1)S(1)} %copy-done.2, bf16[64,2560]{1,0:T(8,128)(2,1)S(1)} %get-tuple-element.31._.refs_0_), custom_call_target="tpu_custom_call" | custom-call | bytes 8388608 | tf_op jit(solution)/shard_map/band/pallas_call | solution.py:62
  12.6 2.1 %collective-permute-done.3.rim = bf16[64,1024]{1,0:T(8,128)(2,1)S(1)} collective-permute-done((bf16[64,1024]{1,0:T(8,128)(2,1)S(1)}, bf16[64,1024]{1,0:T(8,128)(2,1)S(1)}, u32[]{:S(2)}, u32[]{:S(2)}) %collective-permute-start.3) | collective-permute-done | bytes 131104 | tf_op jit(solution)/shard_map/ppermute | solution.py:331
  14.8 1.6 %collective-permute-start.9 = (bf16[64,2560]{1,0:T(8,128)(2,1)S(1)}, bf16[64,2560]{1,0:T(8,128)(2,1)S(1)}, u32[]{:S(2)}, u32[]{:S(2)}) collective-permute-start(bf16[64,2560]{1,0:T(8,128)(2,1)S(1)} %get-tuple-element.32.refs_0_), channel_id=1, source_target_pairs={{0,2},{2,0},{4,6},{6,4},{8,10},{10,8},{12,14},{14,12},{1,3},{3,1},... | collective-permute-start | bytes 983048 | tf_op jit(solution)/shard_map/ppermute | solution.py:331
  17.0 5.2 %collective-permute-start.6 = (bf16[64,2048]{1,0:T(8,128)(2,1)S(1)}, bf16[64,2048]{1,0:T(8,128)(2,1)S(1)}, u32[]{:S(2)}, u32[]{:S(2)}) collective-permute-start(bf16[64,2048]{1,0:T(8,128)(2,1)S(1)} %get-tuple-element.36), channel_id=1, source_target_pairs={{0,4},{2,6},{4,0},{6,2},{8,12},{10,14},{12,8},{14,10},{1,5},{3,7},... | collective-permute-start | bytes 786440 | tf_op jit(solution)/shard_map/ppermute | solution.py:331
  22.2 2.3 %collective-permute-done.1.got = bf16[64,3072]{1,0:T(8,128)(2,1)S(1)} collective-permute-done((bf16[64,3072]{1,0:T(8,128)(2,1)S(1)}, bf16[64,3072]{1,0:T(8,128)(2,1)S(1)}, u32[]{:S(2)}, u32[]{:S(2)}) %collective-permute-start.1) | collective-permute-done | bytes 393248 | tf_op jit(solution)/shard_map/ppermute | solution.py:331
  24.6 1.6 %collective-permute-start.4 = (bf16[64,2560]{1,0:T(8,128)(2,1)S(1)}, bf16[64,2560]{1,0:T(8,128)(2,1)S(1)}, u32[]{:S(2)}, u32[]{:S(2)}) collective-permute-start(bf16[64,2560]{1,0:T(8,128)(2,1)S(1)} %get-tuple-element.34), channel_id=1, source_target_pairs={{0,2},{2,0},{4,6},{6,4},{8,10},{10,8},{12,14},{14,12},{1,3},{3,1},... | collective-permute-start | bytes 983048 | tf_op jit(solution)/shard_map/ppermute | solution.py:331
  26.2 2.5 %collective-permute-start.7 = (bf16[64,1024]{1,0:T(8,128)(2,1)S(1)}, bf16[64,1024]{1,0:T(8,128)(2,1)S(1)}, u32[]{:S(2)}, u32[]{:S(2)}) collective-permute-start(bf16[64,1024]{1,0:T(8,128)(2,1)S(1)} %get-tuple-element.37), channel_id=1, source_target_pairs={{0,12},{2,14},{4,8},{6,10},{8,4},{10,6},{12,0},{14,2},{1,13},{3,15... | collective-permute-start | bytes 393224 | tf_op jit(solution)/shard_map/ppermute | solution.py:331
  29.3 1.5 %image.1 = (bf16[256,1024]{1,0:T(8,128)(2,1)S(1)}, bf16[2,128,512]{2,1,0:T(8,128)(2,1)S(1)}) custom-call(bf16[64,2560]{1,0:T(8,128)(2,1)S(1)} %get-tuple-element.31._.refs_0_, bf16[64,2560]{1,0:T(8,128)(2,1)S(1)} %collective-permute-done.8.refs_1_, bf16[64,2560]{1,0:T(8,128)(2,1)S(1)} %get-tuple-element.39.refs_2_, ...), custom_call_target="tpu_custom_call" | custom-call | flops 1342177280 | bytes 4194304 | tf_op jit(solution)/shard_map/image/pallas_call | solution.py:234
  30.9 2.2 %collective-permute-done.7.rim = bf16[64,1024]{1,0:T(8,128)(2,1)S(1)} collective-permute-done((bf16[64,1024]{1,0:T(8,128)(2,1)S(1)}, bf16[64,1024]{1,0:T(8,128)(2,1)S(1)}, u32[]{:S(2)}, u32[]{:S(2)}) %collective-permute-start.7) | collective-permute-done | bytes 131104 | tf_op jit(solution)/shard_map/ppermute | solution.py:331
  33.2 1.4 %collective-permute-start.11 = (bf16[32,2560]{1,0:T(8,128)(2,1)S(1)}, bf16[32,2560]{1,0:T(8,128)(2,1)S(1)}, u32[]{:S(2)}, u32[]{:S(2)}) collective-permute-start(bf16[32,2560]{1,0:T(8,128)(2,1)S(1)} %get-tuple-element.44), channel_id=1, source_target_pairs={{0,2},{2,0},{4,6},{6,4},{8,10},{10,8},{12,14},{14,12},{1,3},{3,1},... | collective-permute-start | bytes 491528 | tf_op jit(solution)/shard_map/ppermute | solution.py:331
  35.4 4.8 %collective-permute-done.11.refs_4_ = bf16[32,2560]{1,0:T(8,128)(2,1)S(1)} collective-permute-done((bf16[32,2560]{1,0:T(8,128)(2,1)S(1)}, bf16[32,2560]{1,0:T(8,128)(2,1)S(1)}, u32[]{:S(2)}, u32[]{:S(2)}) %collective-permute-start.11) | collective-permute-done | bytes 163872 | tf_op jit(solution)/shard_map/ppermute | solution.py:331
  40.3 1.8 %collective-permute-done.12.refs_5_ = bf16[32,2560]{1,0:T(8,128)(2,1)S(1)} collective-permute-done((bf16[32,2560]{1,0:T(8,128)(2,1)S(1)}, bf16[32,2560]{1,0:T(8,128)(2,1)S(1)}, u32[]{:S(2)}, u32[]{:S(2)}) %collective-permute-start.12) | collective-permute-done | bytes 163872 | tf_op jit(solution)/shard_map/ppermute | solution.py:331
  45.2 1.3 %collective-permute-done.13 = f32[512,256]{1,0:T(8,128)S(1)} collective-permute-done((f32[512,256]{1,0:T(8,128)S(1)}, f32[512,256]{1,0:T(8,128)S(1)}, u32[]{:S(2)}, u32[]{:S(2)}) %collective-permute-start.13) | collective-permute-done | bytes 524320 | tf_op jit(solution)/shard_map/ppermute | solution.py:428
  46.7 3.7 %collective-permute-start.21 = (bf16[2,64,256]{2,1,0:T(8,128)(2,1)S(1)}, bf16[2,64,256]{2,1,0:T(8,128)(2,1)S(1)}, u32[]{:S(2)}, u32[]{:S(2)}) collective-permute-start(bf16[2,64,256]{2,1,0:T(8,128)(2,1)S(1)} %get-tuple-element.52), channel_id=1, source_target_pairs={{0,14},{2,12},{4,10},{6,8},{8,6},{10,4},{12,2},{14,0},{1,15},{3,13... | collective-permute-start | bytes 196616 | tf_op jit(solution)/shard_map/ppermute | solution.py:331
  50.4 1.4 %collective-permute-start.20 = (bf16[2,64,256]{2,1,0:T(8,128)(2,1)S(1)}, bf16[2,64,256]{2,1,0:T(8,128)(2,1)S(1)}, u32[]{:S(2)}, u32[]{:S(2)}) collective-permute-start(bf16[2,64,256]{2,1,0:T(8,128)(2,1)S(1)} %get-tuple-element.53), channel_id=1, source_target_pairs={{0,12},{2,14},{4,8},{6,10},{8,4},{10,6},{12,0},{14,2},{1,13},{3,15... | collective-permute-start | bytes 196616 | tf_op jit(solution)/shard_map/ppermute | solution.py:331
  51.8 2.5 %collective-permute-start.19 = (bf16[2,64,256]{2,1,0:T(8,128)(2,1)S(1)}, bf16[2,64,256]{2,1,0:T(8,128)(2,1)S(1)}, u32[]{:S(2)}, u32[]{:S(2)}) collective-permute-start(bf16[2,64,256]{2,1,0:T(8,128)(2,1)S(1)} %get-tuple-element.54), channel_id=1, source_target_pairs={{0,10},{2,8},{4,2},{6,0},{8,14},{10,12},{12,6},{14,4},{1,11},{3,9}... | collective-permute-start | bytes 196616 | tf_op jit(solution)/shard_map/ppermute | solution.py:331
  54.5 2.6 %collective-permute-start.17 = (bf16[2,64,256]{2,1,0:T(8,128)(2,1)S(1)}, bf16[2,64,256]{2,1,0:T(8,128)(2,1)S(1)}, u32[]{:S(2)}, u32[]{:S(2)}) collective-permute-start(bf16[2,64,256]{2,1,0:T(8,128)(2,1)S(1)} %get-tuple-element.56), channel_id=1, source_target_pairs={{0,6},{2,4},{4,14},{6,12},{8,2},{10,0},{12,10},{14,8},{1,7},{3,5},... | collective-permute-start | bytes 196616 | tf_op jit(solution)/shard_map/ppermute | solution.py:331
  57.1 2.3 %collective-permute-start.16 = (bf16[2,64,256]{2,1,0:T(8,128)(2,1)S(1)}, bf16[2,64,256]{2,1,0:T(8,128)(2,1)S(1)}, u32[]{:S(2)}, u32[]{:S(2)}) collective-permute-start(bf16[2,64,256]{2,1,0:T(8,128)(2,1)S(1)} %get-tuple-element.57), channel_id=1, source_target_pairs={{0,4},{2,6},{4,12},{6,14},{8,0},{10,2},{12,8},{14,10},{1,5},{3,7},... | collective-permute-start | bytes 196616 | tf_op jit(solution)/shard_map/ppermute | solution.py:331
  59.4 2.3 %collective-permute-start.15 = (bf16[2,64,256]{2,1,0:T(8,128)(2,1)S(1)}, bf16[2,64,256]{2,1,0:T(8,128)(2,1)S(1)}, u32[]{:S(2)}, u32[]{:S(2)}) collective-permute-start(bf16[2,64,256]{2,1,0:T(8,128)(2,1)S(1)} %get-tuple-element.51), channel_id=1, source_target_pairs={{0,2},{2,0},{4,6},{6,4},{8,10},{10,8},{12,14},{14,12},{1,3},{3,1},... | collective-permute-start | bytes 196616 | tf_op jit(solution)/shard_map/ppermute | solution.py:331
  62.2 1.7 %collective-permute-done.16 = bf16[2,64,256]{2,1,0:T(8,128)(2,1)S(1)} collective-permute-done((bf16[2,64,256]{2,1,0:T(8,128)(2,1)S(1)}, bf16[2,64,256]{2,1,0:T(8,128)(2,1)S(1)}, u32[]{:S(2)}, u32[]{:S(2)}) %collective-permute-start.16) | collective-permute-done | bytes 65568 | tf_op jit(solution)/shard_map/ppermute | solution.py:331
  (44 shorter events, 9.4 us)
Async XLA Ops:
  0.0 5.2 %collective-permute-start = (bf16[64,4096]{1,0:T(8,128)(2,1)}, bf16[64,4096]{1,0:T(8,128)(2,1)S(1)}, u32[]{:S(2)}, u32[]{:S(2)}) collective-permute-start(bf16[64,4096]{1,0:T(8,128)(2,1)} %bitcast.12), channel_id=1, source_target_pairs={{0,1},{1,0},{2,3},{3,2},{4,5},{5,4},{6,7},{7,6},{8,9},{9,8},{10,11... | collective-permute-start | bytes 1572872 | tf_op jit(solution)/shard_map/ppermute | solution.py:357
  1.5 7.4 %copy-start.1 = (bf16[1,4,16,128,128]{4,3,2,1,0:T(8,128)(2,1)S(1)}, bf16[1,4,16,128,128]{4,3,2,1,0:T(8,128)(2,1)}, u32[]{:S(2)}) copy-start(bf16[1,4,16,128,128]{4,3,2,1,0:T(8,128)(2,1)} %gyro.1) | copy-start | bytes 6291460
  1.5 7.4 %copy-start.3 = (s32[1,4,16]{2,1,0:T(4,128)S(1)}, s32[1,4,16]{2,1,0:T(4,128)}, u32[]{:S(2)}) copy-start(s32[1,4,16]{2,1,0:T(4,128)} %pattern.1) | copy-start | bytes 772
  1.5 11.0 %collective-permute-start.2 = (bf16[64,2048]{1,0:T(8,128)(2,1)S(1)}, bf16[64,2048]{1,0:T(8,128)(2,1)S(1)}, u32[]{:S(2)}, u32[]{:S(2)}) collective-permute-start(bf16[64,2048]{1,0:T(8,128)(2,1)S(1)} %plain.1), channel_id=1, source_target_pairs={{0,8},{2,10},{4,0},{6,2},{8,12},{10,14},{12,4},{14,6},{1,9},{3,11}... | collective-permute-start | bytes 786440 | tf_op jit(solution)/shard_map/ppermute | solution.py:331
  5.4 9.3 %collective-permute-start.3 = (bf16[64,1024]{1,0:T(8,128)(2,1)S(1)}, bf16[64,1024]{1,0:T(8,128)(2,1)S(1)}, u32[]{:S(2)}, u32[]{:S(2)}) collective-permute-start(bf16[64,1024]{1,0:T(8,128)(2,1)S(1)} %get-tuple-element.29), channel_id=1, source_target_pairs={{0,8},{2,10},{4,0},{6,2},{8,12},{10,14},{12,4},{14,6},{1,9},{3,11}... | collective-permute-start | bytes 393224 | tf_op jit(solution)/shard_map/ppermute | solution.py:331
  7.0 17.6 %collective-permute-start.1 = (bf16[64,3072]{1,0:T(8,128)(2,1)S(1)}, bf16[64,3072]{1,0:T(8,128)(2,1)S(1)}, u32[]{:S(2)}, u32[]{:S(2)}) collective-permute-start(bf16[64,3072]{1,0:T(8,128)(2,1)S(1)} %get-tuple-element.28), channel_id=1, source_target_pairs={{0,4},{2,6},{4,12},{6,14},{8,0},{10,2},{12,8},{14,10},{1,5},{3,7},... | collective-permute-start | bytes 1179656 | tf_op jit(solution)/shard_map/ppermute | solution.py:331
  7.4 21.2 %collective-permute-start.8 = (bf16[64,2560]{1,0:T(8,128)(2,1)S(1)}, bf16[64,2560]{1,0:T(8,128)(2,1)S(1)}, u32[]{:S(2)}, u32[]{:S(2)}) collective-permute-start(bf16[64,2560]{1,0:T(8,128)(2,1)S(1)} %get-tuple-element.38), channel_id=1, source_target_pairs={{0,2},{2,0},{4,6},{6,4},{8,10},{10,8},{12,14},{14,12},{1,3},{3,1},... | collective-permute-start | bytes 983048 | tf_op jit(solution)/shard_map/ppermute | solution.py:331
  14.8 14.6 %collective-permute-start.9 = (bf16[64,2560]{1,0:T(8,128)(2,1)S(1)}, bf16[64,2560]{1,0:T(8,128)(2,1)S(1)}, u32[]{:S(2)}, u32[]{:S(2)}) collective-permute-start(bf16[64,2560]{1,0:T(8,128)(2,1)S(1)} %get-tuple-element.32.refs_0_), channel_id=1, source_target_pairs={{0,2},{2,0},{4,6},{6,4},{8,10},{10,8},{12,14},{14,12},{1,3},{3,1},... | collective-permute-start | bytes 983048 | tf_op jit(solution)/shard_map/ppermute | solution.py:331
  16.3 9.9 %collective-permute-start.5 = (bf16[32,2048]{1,0:T(8,128)(2,1)S(1)}, bf16[32,2048]{1,0:T(8,128)(2,1)S(1)}, u32[]{:S(2)}, u32[]{:S(2)}) collective-permute-start(bf16[32,2048]{1,0:T(8,128)(2,1)S(1)} %get-tuple-element.35), channel_id=1, source_target_pairs={{0,0},{2,2},{4,8},{6,10},{8,4},{10,6},{12,12},{14,14},{1,1},{3,3},... | collective-permute-start | bytes 393224 | tf_op jit(solution)/shard_map/ppermute | solution.py:331
  17.0 16.1 %collective-permute-start.6 = (bf16[64,2048]{1,0:T(8,128)(2,1)S(1)}, bf16[64,2048]{1,0:T(8,128)(2,1)S(1)}, u32[]{:S(2)}, u32[]{:S(2)}) collective-permute-start(bf16[64,2048]{1,0:T(8,128)(2,1)S(1)} %get-tuple-element.36), channel_id=1, source_target_pairs={{0,4},{2,6},{4,0},{6,2},{8,12},{10,14},{12,8},{14,10},{1,5},{3,7},... | collective-permute-start | bytes 786440 | tf_op jit(solution)/shard_map/ppermute | solution.py:331
  24.6 17.4 %collective-permute-start.4 = (bf16[64,2560]{1,0:T(8,128)(2,1)S(1)}, bf16[64,2560]{1,0:T(8,128)(2,1)S(1)}, u32[]{:S(2)}, u32[]{:S(2)}) collective-permute-start(bf16[64,2560]{1,0:T(8,128)(2,1)S(1)} %get-tuple-element.34), channel_id=1, source_target_pairs={{0,2},{2,0},{4,6},{6,4},{8,10},{10,8},{12,14},{14,12},{1,3},{3,1},... | collective-permute-start | bytes 983048 | tf_op jit(solution)/shard_map/ppermute | solution.py:331
  26.2 6.9 %collective-permute-start.7 = (bf16[64,1024]{1,0:T(8,128)(2,1)S(1)}, bf16[64,1024]{1,0:T(8,128)(2,1)S(1)}, u32[]{:S(2)}, u32[]{:S(2)}) collective-permute-start(bf16[64,1024]{1,0:T(8,128)(2,1)S(1)} %get-tuple-element.37), channel_id=1, source_target_pairs={{0,12},{2,14},{4,8},{6,10},{8,4},{10,6},{12,0},{14,2},{1,13},{3,15... | collective-permute-start | bytes 393224 | tf_op jit(solution)/shard_map/ppermute | solution.py:331
  28.7 6.0 %collective-permute-start.10 = (bf16[32,2048]{1,0:T(8,128)(2,1)S(1)}, bf16[32,2048]{1,0:T(8,128)(2,1)S(1)}, u32[]{:S(2)}, u32[]{:S(2)}) collective-permute-start(bf16[32,2048]{1,0:T(8,128)(2,1)S(1)} %get-tuple-element.42), channel_id=1, source_target_pairs={{0,0},{2,2},{4,8},{6,10},{8,4},{10,6},{12,12},{14,14},{1,1},{3,3},... | collective-permute-start | bytes 393224 | tf_op jit(solution)/shard_map/ppermute | solution.py:331
  33.2 7.1 %collective-permute-start.11 = (bf16[32,2560]{1,0:T(8,128)(2,1)S(1)}, bf16[32,2560]{1,0:T(8,128)(2,1)S(1)}, u32[]{:S(2)}, u32[]{:S(2)}) collective-permute-start(bf16[32,2560]{1,0:T(8,128)(2,1)S(1)} %get-tuple-element.44), channel_id=1, source_target_pairs={{0,2},{2,0},{4,6},{6,4},{8,10},{10,8},{12,14},{14,12},{1,3},{3,1},... | collective-permute-start | bytes 491528 | tf_op jit(solution)/shard_map/ppermute | solution.py:331
  34.7 7.3 %collective-permute-start.12 = (bf16[32,2560]{1,0:T(8,128)(2,1)S(1)}, bf16[32,2560]{1,0:T(8,128)(2,1)S(1)}, u32[]{:S(2)}, u32[]{:S(2)}) collective-permute-start(bf16[32,2560]{1,0:T(8,128)(2,1)S(1)} %get-tuple-element.45), channel_id=1, source_target_pairs={{0,2},{2,0},{4,6},{6,4},{8,10},{10,8},{12,14},{14,12},{1,3},{3,1},... | collective-permute-start | bytes 491528 | tf_op jit(solution)/shard_map/ppermute | solution.py:331
  43.2 2.0 %collective-permute-start.14 = (f32[512,256]{1,0:T(8,128)S(1)}, f32[512,256]{1,0:T(8,128)S(1)}, u32[]{:S(2)}, u32[]{:S(2)}) collective-permute-start(f32[512,256]{1,0:T(8,128)S(1)} %get-tuple-element.50), channel_id=1, source_target_pairs={{0,1},{1,0},{2,3},{3,2},{4,5},{5,4},{6,7},{7,6},{8,9},{9,8},{10,11... | collective-permute-start | bytes 1572872 | tf_op jit(solution)/shard_map/ppermute | solution.py:428
  44.4 2.1 %collective-permute-start.13 = (f32[512,256]{1,0:T(8,128)S(1)}, f32[512,256]{1,0:T(8,128)S(1)}, u32[]{:S(2)}, u32[]{:S(2)}) collective-permute-start(f32[512,256]{1,0:T(8,128)S(1)} %get-tuple-element.48), channel_id=1, source_target_pairs={{0,1},{1,0},{2,3},{3,2},{4,5},{5,4},{6,7},{7,6},{8,9},{9,8},{10,11... | collective-permute-start | bytes 1572872 | tf_op jit(solution)/shard_map/ppermute | solution.py:428
  46.7 10.4 %collective-permute-start.21 = (bf16[2,64,256]{2,1,0:T(8,128)(2,1)S(1)}, bf16[2,64,256]{2,1,0:T(8,128)(2,1)S(1)}, u32[]{:S(2)}, u32[]{:S(2)}) collective-permute-start(bf16[2,64,256]{2,1,0:T(8,128)(2,1)S(1)} %get-tuple-element.52), channel_id=1, source_target_pairs={{0,14},{2,12},{4,10},{6,8},{8,6},{10,4},{12,2},{14,0},{1,15},{3,13... | collective-permute-start | bytes 196616 | tf_op jit(solution)/shard_map/ppermute | solution.py:331
  50.4 9.0 %collective-permute-start.20 = (bf16[2,64,256]{2,1,0:T(8,128)(2,1)S(1)}, bf16[2,64,256]{2,1,0:T(8,128)(2,1)S(1)}, u32[]{:S(2)}, u32[]{:S(2)}) collective-permute-start(bf16[2,64,256]{2,1,0:T(8,128)(2,1)S(1)} %get-tuple-element.53), channel_id=1, source_target_pairs={{0,12},{2,14},{4,8},{6,10},{8,4},{10,6},{12,0},{14,2},{1,13},{3,15... | collective-permute-start | bytes 196616 | tf_op jit(solution)/shard_map/ppermute | solution.py:331
  51.8 9.9 %collective-permute-start.19 = (bf16[2,64,256]{2,1,0:T(8,128)(2,1)S(1)}, bf16[2,64,256]{2,1,0:T(8,128)(2,1)S(1)}, u32[]{:S(2)}, u32[]{:S(2)}) collective-permute-start(bf16[2,64,256]{2,1,0:T(8,128)(2,1)S(1)} %get-tuple-element.54), channel_id=1, source_target_pairs={{0,10},{2,8},{4,2},{6,0},{8,14},{10,12},{12,6},{14,4},{1,11},{3,9}... | collective-permute-start | bytes 196616 | tf_op jit(solution)/shard_map/ppermute | solution.py:331
  54.2 7.5 %collective-permute-start.18 = (bf16[2,64,256]{2,1,0:T(8,128)(2,1)S(1)}, bf16[2,64,256]{2,1,0:T(8,128)(2,1)S(1)}, u32[]{:S(2)}, u32[]{:S(2)}) collective-permute-start(bf16[2,64,256]{2,1,0:T(8,128)(2,1)S(1)} %get-tuple-element.55), channel_id=1, source_target_pairs={{0,8},{2,10},{4,0},{6,2},{8,12},{10,14},{12,4},{14,6},{1,9},{3,11}... | collective-permute-start | bytes 196616 | tf_op jit(solution)/shard_map/ppermute | solution.py:331
  54.5 7.7 %collective-permute-start.17 = (bf16[2,64,256]{2,1,0:T(8,128)(2,1)S(1)}, bf16[2,64,256]{2,1,0:T(8,128)(2,1)S(1)}, u32[]{:S(2)}, u32[]{:S(2)}) collective-permute-start(bf16[2,64,256]{2,1,0:T(8,128)(2,1)S(1)} %get-tuple-element.56), channel_id=1, source_target_pairs={{0,6},{2,4},{4,14},{6,12},{8,2},{10,0},{12,10},{14,8},{1,7},{3,5},... | collective-permute-start | bytes 196616 | tf_op jit(solution)/shard_map/ppermute | solution.py:331
  57.1 6.8 %collective-permute-start.16 = (bf16[2,64,256]{2,1,0:T(8,128)(2,1)S(1)}, bf16[2,64,256]{2,1,0:T(8,128)(2,1)S(1)}, u32[]{:S(2)}, u32[]{:S(2)}) collective-permute-start(bf16[2,64,256]{2,1,0:T(8,128)(2,1)S(1)} %get-tuple-element.57), channel_id=1, source_target_pairs={{0,4},{2,6},{4,12},{6,14},{8,0},{10,2},{12,8},{14,10},{1,5},{3,7},... | collective-permute-start | bytes 196616 | tf_op jit(solution)/shard_map/ppermute | solution.py:331
  59.4 4.5 %collective-permute-start.15 = (bf16[2,64,256]{2,1,0:T(8,128)(2,1)S(1)}, bf16[2,64,256]{2,1,0:T(8,128)(2,1)S(1)}, u32[]{:S(2)}, u32[]{:S(2)}) collective-permute-start(bf16[2,64,256]{2,1,0:T(8,128)(2,1)S(1)} %get-tuple-element.51), channel_id=1, source_target_pairs={{0,2},{2,0},{4,6},{6,4},{8,10},{10,8},{12,14},{14,12},{1,3},{3,1},... | collective-permute-start | bytes 196616 | tf_op jit(solution)/shard_map/ppermute | solution.py:331
  (2 other events, 2.6 us)

commit v8 on v7

--- a/solution.py
+++ b/solution.py
@@ -428,13 +428,18 @@
         sums.append(keep + lax.ppermute(send, "sub", [(0, 1), (1, 0)]))
     chip = jnp.stack(sums)
     result = chip[:, :width]
-    for slot, to in ((0, to_same), (1, to_behind), (2, to_ahead), (3, to_far)):
-        for flip in range(X):
-            if slot == 0 and flip == 0:
-                continue
-            first = (slot * X + flip) * width
-            message = chip[:, first : first + width].astype(jnp.bfloat16)
-            result = result + move(message, (to, flip)).astype(jnp.float32)
+    for slot, flip, to in (
+        (3, 0, to_far),
+        (0, 1, to_same),
+        (2, 0, to_ahead),
+        (2, 1, to_ahead),
+        (1, 0, to_behind),
+        (1, 1, to_behind),
+        (3, 1, to_far),
+    ):
+        first = (slot * X + flip) * width
+        message = chip[:, first : first + width].astype(jnp.bfloat16)
+        result = result + move(message, (to, flip)).astype(jnp.float32)
     if dof_count > 1:
         result = lax.psum_scatter(result, "dof", scatter_dimension=2, tiled=True)
     return result.transpose(0, 2, 1)

time: 64.8 us -> 64.2 us (level)
  starting transfers between devices: 37.6 us -> 35.4 us
  waiting for transfers between devices: 17 us -> 18.6 us
    ppermute x19, starting transfers between devices: 36.5 us -> 34.3 us  [move(): return lax.ppermute(array, 'mode', pairs)]
    ppermute x19, waiting for transfers between devices: 15.5 us -> 17.1 us  [move(): return lax.ppermute(array, 'mode', pairs)]
where the time goes in v8:
time: 64.2 us; the launch traced here: 64 us
  starting transfers between devices  35.4 us (55%)
  waiting for transfers between devices  18.6 us (29%)
  Pallas kernels  6.31 us (10%)
  local copies, waits for them, and re-layouts  2.67 us (4%)
  other arithmetic  0.92 us (1%)
    ppermute x19, starting transfers between devices, move(): return lax.ppermute(array, 'mode', pairs)  34.3 us
    ppermute x19, waiting for transfers between devices, move(): return lax.ppermute(array, 'mode', pairs)  17.1 us
    unnamed x8, local copies, waits for them, and re-layouts  2.64 us
    pallas_call x2, Pallas kernels, make_projection(): pl.pallas_call(functools.partial(project_kernel, matrix, layout, slice(2...  2.29 us
    pallas_call x1, Pallas kernels, make_band(): pl.pallas_call(functools.partial(band_kernel, per_unit, block_total), out...  2.03 us
    pallas_call x1, Pallas kernels, make_image(): pl.pallas_call(functools.partial(image_kernel, layout, slice(2 * group, 3...  1.55 us
    ppermute x2, waiting for transfers between devices, body(): sums.append(keep + lax.ppermute(send, 'sub', [(0, 1), (1, 0)]))  1.47 us
  transfers between devices with their start and end apart: 22, of which 9 were waited for; matrix products, arithmetic and copies ran while one was open for 0% of the time, Pallas kernels for 8%

profile of v8, /device:TPU:0, one launch (start us, length us, event | category | flops | bytes accessed | tf_op | source)
XLA Modules:
  0.0 64.0 jit_solution(9287387384284864368)
XLA Ops:
  1.5 3.6 %collective-permute-start.2 = (bf16[64,2048]{1,0:T(8,128)(2,1)S(1)}, bf16[64,2048]{1,0:T(8,128)(2,1)S(1)}, u32[]{:S(2)}, u32[]{:S(2)}) collective-permute-start(bf16[64,2048]{1,0:T(8,128)(2,1)S(1)} %plain.1), channel_id=1, source_target_pairs={{0,8},{2,10},{4,0},{6,2},{8,12},{10,14},{12,4},{14,6},{1,9},{3,11}... | collective-permute-start | bytes 786440 | tf_op jit(solution)/shard_map/ppermute | solution.py:331
  5.4 1.6 %collective-permute-start.3 = (bf16[64,1024]{1,0:T(8,128)(2,1)S(1)}, bf16[64,1024]{1,0:T(8,128)(2,1)S(1)}, u32[]{:S(2)}, u32[]{:S(2)}) collective-permute-start(bf16[64,1024]{1,0:T(8,128)(2,1)S(1)} %get-tuple-element.29), channel_id=1, source_target_pairs={{0,8},{2,10},{4,0},{6,2},{8,12},{10,14},{12,4},{14,6},{1,9},{3,11}... | collective-permute-start | bytes 393224 | tf_op jit(solution)/shard_map/ppermute | solution.py:331
  7.4 1.5 %collective-permute-start.8 = (bf16[64,2560]{1,0:T(8,128)(2,1)S(1)}, bf16[64,2560]{1,0:T(8,128)(2,1)S(1)}, u32[]{:S(2)}, u32[]{:S(2)}) collective-permute-start(bf16[64,2560]{1,0:T(8,128)(2,1)S(1)} %get-tuple-element.38), channel_id=1, source_target_pairs={{0,2},{2,0},{4,6},{6,4},{8,10},{10,8},{12,14},{14,12},{1,3},{3,1},... | collective-permute-start | bytes 983048 | tf_op jit(solution)/shard_map/ppermute | solution.py:331
  8.9 1.6 %copy-done.2 = bf16[1,4,16,128,128]{4,3,2,1,0:T(8,128)(2,1)S(1)} copy-done((bf16[1,4,16,128,128]{4,3,2,1,0:T(8,128)(2,1)S(1)}, bf16[1,4,16,128,128]{4,3,2,1,0:T(8,128)(2,1)}, u32[]{:S(2)}) %copy-start.2) | copy-done | bytes 2097176
  10.5 2.0 %band.1 = bf16[2,4,128,2560]{3,2,1,0:T(8,128)(2,1)S(1)} custom-call(s32[1,4,16]{2,1,0:T(4,128)S(1)} %copy-done.3, bf16[1,4,16,128,128]{4,3,2,1,0:T(8,128)(2,1)S(1)} %copy-done.1, bf16[1,4,16,128,128]{4,3,2,1,0:T(8,128)(2,1)S(1)} %copy-done.2, bf16[64,2560]{1,0:T(8,128)(2,1)S(1)} %get-tuple-element.31._.refs_0_), custom_call_target="tpu_custom_call" | custom-call | bytes 8388608 | tf_op jit(solution)/shard_map/band/pallas_call | solution.py:62
  12.6 2.1 %collective-permute-done.3.rim = bf16[64,1024]{1,0:T(8,128)(2,1)S(1)} collective-permute-done((bf16[64,1024]{1,0:T(8,128)(2,1)S(1)}, bf16[64,1024]{1,0:T(8,128)(2,1)S(1)}, u32[]{:S(2)}, u32[]{:S(2)}) %collective-permute-start.3) | collective-permute-done | bytes 131104 | tf_op jit(solution)/shard_map/ppermute | solution.py:331
  14.8 1.6 %collective-permute-start.9 = (bf16[64,2560]{1,0:T(8,128)(2,1)S(1)}, bf16[64,2560]{1,0:T(8,128)(2,1)S(1)}, u32[]{:S(2)}, u32[]{:S(2)}) collective-permute-start(bf16[64,2560]{1,0:T(8,128)(2,1)S(1)} %get-tuple-element.32.refs_0_), channel_id=1, source_target_pairs={{0,2},{2,0},{4,6},{6,4},{8,10},{10,8},{12,14},{14,12},{1,3},{3,1},... | collective-permute-start | bytes 983048 | tf_op jit(solution)/shard_map/ppermute | solution.py:331
  17.0 5.2 %collective-permute-start.6 = (bf16[64,2048]{1,0:T(8,128)(2,1)S(1)}, bf16[64,2048]{1,0:T(8,128)(2,1)S(1)}, u32[]{:S(2)}, u32[]{:S(2)}) collective-permute-start(bf16[64,2048]{1,0:T(8,128)(2,1)S(1)} %get-tuple-element.36), channel_id=1, source_target_pairs={{0,4},{2,6},{4,0},{6,2},{8,12},{10,14},{12,8},{14,10},{1,5},{3,7},... | collective-permute-start | bytes 786440 | tf_op jit(solution)/shard_map/ppermute | solution.py:331
  22.2 2.3 %collective-permute-done.1.got = bf16[64,3072]{1,0:T(8,128)(2,1)S(1)} collective-permute-done((bf16[64,3072]{1,0:T(8,128)(2,1)S(1)}, bf16[64,3072]{1,0:T(8,128)(2,1)S(1)}, u32[]{:S(2)}, u32[]{:S(2)}) %collective-permute-start.1) | collective-permute-done | bytes 393248 | tf_op jit(solution)/shard_map/ppermute | solution.py:331
  24.6 1.6 %collective-permute-start.4 = (bf16[64,2560]{1,0:T(8,128)(2,1)S(1)}, bf16[64,2560]{1,0:T(8,128)(2,1)S(1)}, u32[]{:S(2)}, u32[]{:S(2)}) collective-permute-start(bf16[64,2560]{1,0:T(8,128)(2,1)S(1)} %get-tuple-element.34), channel_id=1, source_target_pairs={{0,2},{2,0},{4,6},{6,4},{8,10},{10,8},{12,14},{14,12},{1,3},{3,1},... | collective-permute-start | bytes 983048 | tf_op jit(solution)/shard_map/ppermute | solution.py:331
  26.2 2.5 %collective-permute-start.7 = (bf16[64,1024]{1,0:T(8,128)(2,1)S(1)}, bf16[64,1024]{1,0:T(8,128)(2,1)S(1)}, u32[]{:S(2)}, u32[]{:S(2)}) collective-permute-start(bf16[64,1024]{1,0:T(8,128)(2,1)S(1)} %get-tuple-element.37), channel_id=1, source_target_pairs={{0,12},{2,14},{4,8},{6,10},{8,4},{10,6},{12,0},{14,2},{1,13},{3,15... | collective-permute-start | bytes 393224 | tf_op jit(solution)/shard_map/ppermute | solution.py:331
  29.3 1.5 %image.1 = (bf16[256,1024]{1,0:T(8,128)(2,1)S(1)}, bf16[2,128,512]{2,1,0:T(8,128)(2,1)S(1)}) custom-call(bf16[64,2560]{1,0:T(8,128)(2,1)S(1)} %get-tuple-element.31._.refs_0_, bf16[64,2560]{1,0:T(8,128)(2,1)S(1)} %collective-permute-done.8.refs_1_, bf16[64,2560]{1,0:T(8,128)(2,1)S(1)} %get-tuple-element.39.refs_2_, ...), custom_call_target="tpu_custom_call" | custom-call | flops 1342177280 | bytes 4194304 | tf_op jit(solution)/shard_map/image/pallas_call | solution.py:234
  30.9 2.2 %collective-permute-done.7.rim = bf16[64,1024]{1,0:T(8,128)(2,1)S(1)} collective-permute-done((bf16[64,1024]{1,0:T(8,128)(2,1)S(1)}, bf16[64,1024]{1,0:T(8,128)(2,1)S(1)}, u32[]{:S(2)}, u32[]{:S(2)}) %collective-permute-start.7) | collective-permute-done | bytes 131104 | tf_op jit(solution)/shard_map/ppermute | solution.py:331
  33.2 1.4 %collective-permute-start.11 = (bf16[32,2560]{1,0:T(8,128)(2,1)S(1)}, bf16[32,2560]{1,0:T(8,128)(2,1)S(1)}, u32[]{:S(2)}, u32[]{:S(2)}) collective-permute-start(bf16[32,2560]{1,0:T(8,128)(2,1)S(1)} %get-tuple-element.44), channel_id=1, source_target_pairs={{0,2},{2,0},{4,6},{6,4},{8,10},{10,8},{12,14},{14,12},{1,3},{3,1},... | collective-permute-start | bytes 491528 | tf_op jit(solution)/shard_map/ppermute | solution.py:331
  35.4 4.8 %collective-permute-done.11.refs_4_ = bf16[32,2560]{1,0:T(8,128)(2,1)S(1)} collective-permute-done((bf16[32,2560]{1,0:T(8,128)(2,1)S(1)}, bf16[32,2560]{1,0:T(8,128)(2,1)S(1)}, u32[]{:S(2)}, u32[]{:S(2)}) %collective-permute-start.11) | collective-permute-done | bytes 163872 | tf_op jit(solution)/shard_map/ppermute | solution.py:331
  40.3 1.8 %collective-permute-done.12.refs_5_ = bf16[32,2560]{1,0:T(8,128)(2,1)S(1)} collective-permute-done((bf16[32,2560]{1,0:T(8,128)(2,1)S(1)}, bf16[32,2560]{1,0:T(8,128)(2,1)S(1)}, u32[]{:S(2)}, u32[]{:S(2)}) %collective-permute-start.12) | collective-permute-done | bytes 163872 | tf_op jit(solution)/shard_map/ppermute | solution.py:331
  43.2 1.1 %project.2 = (f32[512,256]{1,0:T(8,128)S(1)}, f32[512,256]{1,0:T(8,128)S(1)}) custom-call(bf16[64,2560]{1,0:T(8,128)(2,1)S(1)} %get-tuple-element.33.refs_0_, bf16[64,2560]{1,0:T(8,128)(2,1)S(1)} %collective-permute-done.4.refs_1_, bf16[32,2560]{1,0:T(8,128)(2,1)S(1)} %get-tuple-element.41.refs_2_, bf16[32,2560]{1,0:T(8,128)(2,1)S(1)} %get-tuple-element.43.refs_3_, ...), custom_call_target="tpu_custom_call" | custom-call | flops 268435456 | bytes 2097152 | tf_op jit(solution)/shard_map/project/pallas_call | solution.py:294
  45.2 1.3 %collective-permute-done.13 = f32[512,256]{1,0:T(8,128)S(1)} collective-permute-done((f32[512,256]{1,0:T(8,128)S(1)}, f32[512,256]{1,0:T(8,128)S(1)}, u32[]{:S(2)}, u32[]{:S(2)}) %collective-permute-start.13) | collective-permute-done | bytes 524320 | tf_op jit(solution)/shard_map/ppermute | solution.py:428
  46.7 3.7 %collective-permute-start.21 = (bf16[2,64,256]{2,1,0:T(8,128)(2,1)S(1)}, bf16[2,64,256]{2,1,0:T(8,128)(2,1)S(1)}, u32[]{:S(2)}, u32[]{:S(2)}) collective-permute-start(bf16[2,64,256]{2,1,0:T(8,128)(2,1)S(1)} %get-tuple-element.52), channel_id=1, source_target_pairs={{0,14},{2,12},{4,10},{6,8},{8,6},{10,4},{12,2},{14,0},{1,15},{3,13... | collective-permute-start | bytes 196616 | tf_op jit(solution)/shard_map/ppermute | solution.py:331
  50.4 2.4 %collective-permute-start.20 = (bf16[2,64,256]{2,1,0:T(8,128)(2,1)S(1)}, bf16[2,64,256]{2,1,0:T(8,128)(2,1)S(1)}, u32[]{:S(2)}, u32[]{:S(2)}) collective-permute-start(bf16[2,64,256]{2,1,0:T(8,128)(2,1)S(1)} %get-tuple-element.53), channel_id=1, source_target_pairs={{0,6},{2,4},{4,14},{6,12},{8,2},{10,0},{12,10},{14,8},{1,7},{3,5},... | collective-permute-start | bytes 196616 | tf_op jit(solution)/shard_map/ppermute | solution.py:331
  52.7 3.8 %collective-permute-start.18 = (bf16[2,64,256]{2,1,0:T(8,128)(2,1)S(1)}, bf16[2,64,256]{2,1,0:T(8,128)(2,1)S(1)}, u32[]{:S(2)}, u32[]{:S(2)}) collective-permute-start(bf16[2,64,256]{2,1,0:T(8,128)(2,1)S(1)} %get-tuple-element.55), channel_id=1, source_target_pairs={{0,10},{2,8},{4,2},{6,0},{8,14},{10,12},{12,6},{14,4},{1,11},{3,9}... | collective-permute-start | bytes 196616 | tf_op jit(solution)/shard_map/ppermute | solution.py:331
  57.1 2.4 %collective-permute-start.15 = (bf16[2,64,256]{2,1,0:T(8,128)(2,1)S(1)}, bf16[2,64,256]{2,1,0:T(8,128)(2,1)S(1)}, u32[]{:S(2)}, u32[]{:S(2)}) collective-permute-start(bf16[2,64,256]{2,1,0:T(8,128)(2,1)S(1)} %get-tuple-element.51), channel_id=1, source_target_pairs={{0,12},{2,14},{4,8},{6,10},{8,4},{10,6},{12,0},{14,2},{1,13},{3,15... | collective-permute-start | bytes 196616 | tf_op jit(solution)/shard_map/ppermute | solution.py:331
  59.5 2.6 %collective-permute-done.19 = bf16[2,64,256]{2,1,0:T(8,128)(2,1)S(1)} collective-permute-done((bf16[2,64,256]{2,1,0:T(8,128)(2,1)S(1)}, bf16[2,64,256]{2,1,0:T(8,128)(2,1)S(1)}, u32[]{:S(2)}, u32[]{:S(2)}) %collective-permute-start.19) | collective-permute-done | bytes 65568 | tf_op jit(solution)/shard_map/ppermute | solution.py:331
  62.1 1.3 %collective-permute-done.15 = bf16[2,64,256]{2,1,0:T(8,128)(2,1)S(1)} collective-permute-done((bf16[2,64,256]{2,1,0:T(8,128)(2,1)S(1)}, bf16[2,64,256]{2,1,0:T(8,128)(2,1)S(1)}, u32[]{:S(2)}, u32[]{:S(2)}) %collective-permute-start.15) | collective-permute-done | bytes 65568 | tf_op jit(solution)/shard_map/ppermute | solution.py:331
  (44 shorter events, 8.0 us)
Async XLA Ops:
  0.0 5.2 %collective-permute-start = (bf16[64,4096]{1,0:T(8,128)(2,1)}, bf16[64,4096]{1,0:T(8,128)(2,1)S(1)}, u32[]{:S(2)}, u32[]{:S(2)}) collective-permute-start(bf16[64,4096]{1,0:T(8,128)(2,1)} %bitcast.12), channel_id=1, source_target_pairs={{0,1},{1,0},{2,3},{3,2},{4,5},{5,4},{6,7},{7,6},{8,9},{9,8},{10,11... | collective-permute-start | bytes 1572872 | tf_op jit(solution)/shard_map/ppermute | solution.py:357
  1.5 7.4 %copy-start.1 = (bf16[1,4,16,128,128]{4,3,2,1,0:T(8,128)(2,1)S(1)}, bf16[1,4,16,128,128]{4,3,2,1,0:T(8,128)(2,1)}, u32[]{:S(2)}) copy-start(bf16[1,4,16,128,128]{4,3,2,1,0:T(8,128)(2,1)} %gyro.1) | copy-start | bytes 6291460
  1.5 7.4 %copy-start.3 = (s32[1,4,16]{2,1,0:T(4,128)S(1)}, s32[1,4,16]{2,1,0:T(4,128)}, u32[]{:S(2)}) copy-start(s32[1,4,16]{2,1,0:T(4,128)} %pattern.1) | copy-start | bytes 772
  1.5 11.0 %collective-permute-start.2 = (bf16[64,2048]{1,0:T(8,128)(2,1)S(1)}, bf16[64,2048]{1,0:T(8,128)(2,1)S(1)}, u32[]{:S(2)}, u32[]{:S(2)}) collective-permute-start(bf16[64,2048]{1,0:T(8,128)(2,1)S(1)} %plain.1), channel_id=1, source_target_pairs={{0,8},{2,10},{4,0},{6,2},{8,12},{10,14},{12,4},{14,6},{1,9},{3,11}... | collective-permute-start | bytes 786440 | tf_op jit(solution)/shard_map/ppermute | solution.py:331
  5.4 9.3 %collective-permute-start.3 = (bf16[64,1024]{1,0:T(8,128)(2,1)S(1)}, bf16[64,1024]{1,0:T(8,128)(2,1)S(1)}, u32[]{:S(2)}, u32[]{:S(2)}) collective-permute-start(bf16[64,1024]{1,0:T(8,128)(2,1)S(1)} %get-tuple-element.29), channel_id=1, source_target_pairs={{0,8},{2,10},{4,0},{6,2},{8,12},{10,14},{12,4},{14,6},{1,9},{3,11}... | collective-permute-start | bytes 393224 | tf_op jit(solution)/shard_map/ppermute | solution.py:331
  7.0 17.6 %collective-permute-start.1 = (bf16[64,3072]{1,0:T(8,128)(2,1)S(1)}, bf16[64,3072]{1,0:T(8,128)(2,1)S(1)}, u32[]{:S(2)}, u32[]{:S(2)}) collective-permute-start(bf16[64,3072]{1,0:T(8,128)(2,1)S(1)} %get-tuple-element.28), channel_id=1, source_target_pairs={{0,4},{2,6},{4,12},{6,14},{8,0},{10,2},{12,8},{14,10},{1,5},{3,7},... | collective-permute-start | bytes 1179656 | tf_op jit(solution)/shard_map/ppermute | solution.py:331
  7.4 21.2 %collective-permute-start.8 = (bf16[64,2560]{1,0:T(8,128)(2,1)S(1)}, bf16[64,2560]{1,0:T(8,128)(2,1)S(1)}, u32[]{:S(2)}, u32[]{:S(2)}) collective-permute-start(bf16[64,2560]{1,0:T(8,128)(2,1)S(1)} %get-tuple-element.38), channel_id=1, source_target_pairs={{0,2},{2,0},{4,6},{6,4},{8,10},{10,8},{12,14},{14,12},{1,3},{3,1},... | collective-permute-start | bytes 983048 | tf_op jit(solution)/shard_map/ppermute | solution.py:331
  14.8 14.6 %collective-permute-start.9 = (bf16[64,2560]{1,0:T(8,128)(2,1)S(1)}, bf16[64,2560]{1,0:T(8,128)(2,1)S(1)}, u32[]{:S(2)}, u32[]{:S(2)}) collective-permute-start(bf16[64,2560]{1,0:T(8,128)(2,1)S(1)} %get-tuple-element.32.refs_0_), channel_id=1, source_target_pairs={{0,2},{2,0},{4,6},{6,4},{8,10},{10,8},{12,14},{14,12},{1,3},{3,1},... | collective-permute-start | bytes 983048 | tf_op jit(solution)/shard_map/ppermute | solution.py:331
  16.3 9.9 %collective-permute-start.5 = (bf16[32,2048]{1,0:T(8,128)(2,1)S(1)}, bf16[32,2048]{1,0:T(8,128)(2,1)S(1)}, u32[]{:S(2)}, u32[]{:S(2)}) collective-permute-start(bf16[32,2048]{1,0:T(8,128)(2,1)S(1)} %get-tuple-element.35), channel_id=1, source_target_pairs={{0,0},{2,2},{4,8},{6,10},{8,4},{10,6},{12,12},{14,14},{1,1},{3,3},... | collective-permute-start | bytes 393224 | tf_op jit(solution)/shard_map/ppermute | solution.py:331
  17.0 16.1 %collective-permute-start.6 = (bf16[64,2048]{1,0:T(8,128)(2,1)S(1)}, bf16[64,2048]{1,0:T(8,128)(2,1)S(1)}, u32[]{:S(2)}, u32[]{:S(2)}) collective-permute-start(bf16[64,2048]{1,0:T(8,128)(2,1)S(1)} %get-tuple-element.36), channel_id=1, source_target_pairs={{0,4},{2,6},{4,0},{6,2},{8,12},{10,14},{12,8},{14,10},{1,5},{3,7},... | collective-permute-start | bytes 786440 | tf_op jit(solution)/shard_map/ppermute | solution.py:331
  24.6 17.4 %collective-permute-start.4 = (bf16[64,2560]{1,0:T(8,128)(2,1)S(1)}, bf16[64,2560]{1,0:T(8,128)(2,1)S(1)}, u32[]{:S(2)}, u32[]{:S(2)}) collective-permute-start(bf16[64,2560]{1,0:T(8,128)(2,1)S(1)} %get-tuple-element.34), channel_id=1, source_target_pairs={{0,2},{2,0},{4,6},{6,4},{8,10},{10,8},{12,14},{14,12},{1,3},{3,1},... | collective-permute-start | bytes 983048 | tf_op jit(solution)/shard_map/ppermute | solution.py:331
  26.2 6.9 %collective-permute-start.7 = (bf16[64,1024]{1,0:T(8,128)(2,1)S(1)}, bf16[64,1024]{1,0:T(8,128)(2,1)S(1)}, u32[]{:S(2)}, u32[]{:S(2)}) collective-permute-start(bf16[64,1024]{1,0:T(8,128)(2,1)S(1)} %get-tuple-element.37), channel_id=1, source_target_pairs={{0,12},{2,14},{4,8},{6,10},{8,4},{10,6},{12,0},{14,2},{1,13},{3,15... | collective-permute-start | bytes 393224 | tf_op jit(solution)/shard_map/ppermute | solution.py:331
  28.7 6.0 %collective-permute-start.10 = (bf16[32,2048]{1,0:T(8,128)(2,1)S(1)}, bf16[32,2048]{1,0:T(8,128)(2,1)S(1)}, u32[]{:S(2)}, u32[]{:S(2)}) collective-permute-start(bf16[32,2048]{1,0:T(8,128)(2,1)S(1)} %get-tuple-element.42), channel_id=1, source_target_pairs={{0,0},{2,2},{4,8},{6,10},{8,4},{10,6},{12,12},{14,14},{1,1},{3,3},... | collective-permute-start | bytes 393224 | tf_op jit(solution)/shard_map/ppermute | solution.py:331
  33.2 7.1 %collective-permute-start.11 = (bf16[32,2560]{1,0:T(8,128)(2,1)S(1)}, bf16[32,2560]{1,0:T(8,128)(2,1)S(1)}, u32[]{:S(2)}, u32[]{:S(2)}) collective-permute-start(bf16[32,2560]{1,0:T(8,128)(2,1)S(1)} %get-tuple-element.44), channel_id=1, source_target_pairs={{0,2},{2,0},{4,6},{6,4},{8,10},{10,8},{12,14},{14,12},{1,3},{3,1},... | collective-permute-start | bytes 491528 | tf_op jit(solution)/shard_map/ppermute | solution.py:331
  34.7 7.3 %collective-permute-start.12 = (bf16[32,2560]{1,0:T(8,128)(2,1)S(1)}, bf16[32,2560]{1,0:T(8,128)(2,1)S(1)}, u32[]{:S(2)}, u32[]{:S(2)}) collective-permute-start(bf16[32,2560]{1,0:T(8,128)(2,1)S(1)} %get-tuple-element.45), channel_id=1, source_target_pairs={{0,2},{2,0},{4,6},{6,4},{8,10},{10,8},{12,14},{14,12},{1,3},{3,1},... | collective-permute-start | bytes 491528 | tf_op jit(solution)/shard_map/ppermute | solution.py:331
  43.2 2.0 %collective-permute-start.14 = (f32[512,256]{1,0:T(8,128)S(1)}, f32[512,256]{1,0:T(8,128)S(1)}, u32[]{:S(2)}, u32[]{:S(2)}) collective-permute-start(f32[512,256]{1,0:T(8,128)S(1)} %get-tuple-element.50), channel_id=1, source_target_pairs={{0,1},{1,0},{2,3},{3,2},{4,5},{5,4},{6,7},{7,6},{8,9},{9,8},{10,11... | collective-permute-start | bytes 1572872 | tf_op jit(solution)/shard_map/ppermute | solution.py:428
  44.4 2.1 %collective-permute-start.13 = (f32[512,256]{1,0:T(8,128)S(1)}, f32[512,256]{1,0:T(8,128)S(1)}, u32[]{:S(2)}, u32[]{:S(2)}) collective-permute-start(f32[512,256]{1,0:T(8,128)S(1)} %get-tuple-element.48), channel_id=1, source_target_pairs={{0,1},{1,0},{2,3},{3,2},{4,5},{5,4},{6,7},{7,6},{8,9},{9,8},{10,11... | collective-permute-start | bytes 1572872 | tf_op jit(solution)/shard_map/ppermute | solution.py:428
  46.7 9.9 %collective-permute-start.21 = (bf16[2,64,256]{2,1,0:T(8,128)(2,1)S(1)}, bf16[2,64,256]{2,1,0:T(8,128)(2,1)S(1)}, u32[]{:S(2)}, u32[]{:S(2)}) collective-permute-start(bf16[2,64,256]{2,1,0:T(8,128)(2,1)S(1)} %get-tuple-element.52), channel_id=1, source_target_pairs={{0,14},{2,12},{4,10},{6,8},{8,6},{10,4},{12,2},{14,0},{1,15},{3,13... | collective-permute-start | bytes 196616 | tf_op jit(solution)/shard_map/ppermute | solution.py:331
  50.4 6.7 %collective-permute-start.20 = (bf16[2,64,256]{2,1,0:T(8,128)(2,1)S(1)}, bf16[2,64,256]{2,1,0:T(8,128)(2,1)S(1)}, u32[]{:S(2)}, u32[]{:S(2)}) collective-permute-start(bf16[2,64,256]{2,1,0:T(8,128)(2,1)S(1)} %get-tuple-element.53), channel_id=1, source_target_pairs={{0,6},{2,4},{4,14},{6,12},{8,2},{10,0},{12,10},{14,8},{1,7},{3,5},... | collective-permute-start | bytes 196616 | tf_op jit(solution)/shard_map/ppermute | solution.py:331
  52.7 9.3 %collective-permute-start.19 = (bf16[2,64,256]{2,1,0:T(8,128)(2,1)S(1)}, bf16[2,64,256]{2,1,0:T(8,128)(2,1)S(1)}, u32[]{:S(2)}, u32[]{:S(2)}) collective-permute-start(bf16[2,64,256]{2,1,0:T(8,128)(2,1)S(1)} %get-tuple-element.54), channel_id=1, source_target_pairs={{0,4},{2,6},{4,12},{6,14},{8,0},{10,2},{12,8},{14,10},{1,5},{3,7},... | collective-permute-start | bytes 196616 | tf_op jit(solution)/shard_map/ppermute | solution.py:331
  52.7 9.3 %collective-permute-start.18 = (bf16[2,64,256]{2,1,0:T(8,128)(2,1)S(1)}, bf16[2,64,256]{2,1,0:T(8,128)(2,1)S(1)}, u32[]{:S(2)}, u32[]{:S(2)}) collective-permute-start(bf16[2,64,256]{2,1,0:T(8,128)(2,1)S(1)} %get-tuple-element.55), channel_id=1, source_target_pairs={{0,10},{2,8},{4,2},{6,0},{8,14},{10,12},{12,6},{14,4},{1,11},{3,9}... | collective-permute-start | bytes 196616 | tf_op jit(solution)/shard_map/ppermute | solution.py:331
  56.5 5.5 %collective-permute-start.17 = (bf16[2,64,256]{2,1,0:T(8,128)(2,1)S(1)}, bf16[2,64,256]{2,1,0:T(8,128)(2,1)S(1)}, u32[]{:S(2)}, u32[]{:S(2)}) collective-permute-start(bf16[2,64,256]{2,1,0:T(8,128)(2,1)S(1)} %get-tuple-element.56), channel_id=1, source_target_pairs={{0,8},{2,10},{4,0},{6,2},{8,12},{10,14},{12,4},{14,6},{1,9},{3,11}... | collective-permute-start | bytes 196616 | tf_op jit(solution)/shard_map/ppermute | solution.py:331
  56.5 5.5 %collective-permute-start.16 = (bf16[2,64,256]{2,1,0:T(8,128)(2,1)S(1)}, bf16[2,64,256]{2,1,0:T(8,128)(2,1)S(1)}, u32[]{:S(2)}, u32[]{:S(2)}) collective-permute-start(bf16[2,64,256]{2,1,0:T(8,128)(2,1)S(1)} %get-tuple-element.57), channel_id=1, source_target_pairs={{0,2},{2,0},{4,6},{6,4},{8,10},{10,8},{12,14},{14,12},{1,3},{3,1},... | collective-permute-start | bytes 196616 | tf_op jit(solution)/shard_map/ppermute | solution.py:331
  57.1 6.2 %collective-permute-start.15 = (bf16[2,64,256]{2,1,0:T(8,128)(2,1)S(1)}, bf16[2,64,256]{2,1,0:T(8,128)(2,1)S(1)}, u32[]{:S(2)}, u32[]{:S(2)}) collective-permute-start(bf16[2,64,256]{2,1,0:T(8,128)(2,1)S(1)} %get-tuple-element.51), channel_id=1, source_target_pairs={{0,12},{2,14},{4,8},{6,10},{8,4},{10,6},{12,0},{14,2},{1,13},{3,15... | collective-permute-start | bytes 196616 | tf_op jit(solution)/shard_map/ppermute | solution.py:331
  (2 other events, 2.6 us)
